TPU v7x, 256 devices: a whole 4x4x8 slice. The times are simulated.
256 devices in a mesh: pipe: 16 (over x, y_hi, core), expert: 16 (over y_lo, z).
Axes of the slice: x: 4, y: 4 (y_hi: 2, y_lo: 2; y = y_hi * 2 + y_lo), z: 8, core: 2. Of those that a mesh axis runs over, the one named last changes fastest.
Arguments:
- tokens: bfloat16 [2048, 7168], P('expert'), may hold values from -6 to 6
- route_ids: int32 [2048, 8], P('expert'), may hold values from 0 to 255, all different within a row; in each aligned block of 128 rows (0 to 127, 128 to 255, ...) at most 8 rows name the same one
- route_gates: float32 [2048, 8], P('expert'), may hold values from 0.05 to 1
- w_gate: bfloat16 [16, 7168, 2048], P('expert', None, 'pipe'), may hold values from -0.0625 to 0.0625
- w_up: bfloat16 [16, 7168, 2048], P('expert', None, 'pipe'), may hold values from -0.0625 to 0.0625
- w_down: bfloat16 [16, 2048, 7168], P('expert', 'pipe'), may hold values from -0.125 to 0.125
- out_grad: bfloat16 [2048, 7168], P('expert'), may hold values from -6 to 6
- latent_grad: bfloat16 [16, 2048, 512], P('pipe', 'expert'), may hold values from -0.119628906 to 0.119628906
Outputs:
- routed: bfloat16 [2048, 7168], P('expert')
- token_grad: bfloat16 [2048, 7168], P('expert')
- kv_grad: bfloat16 [16, 7168, 512], P('pipe', 'expert')
Inputs may be any that keep to these rules, and one draw needn't show every extreme that they name: `route_ids`: each row names 8 different experts. In the rows of one device no expert is named by more than 8 rows. Only experts below 16 are computed.
All inputs are finite; a program needn't handle non-finite values.
Results may differ from a plain program's by a relative error of at most 0.024.
Values may be sent and summed in bfloat16 or wider, within the bound.
No kernel may reach another device: no remote copies, remote signals or barrier semaphores. Data moves between devices by JAX's collectives and lax.ppermute only.
A program may use at most 192 MiB of HBM per device.

v0:
```python
import jax
import jax.numpy as jnp
from jax import lax
from jax.sharding import PartitionSpec as P

SLOT = 8


def swapped(value, axis, distance):
    mask = 2**distance
    pairs = [(source, source ^ mask) for source in range(lax.axis_size(axis))]
    return lax.ppermute(value, axis, pairs)


def routing(ids, gates, n_exp):
    tok = ids.shape[0]
    topk = ids.shape[1]
    flat = ids.reshape(-1)
    inside = flat < n_exp
    onehot = jnp.logical_and(
        flat[:, None] == jnp.arange(n_exp, dtype=jnp.int32)[None, :], inside[:, None]
    ).astype(jnp.int32)
    before = jnp.cumsum(onehot, axis=0) - onehot
    place = jnp.sum(before * onehot, axis=1)
    target = jnp.where(inside, flat * SLOT + place, -1)
    match = (target[:, None] == jnp.arange(n_exp * SLOT, dtype=jnp.int32)[None, :]).reshape(
        tok, topk, n_exp * SLOT
    )
    matched = match.astype(jnp.float32)
    select = jnp.sum(matched, axis=1)
    mixing = jnp.sum(matched * gates[:, :, None], axis=1)
    slot_gate = jnp.sum(mixing, axis=0)
    return (select, mixing, slot_gate)


def combine_rows(flat, mixing):
    total = jnp.dot(mixing, flat.astype(jnp.float32), precision=lax.Precision.HIGHEST)
    return total.astype(jnp.bfloat16)


def deliver(buffer, n_exp):
    width = buffer.shape[1]
    shaped = buffer.reshape(n_exp, SLOT, width)
    whole = lax.all_to_all(shaped, "expert", split_axis=0, concat_axis=0, tiled=True)
    return whole.reshape(n_exp * SLOT, width)


def settle(partial_value, mixing, n_exp):
    width = partial_value.shape[1]
    shaped = partial_value.reshape(n_exp, SLOT, width)
    summed = lax.psum(shaped.astype(jnp.bfloat16), "pipe")
    returned = lax.all_to_all(summed, "expert", split_axis=0, concat_axis=0, tiled=True)
    return combine_rows(returned.reshape(n_exp * SLOT, width), mixing)


def per_device(tokens, route_ids, route_gates, w_gate, w_up, w_down, out_grad, latent_grad):
    n_exp = lax.axis_size("expert")
    select, mixing, slot_gate = routing(route_ids, route_gates, n_exp)
    select_bf = select.astype(jnp.bfloat16)
    wg = w_gate[0]
    wu = w_up[0]
    wd = w_down[0]
    sent = jnp.dot(select_bf.T, tokens, preferred_element_type=jnp.float32).astype(jnp.bfloat16)
    rows = deliver(sent, n_exp)
    gate_act = jnp.dot(rows, wg, preferred_element_type=jnp.float32)
    up_act = jnp.dot(rows, wu, preferred_element_type=jnp.float32)
    sg = jax.nn.sigmoid(gate_act)
    hidden = (gate_act * sg * up_act).astype(jnp.bfloat16)
    partial_value = jnp.dot(hidden, wd, preferred_element_type=jnp.float32)
    routed = settle(partial_value, mixing, n_exp)
    picked_grad = jnp.dot(select_bf.T, out_grad, preferred_element_type=jnp.float32)
    dsent = (picked_grad * slot_gate[:, None]).astype(jnp.bfloat16)
    drows = deliver(dsent, n_exp)
    hidden_grad = jnp.einsum("rd,fd->rf", drows, wd, preferred_element_type=jnp.float32)
    gate_grad = (hidden_grad * up_act * sg * (1.0 + gate_act * (1.0 - sg))).astype(jnp.bfloat16)
    up_grad = (hidden_grad * gate_act * sg).astype(jnp.bfloat16)
    dpartial = jnp.einsum("rf,df->rd", gate_grad, wg, preferred_element_type=jnp.float32)
    dpartial = dpartial + jnp.einsum("rf,df->rd", up_grad, wu, preferred_element_type=jnp.float32)
    token_grad = settle(dpartial, select, n_exp)
    latent = latent_grad[0]
    share = lax.psum_scatter(
        jnp.einsum("td,tk->dk", tokens, latent, preferred_element_type=jnp.float32).astype(
            jnp.bfloat16
        ),
        "expert",
        scatter_dimension=0,
        tiled=True,
    ).astype(jnp.float32)
    paired = share
    for bit in range(lax.axis_size("pipe").bit_length() - 1):
        paired = swapped(paired.astype(jnp.bfloat16), "pipe", bit).astype(paired.dtype)
    total = share + paired
    kv_grad = total.astype(jnp.bfloat16)[None]
    return (routed, token_grad, kv_grad)


def solution(mesh):
    return jax.shard_map(
        per_device,
        mesh=mesh,
        in_specs=(
            P("expert", None),
            P("expert", None),
            P("expert", None),
            P("expert", None, "pipe"),
            P("expert", None, "pipe"),
            P("expert", "pipe", None),
            P("expert", None),
            P("pipe", "expert", None),
        ),
        out_specs=(P("expert", None), P("expert", None), P("pipe", "expert", None)),
        check_vma=False,
    )
```

profile of v0, /device:TPU:1, one launch (start us, length us, event | category | flops | bytes accessed | tf_op | source)
XLA Modules:
  0.0 460.1 jit_solution(5423229628938565184)
XLA Ops:
  8.0 0.0 copy-start
  8.0 0.9 copy.33
  8.9 0.1 eq.43
  9.0 0.1 eq.39
  9.2 4.5 reduce-window.6
  13.7 0.1 slice.8
  13.8 0.1 copy.35
  13.9 0.1 copy.36
  14.0 0.1 broadcast_add_fusion
  14.1 0.1 reduce_sum.39
  14.3 0.7 add_select_fusion
  15.0 0.1 copy.38
  15.1 0.8 copy.39
  15.9 0.4 select_reduce_fusion
  16.3 0.0 copy-done
  16.3 1.9 fusion.2
  18.2 10.2 %all-to-all-start = ((bf16[16,8,7168]{2,1,0:T(8,128)(2,1)}), bf16[16,8,7168]{2,1,0:T(8,128)(2,1)}, u32[]{:S(2)}, u32[]{:S(2)}) async-start(bf16[16,8,7168]{2,1,0:T(8,128)(2,1)} %fusion.2), calls=%async_computation | async-start | bytes 3670016 | tf_op jit(solution)/shard_map/all_to_all | solution.py:44
  28.3 3.4 fusion.4
  31.7 38.3 %all-to-all-done = bf16[16,8,7168]{2,1,0:T(8,128)(2,1)} async-done(((bf16[16,8,7168]{2,1,0:T(8,128)(2,1)}), bf16[16,8,7168]{2,1,0:T(8,128)(2,1)}, u32[]{:S(2)}, u32[]{:S(2)}) %all-to-all-start) | async-done | bytes 1835040 | tf_op jit(solution)/shard_map/all_to_all | solution.py:44
  70.0 7.4 %all-to-all-start.2 = ((bf16[16,8,7168]{2,1,0:T(8,128)(2,1)}), bf16[16,8,7168]{2,1,0:T(8,128)(2,1)}, u32[]{:S(2)}, u32[]{:S(2)}) async-start(bf16[16,8,7168]{2,1,0:T(8,128)(2,1)} %fusion.4), calls=%async_computation.2 | async-start | bytes 3670016 | tf_op jit(solution)/shard_map/all_to_all | solution.py:44
  77.5 0.0 all-reduce.3.cloned.1.call-start
  77.5 0.0 copy-start.1
  77.5 2.8 fusion.16
  80.3 0.0 copy-done.1
  80.3 0.0 copy-start.3
  80.4 2.3 fusion.12
  82.6 0.0 copy-done.3
  82.6 1.9 convolution_convert_fusion.3
  84.5 35.3 %all-to-all-done.2 = bf16[16,8,7168]{2,1,0:T(8,128)(2,1)} async-done(((bf16[16,8,7168]{2,1,0:T(8,128)(2,1)}), bf16[16,8,7168]{2,1,0:T(8,128)(2,1)}, u32[]{:S(2)}, u32[]{:S(2)}) %all-to-all-start.2) | async-done | bytes 1835040 | tf_op jit(solution)/shard_map/all_to_all | solution.py:44
  119.8 0.0 copy-start.4
  119.8 2.8 fusion.6
  122.6 0.0 copy-done.4
  122.6 0.0 copy-start.2
  122.6 0.6 fusion.14
  123.3 0.8 copy-done.2
  124.1 1.9 fusion.3
  126.0 0.0 copy-start.6
  126.0 0.0 all-reduce.3.cloned.1.call-update
  126.0 0.0 reduce-scatter.2.cloned.1.call-start
  126.1 0.8 copy-done.6
  126.9 5.0 %convolution_convert_fusion = bf16[7168,512]{1,0:T(8,128)(2,1)} fusion(bf16[128,7168]{1,0:T(8,128)(2,1)S(1)} %copy-done, bf16[1,128,512]{2,1,0:T(8,128)(2,1)S(1)} %copy-done.6), kind=kOutput, calls=%fused_computation | convolution fusion | flops 943194112 | bytes 9306112 | tf_op jit(solution)/shard_map/td,tk->dk/dot_general | solution.py:82
  131.9 0.0 reduce-scatter.2.cloned.1.call-update
  132.0 218.7 %all-reduce.3.cloned.1.call-done = (bf16[16,8,7168]{2,1,0:T(8,128)(2,1)}, bf16[16,8,7168]{2,1,0:T(8,128)(2,1)}) async-done(((bf16[16,8,7168]{2,1,0:T(8,128)(2,1)}, bf16[16,8,7168]{2,1,0:T(8,128)(2,1)}), (bf16[16,8,7168]{2,1,0:T(8,128)(2,1)}, bf16[16,8,7168]{2,1,0:T(8,128)(2,1)})) %all-reduce.3.cloned.1.call-update) | async-done | bytes 3670032 | tf_op jit(solution)/shard_map/psum | solution.py:51
  350.7 48.7 %all_to_all.20 = bf16[16,8,7168]{2,1,0:T(8,128)(2,1)} all-to-all(bf16[16,8,7168]{2,1,0:T(8,128)(2,1)} %get-tuple-element.7), channel_id=1, replica_groups=mesh['pipe'=16,'expert'=16] {'expert'}, dimensions={0} | all-to-all | bytes 3670016 | tf_op jit(solution)/shard_map/all_to_all | solution.py:52
  399.3 6.0 %all-to-all-start.1 = ((bf16[16,8,7168]{2,1,0:T(8,128)(2,1)}), bf16[16,8,7168]{2,1,0:T(8,128)(2,1)}, u32[]{:S(2)}, u32[]{:S(2)}) async-start(bf16[16,8,7168]{2,1,0:T(8,128)(2,1)} %get-tuple-element.6), calls=%async_computation.1 | async-start | bytes 3670016 | tf_op jit(solution)/shard_map/all_to_all | solution.py:52
  405.3 0.0 reduce-scatter.2.cloned.1.call-done
  405.3 1.9 collective-permute-start
  407.2 1.7 collective-permute-done
  408.9 0.0 collective-permute-start.1
  408.9 19.6 %collective-permute-done.1 = bf16[448,512]{1,0:T(8,128)(2,1)S(1)} collective-permute-done((bf16[448,512]{1,0:T(8,128)(2,1)S(1)}, bf16[448,512]{1,0:T(8,128)(2,1)S(1)}, u32[]{:S(2)}, u32[]{:S(2)}) %collective-permute-start.1) | collective-permute-done | bytes 458784 | tf_op jit(solution)/shard_map/ppermute | solution.py:12
  428.4 0.0 collective-permute-start.2
  428.5 11.4 %collective-permute-done.2 = bf16[448,512]{1,0:T(8,128)(2,1)S(1)} collective-permute-done((bf16[448,512]{1,0:T(8,128)(2,1)S(1)}, bf16[448,512]{1,0:T(8,128)(2,1)S(1)}, u32[]{:S(2)}, u32[]{:S(2)}) %collective-permute-start.2) | collective-permute-done | bytes 458784 | tf_op jit(solution)/shard_map/ppermute | solution.py:12
  439.8 2.5 collective-permute-start.3
  442.3 4.3 convolution_convert_fusion.1
  446.6 0.1 all-to-all-done.1
  446.7 0.0 copy-start.5
  446.7 4.4 convolution_convert_fusion.2
  451.1 0.7 collective-permute-done.3
  451.7 0.0 copy-done.5
  451.7 0.9 fusion.20
  (7 shorter events, 0.1 us)
Async XLA Ops:
  8.0 8.3 %copy-start = (bf16[128,7168]{1,0:T(8,128)(2,1)S(1)}, bf16[128,7168]{1,0:T(8,128)(2,1)}, u32[]{:S(2)}) copy-start(bf16[128,7168]{1,0:T(8,128)(2,1)} %param.8) | copy-start | bytes 5505028
  18.2 51.9 %all-to-all-start = ((bf16[16,8,7168]{2,1,0:T(8,128)(2,1)}), bf16[16,8,7168]{2,1,0:T(8,128)(2,1)}, u32[]{:S(2)}, u32[]{:S(2)}) async-start(bf16[16,8,7168]{2,1,0:T(8,128)(2,1)} %fusion.2), calls=%async_computation | async-start | bytes 3670016 | tf_op jit(solution)/shard_map/all_to_all | solution.py:44
  70.0 49.7 %all-to-all-start.2 = ((bf16[16,8,7168]{2,1,0:T(8,128)(2,1)}), bf16[16,8,7168]{2,1,0:T(8,128)(2,1)}, u32[]{:S(2)}, u32[]{:S(2)}) async-start(bf16[16,8,7168]{2,1,0:T(8,128)(2,1)} %fusion.4), calls=%async_computation.2 | async-start | bytes 3670016 | tf_op jit(solution)/shard_map/all_to_all | solution.py:44
  77.5 273.2 %all-reduce.3.cloned.1.call-start = ((), (), s32[]{:S(2)}) async-start(), calls=%async_computation.6 | async-start | bytes 7340032 | tf_op jit(solution)/shard_map/psum | solution.py:51
  77.5 2.8 copy-start.1
  80.3 2.3 copy-start.3
  119.8 2.8 copy-start.4
  122.6 1.5 copy-start.2
  126.0 0.9 copy-start.6
  126.0 279.3 %reduce-scatter.2.cloned.1.call-start = ((), (), s32[]{:S(2)}) async-start(), calls=%async_computation.5 | async-start | bytes 7798784 | tf_op jit(solution)/shard_map/reduce_scatter | solution.py:81
  399.3 47.4 %all-to-all-start.1 = ((bf16[16,8,7168]{2,1,0:T(8,128)(2,1)}), bf16[16,8,7168]{2,1,0:T(8,128)(2,1)}, u32[]{:S(2)}, u32[]{:S(2)}) async-start(bf16[16,8,7168]{2,1,0:T(8,128)(2,1)} %get-tuple-element.6), calls=%async_computation.1 | async-start | bytes 3670016 | tf_op jit(solution)/shard_map/all_to_all | solution.py:52
  405.3 3.6 collective-permute-start
  408.9 19.6 %collective-permute-start.1 = (bf16[448,512]{1,0:T(8,128)(2,1)S(1)}, bf16[448,512]{1,0:T(8,128)(2,1)S(1)}, u32[]{:S(2)}, u32[]{:S(2)}) collective-permute-start(bf16[448,512]{1,0:T(8,128)(2,1)S(1)} %collective-permute-done), channel_id=1, source_target_pairs={{0,32},{16,48},{32,0},{48,16},{64,96},{80,112},{96,64},{112,80},{1... | collective-permute-start | bytes 1376264 | tf_op jit(solution)/shard_map/ppermute | solution.py:12
  428.4 11.4 %collective-permute-start.2 = (bf16[448,512]{1,0:T(8,128)(2,1)S(1)}, bf16[448,512]{1,0:T(8,128)(2,1)S(1)}, u32[]{:S(2)}, u32[]{:S(2)}) collective-permute-start(bf16[448,512]{1,0:T(8,128)(2,1)S(1)} %collective-permute-done.1), channel_id=1, source_target_pairs={{0,64},{16,80},{32,96},{48,112},{64,0},{80,16},{96,32},{112,48},{1... | collective-permute-start | bytes 1376264 | tf_op jit(solution)/shard_map/ppermute | solution.py:12
  439.8 11.9 %collective-permute-start.3 = (bf16[448,512]{1,0:T(8,128)(2,1)S(1)}, bf16[448,512]{1,0:T(8,128)(2,1)S(1)}, u32[]{:S(2)}, u32[]{:S(2)}) collective-permute-start(bf16[448,512]{1,0:T(8,128)(2,1)S(1)} %collective-permute-done.2), channel_id=1, source_target_pairs={{0,128},{16,144},{32,160},{48,176},{64,192},{80,208},{96,224},{112... | collective-permute-start | bytes 1376264 | tf_op jit(solution)/shard_map/ppermute | solution.py:12
  446.7 5.0 %copy-start.5 = (bf16[448,512]{1,0:T(8,128)(2,1)S(1)}, bf16[448,512]{1,0:T(8,128)(2,1)}, u32[]{:S(2)}) copy-start(bf16[448,512]{1,0:T(8,128)(2,1)} %reduce-scatter.2.cloned.1.call-done) | copy-start | bytes 1376260
Sparse Core Ops, SparseCore 0:
  126.1 224.4 all-reduce.2
Sparse Core Ops, SparseCore 1:
  132.1 89.7 reduce-scatter.1
where the time goes:
time: 465 us; the launch traced here: 460 us
  waiting for transfers between devices  326 us (70%)
  blocking collectives  48.7 us (10%)
  matrix products  31.3 us (7%)
  starting transfers between devices  28 us (6%)
  between operations  15.7 us (3%)
  other arithmetic  6.67 us (1%)
    psum x1, waiting for transfers between devices, settle(): summed = lax.psum(shaped.astype(jnp.bfloat16), 'pipe')  219 us
    all_to_all x2, waiting for transfers between devices, deliver(): lax.all_to_all(shaped, 'expert', split_axis=0, concat_axis=0, tiled=True)  73.6 us
    all_to_all x1, blocking collectives, settle(): lax.all_to_all(summed, 'expert', split_axis=0, concat_axis=0, tiled=True)  48.7 us
    ppermute x4, waiting for transfers between devices, swapped(): return lax.ppermute(value, axis, pairs)  33.2 us
    all_to_all x2, starting transfers between devices, deliver(): lax.all_to_all(shaped, 'expert', split_axis=0, concat_axis=0, tiled=True)  17.6 us
  transfers between devices with their start and end apart: 9, of which 8 were waited for; matrix products, arithmetic and copies ran while one was open for 5% of the time, Pallas kernels for 0%

commit v1 on v0

v1 whole, which is shorter than its diff:
```python
import numpy as np
import jax
import jax.numpy as jnp
from jax import lax
from jax.sharding import PartitionSpec as P

SLOT = 8
BF = jnp.bfloat16
F32 = jnp.float32
CORE, Y_HI, X_LOW = 1, 2, 4


def across(value, mask):
    return lax.ppermute(value, "pipe", [(i, i ^ mask) for i in range(16)])


def delta(p, j):
    return (p & 1) * 8 + j * 4 + (p >> 2)


def shifted(value, j):
    pairs = [(p * 16 + e, p * 16 + (e ^ delta(p, j))) for p in range(16) for e in range(16)]
    return lax.ppermute(value, ("pipe", "expert"), pairs)


def gather_x(block):
    return [block] + [across(block, X_LOW * off) for off in (1, 2, 3)]


def scatter_x(partial):
    size = partial.shape[0] // 4
    total = partial[:size].astype(F32)
    parts = [across(partial[k * size : (k + 1) * size], X_LOW * k) for k in (1, 2, 3)]
    for part in parts:
        total = total + part.astype(F32)
    return total.astype(BF)


def dispatch(sent):
    block = jnp.concatenate([shifted(sent[:SLOT], 0), shifted(sent[SLOT:], 1)], axis=0)
    return jnp.concatenate(gather_x(block), axis=0)


def collect(partial):
    half = scatter_x(partial)
    full = (half.astype(F32) + across(half, Y_HI).astype(F32)).astype(BF)
    block = jnp.concatenate([shifted(full[:SLOT], 0), shifted(full[SLOT:], 1)], axis=0)
    own = jnp.concatenate(gather_x(block), axis=0)
    return jnp.concatenate([own, across(own, CORE)], axis=0)


def routing(ids, gates, experts):
    match = ids[None] == experts[:, None, None]
    named = jnp.any(match, axis=2)
    gate = jnp.sum(jnp.where(match, gates[None], 0.0), axis=2)
    tok = ids.shape[0]
    earlier = jnp.asarray(np.triu(np.ones((tok, tok), np.float32), 1), BF)
    before = jnp.dot(named.astype(BF), earlier, preferred_element_type=F32)
    slots = jnp.arange(SLOT, dtype=F32)
    sel = jnp.logical_and(named[:, None, :], before[:, None, :] == slots[None, :, None])
    mix = jnp.where(sel, gate[:, None, :], 0.0)
    rows = experts.shape[0] * SLOT
    return sel.reshape(rows, tok), mix.reshape(rows, tok)


def rdot(a, b):
    return jnp.dot(a, b, preferred_element_type=F32)


def tdot(a, b):
    return jnp.einsum("rd,fd->rf", a, b, preferred_element_type=F32)


def ldot(a, b):
    return jnp.einsum("rt,rd->td", a, b, preferred_element_type=F32)


def per_device(tokens, route_ids, route_gates, w_gate, w_up, w_down, out_grad, latent_grad):
    p = lax.axis_index("pipe")
    s = lax.axis_index("expert")
    wg, wu, wd = w_gate[0], w_up[0], w_down[0]
    wg2, wu2, wd2 = across(wg, CORE), across(wu, CORE), across(wd, CORE)

    latent = latent_grad[0]
    width = latent.shape[1] // 2
    low = p < 8
    mine = jnp.where(low, latent[:, :width], latent[:, width:])
    other = jnp.where(low, latent[:, width:], latent[:, :width])
    got = lax.ppermute(other, "pipe", [(i, 15 - i) for i in range(16)])
    both = (mine.astype(F32) + got.astype(F32)).astype(BF)
    part = jnp.einsum("td,tk->dk", tokens, both, preferred_element_type=F32).astype(BF)
    share = lax.psum_scatter(part, "expert", scatter_dimension=0, tiled=True)
    theirs = lax.ppermute(share, "pipe", [(i, 15 - i) for i in range(16)])
    kv_grad = jnp.concatenate(
        [jnp.where(low, share, theirs), jnp.where(low, theirs, share)], axis=1
    )[None]

    order = np.array([c * 8 + j * 4 + x for c in (0, 1) for x in range(4) for j in (0, 1)])
    experts = s ^ delta(p, 0) ^ jnp.asarray(order, jnp.int32)
    sel, mix = routing(route_ids, route_gates, experts)
    sel_bf = sel.astype(BF)
    first = sel_bf[: 2 * SLOT]
    sent = rdot(first, tokens).astype(BF)
    slot_gate = jnp.sum(mix[: 2 * SLOT], axis=1)
    dsent = (rdot(first, out_grad) * slot_gate[:, None]).astype(BF)

    rows = dispatch(sent)
    drows = dispatch(dsent)

    gate_act = jnp.concatenate([rdot(rows, wg), rdot(rows, wg2)], axis=1)
    up_act = jnp.concatenate([rdot(rows, wu), rdot(rows, wu2)], axis=1)
    sg = jax.nn.sigmoid(gate_act)
    hidden = (gate_act * sg * up_act).astype(BF)
    f = wg.shape[1]
    partial = (rdot(hidden[:, :f], wd) + rdot(hidden[:, f:], wd2)).astype(BF)
    back = collect(partial)
    mix_hi = mix.astype(BF)
    mix_lo = (mix - mix_hi.astype(F32)).astype(BF)
    routed = (ldot(mix_hi, back) + ldot(mix_lo, back)).astype(BF)

    hidden_grad = jnp.concatenate([tdot(drows, wd), tdot(drows, wd2)], axis=1)
    gate_grad = (hidden_grad * up_act * sg * (1.0 + gate_act * (1.0 - sg))).astype(BF)
    up_grad = (hidden_grad * gate_act * sg).astype(BF)
    dpartial = (
        tdot(gate_grad[:, :f], wg)
        + tdot(gate_grad[:, f:], wg2)
        + tdot(up_grad[:, :f], wu)
        + tdot(up_grad[:, f:], wu2)
    ).astype(BF)
    dback = collect(dpartial)
    token_grad = ldot(sel_bf, dback).astype(BF)
    return routed, token_grad, kv_grad


def solution(mesh):
    return jax.shard_map(
        per_device,
        mesh=mesh,
        in_specs=(
            P("expert", None),
            P("expert", None),
            P("expert", None),
            P("expert", None, "pipe"),
            P("expert", None, "pipe"),
            P("expert", "pipe", None),
            P("expert", None),
            P("pipe", "expert", None),
        ),
        out_specs=(P("expert", None), P("expert", None), P("pipe", "expert", None)),
        check_vma=False,
    )
```

time: 465 us -> 195 us (0.42)
  waiting for transfers between devices: 326 us -> 60.9 us
  blocking collectives: 48.7 us -> 0 us
  starting transfers between devices: 28 us -> 71.6 us
  local copies, waits for them, and re-layouts: 4.11 us -> 13.2 us
    psum x1 -> x0, waiting for transfers between devices: 219 us -> none  [settle(): summed = lax.psum(shaped.astype(jnp.bfloat16), 'pipe')]
    all_to_all x3 -> x0, waiting for transfers between devices: 73.7 us -> none  [the longest x2 73.6 us: deliver(): lax.all_to_all(shaped, 'expert', split_axis=0, concat_axis=0, tiled=True)]
    ppermute x4 -> x35, starting transfers between devices: 4.4 us -> 71.6 us  [the longest x25 34.7 us: across(): return lax.ppermute(value, 'pipe', [(i, i ^ mask) for i in range(16)])]
    all_to_all x1 -> x0, blocking collectives: 48.7 us -> none  [settle(): lax.all_to_all(summed, 'expert', split_axis=0, concat_axis=0, tiled=True)]
    ppermute x4 -> x35, waiting for transfers between devices: 33.2 us -> 60.9 us  [the longest x25 41.7 us: across(): return lax.ppermute(value, 'pipe', [(i, i ^ mask) for i in range(16)])]
    all_to_all x3 -> x0, starting transfers between devices: 23.5 us -> none  [the longest x2 17.6 us: deliver(): lax.all_to_all(shaped, 'expert', split_axis=0, concat_axis=0, tiled=True)]
    unnamed x16 -> x27, local copies, waits for them, and re-layouts: 3.41 us -> 11 us
    dot_general x11 -> x19, matrix products: 31.3 us -> 31.7 us  [the longest x8 11 us: rdot(): return jnp.dot(a, b, preferred_element_type=F32)]
  transfers between devices with their start and end apart: 9 -> 36, of which waited for: 8 -> 14; matrix products, arithmetic and copies ran while one was open for 5% -> 22% of each run, Pallas kernels for 0% -> 0%
where the time goes in v1:
time: 195 us; the launch traced here: 194 us
  starting transfers between devices  71.6 us (37%)
  waiting for transfers between devices  60.9 us (31%)
  matrix products  31.7 us (16%)
  between operations  14.5 us (7%)
  local copies, waits for them, and re-layouts  13.2 us (7%)
  other arithmetic  2.27 us (1%)
    ppermute x25, waiting for transfers between devices, across(): return lax.ppermute(value, 'pipe', [(i, i ^ mask) for i in range(16)])  41.7 us
    ppermute x25, starting transfers between devices, across(): return lax.ppermute(value, 'pipe', [(i, i ^ mask) for i in range(16)])  34.7 us
    ppermute x8, starting transfers between devices, shifted(): return lax.ppermute(value, ('pipe', 'expert'), pairs)  26.3 us
    ppermute x8, waiting for transfers between devices, shifted(): return lax.ppermute(value, ('pipe', 'expert'), pairs)  15.6 us
    dot_general x8, matrix products, rdot(): return jnp.dot(a, b, preferred_element_type=F32)  11 us
    unnamed x27, local copies, waits for them, and re-layouts  11 us
    dot_general x6, matrix products, tdot(): return jnp.einsum('rd,fd->rf', a, b, preferred_element_type=F32)  10.6 us
    dot_general x3, matrix products, ldot(): return jnp.einsum('rt,rd->td', a, b, preferred_element_type=F32)  6.18 us
  transfers between devices with their start and end apart: 36, of which 14 were waited for; matrix products, arithmetic and copies ran while one was open for 22% of the time, Pallas kernels for 0%

profile of v1, /device:TPU:1, one launch (start us, length us, event | category | flops | bytes accessed | tf_op | source)
XLA Modules:
  0.0 194.2 jit_solution(12501042461738013050)
XLA Ops:
  7.3 0.8 broadcast_xor_fusion
  8.1 0.8 compare_reduce_fusion
  8.8 0.9 fusion.61
  10.1 4.0 %collective-permute-start = (bf16[8,7168]{1,0:T(8,128)(2,1)S(1)}, bf16[8,7168]{1,0:T(8,128)(2,1)S(1)}, u32[]{:S(2)}, u32[]{:S(2)}) collective-permute-start(bf16[8,7168]{1,0:T(8,128)(2,1)S(1)} %get-tuple-element.42), channel_id=1, source_target_pairs={{0,0},{1,1},{2,2},{3,3},{4,4},{5,5},{6,6},{7,7},{8,8},{9,9},{10,10... | collective-permute-start | bytes 344072 | tf_op jit(solution)/shard_map/ppermute | solution.py:23
  14.2 6.9 %collective-permute-start.1 = (bf16[8,7168]{1,0:T(8,128)(2,1)S(1)}, bf16[8,7168]{1,0:T(8,128)(2,1)S(1)}, u32[]{:S(2)}, u32[]{:S(2)}) collective-permute-start(bf16[8,7168]{1,0:T(8,128)(2,1)S(1)} %get-tuple-element.41), channel_id=1, source_target_pairs={{0,4},{1,5},{2,6},{3,7},{4,0},{5,1},{6,2},{7,3},{8,12},{9,13},{10,... | collective-permute-start | bytes 344072 | tf_op jit(solution)/shard_map/ppermute | solution.py:23
  21.6 5.4 %collective-permute-start.33 = (bf16[128,256]{1,0:T(8,128)(2,1)S(1)}, bf16[128,256]{1,0:T(8,128)(2,1)S(1)}, u32[]{:S(2)}, u32[]{:S(2)}) collective-permute-start(bf16[128,256]{1,0:T(8,128)(2,1)S(1)} %broadcast_select_fusion.2), channel_id=1, source_target_pairs={{0,240},{16,224},{32,208},{48,192},{64,176},{80,160},{96,144},{112... | collective-permute-start | bytes 196616 | tf_op jit(solution)/shard_map/ppermute | solution.py:89
  27.3 1.9 fusion.4
  29.3 2.9 %collective-permute-start.18 = (bf16[8,7168]{1,0:T(8,128)(2,1)S(1)}, bf16[8,7168]{1,0:T(8,128)(2,1)S(1)}, u32[]{:S(2)}, u32[]{:S(2)}) collective-permute-start(bf16[8,7168]{1,0:T(8,128)(2,1)S(1)} %get-tuple-element.32), channel_id=1, source_target_pairs={{0,0},{1,1},{2,2},{3,3},{4,4},{5,5},{6,6},{7,7},{8,8},{9,9},{10,10... | collective-permute-start | bytes 344072 | tf_op jit(solution)/shard_map/ppermute | solution.py:23
  32.2 2.9 %fusion = bf16[7168,256]{0,1:T(8,128)(2,1)} fusion(bf16[128,7168]{1,0:T(8,128)(2,1)S(1)} %copy-done, bf16[128,256]{1,0:T(8,128)(2,1)S(1)} %collective-permute-done.33, pred[]{:T(512)S(6)} %lt.3, bf16[128,512]{1,0:T(8,128)(2,1)S(1)} %bitcast.84), kind=kOutput, calls=%fused_computation.1 | convolution fusion | flops 471760896 | bytes 5701633 | tf_op jit(solution)/shard_map/td,tk->dk/dot_general | solution.py:91
  35.1 5.9 %copy.23 = bf16[7168,256]{1,0:T(8,128)(2,1)} copy(bf16[7168,256]{0,1:T(8,128)(2,1)} %fusion) | data formatting | bytes 7340032
  41.1 1.8 collective-permute-start.19
  43.2 6.9 %collective-permute-done.19 = bf16[8,7168]{1,0:T(8,128)(2,1)S(1)} collective-permute-done((bf16[8,7168]{1,0:T(8,128)(2,1)S(1)}, bf16[8,7168]{1,0:T(8,128)(2,1)S(1)}, u32[]{:S(2)}, u32[]{:S(2)}) %collective-permute-start.19) | collective-permute-done | bytes 114720 | tf_op jit(solution)/shard_map/ppermute | solution.py:23
  50.0 2.0 %collective-permute-start.3 = (bf16[16,7168]{1,0:T(8,128)(2,1)S(1)}, bf16[16,7168]{1,0:T(8,128)(2,1)S(1)}, u32[]{:S(2)}, u32[]{:S(2)}) collective-permute-start(bf16[16,7168]{1,0:T(8,128)(2,1)S(1)} %get-tuple-element.62), channel_id=1, source_target_pairs={{0,128},{16,144},{32,160},{48,176},{64,192},{80,208},{96,224},{112... | collective-permute-start | bytes 688136 | tf_op jit(solution)/shard_map/ppermute | solution.py:14
  52.0 2.7 %collective-permute-start.4 = (bf16[16,7168]{1,0:T(8,128)(2,1)S(1)}, bf16[16,7168]{1,0:T(8,128)(2,1)S(1)}, u32[]{:S(2)}, u32[]{:S(2)}) collective-permute-start(bf16[16,7168]{1,0:T(8,128)(2,1)S(1)} %get-tuple-element.62), channel_id=1, source_target_pairs={{0,192},{16,208},{32,224},{48,240},{64,128},{80,144},{96,160},{112... | collective-permute-start | bytes 688136 | tf_op jit(solution)/shard_map/ppermute | solution.py:14
  54.7 3.6 %collective-permute-done.3 = bf16[16,7168]{1,0:T(8,128)(2,1)S(1)} collective-permute-done((bf16[16,7168]{1,0:T(8,128)(2,1)S(1)}, bf16[16,7168]{1,0:T(8,128)(2,1)S(1)}, u32[]{:S(2)}, u32[]{:S(2)}) %collective-permute-start.3) | collective-permute-done | bytes 229408 | tf_op jit(solution)/shard_map/ppermute | solution.py:14
  58.3 3.0 %collective-permute-start.20 = (bf16[16,7168]{1,0:T(8,128)(2,1)S(1)}, bf16[16,7168]{1,0:T(8,128)(2,1)S(1)}, u32[]{:S(2)}, u32[]{:S(2)}) collective-permute-start(bf16[16,7168]{1,0:T(8,128)(2,1)S(1)} %get-tuple-element.52), channel_id=1, source_target_pairs={{0,64},{16,80},{32,96},{48,112},{64,0},{80,16},{96,32},{112,48},{1... | collective-permute-start | bytes 688136 | tf_op jit(solution)/shard_map/ppermute | solution.py:14
  61.3 3.5 %collective-permute-done.4 = bf16[16,7168]{1,0:T(8,128)(2,1)S(1)} collective-permute-done((bf16[16,7168]{1,0:T(8,128)(2,1)S(1)}, bf16[16,7168]{1,0:T(8,128)(2,1)S(1)}, u32[]{:S(2)}, u32[]{:S(2)}) %collective-permute-start.4) | collective-permute-done | bytes 229408 | tf_op jit(solution)/shard_map/ppermute | solution.py:14
  64.8 1.3 collective-permute-start.21
  66.1 0.7 collective-permute-done.20
  66.8 3.1 %collective-permute-start.22 = (bf16[16,7168]{1,0:T(8,128)(2,1)S(1)}, bf16[16,7168]{1,0:T(8,128)(2,1)S(1)}, u32[]{:S(2)}, u32[]{:S(2)}) collective-permute-start(bf16[16,7168]{1,0:T(8,128)(2,1)S(1)} %get-tuple-element.52), channel_id=1, source_target_pairs={{0,192},{16,208},{32,224},{48,240},{64,128},{80,144},{96,160},{112... | collective-permute-start | bytes 688136 | tf_op jit(solution)/shard_map/ppermute | solution.py:14
  69.9 4.6 %collective-permute-done.21 = bf16[16,7168]{1,0:T(8,128)(2,1)S(1)} collective-permute-done((bf16[16,7168]{1,0:T(8,128)(2,1)S(1)}, bf16[16,7168]{1,0:T(8,128)(2,1)S(1)}, u32[]{:S(2)}, u32[]{:S(2)}) %collective-permute-start.21) | collective-permute-done | bytes 229408 | tf_op jit(solution)/shard_map/ppermute | solution.py:14
  74.6 2.0 %fusion.48 = f32[64,128]{1,0:T(8,128)S(1)} fusion(bf16[64,7168]{1,0:T(8,128)(2,1)S(1)} %constant_dynamic-update-slice_fusion.2, bf16[1,7168,128]{2,1,0:T(8,128)(2,1)} %param.14), kind=kOutput, calls=%fused_computation.117 | convolution fusion | flops 117440512 | bytes 2785280 | tf_op jit(solution)/shard_map/dot_general | solution.py:67
  76.6 2.1 %fusion.51 = f32[64,128]{1,0:T(8,128)S(1)} fusion(bf16[64,7168]{1,0:T(8,128)(2,1)S(1)} %constant_dynamic-update-slice_fusion.2, bf16[1,7168,128]{2,1,0:T(8,128)(2,1)} %param.13), kind=kOutput, calls=%fused_computation.120 | convolution fusion | flops 117440512 | bytes 2785280 | tf_op jit(solution)/shard_map/dot_general | solution.py:67
  78.7 0.9 collective-permute-done.22
  79.6 0.7 fusion.44
  80.4 2.0 %fusion.62 = f32[64,128]{1,0:T(8,128)S(1)} fusion(bf16[64,7168]{1,0:T(8,128)(2,1)S(1)} %constant_dynamic-update-slice_fusion.2, bf16[7168,128]{1,0:T(8,128)(2,1)} %collective-permute-done.5), kind=kOutput, calls=%fused_computation.131 | convolution fusion | flops 117440512 | bytes 2785280 | tf_op jit(solution)/shard_map/dot_general | solution.py:67
  82.4 2.0 %fusion.63 = f32[64,128]{1,0:T(8,128)S(1)} fusion(bf16[64,7168]{1,0:T(8,128)(2,1)S(1)} %constant_dynamic-update-slice_fusion.2, bf16[7168,128]{1,0:T(8,128)(2,1)} %collective-permute-done.6), kind=kOutput, calls=%fused_computation.132 | convolution fusion | flops 117440512 | bytes 2785280 | tf_op jit(solution)/shard_map/dot_general | solution.py:67
  84.4 0.7 fusion.64
  85.2 2.3 %fusion.35 = f32[64,7168]{1,0:T(8,128)S(1)} fusion(bf16[64,256]{1,0:T(8,128)(2,1)S(1)} %get-tuple-element.44, bf16[1,7168,128]{2,1,0:T(8,128)(2,1)} %param.13), kind=kOutput, calls=%fused_computation.102 | convolution fusion | flops 117440512 | bytes 3686400 | tf_op jit(solution)/shard_map/rd,fd->rf/dot_general | solution.py:71
  88.3 2.7 %collective-permute-start.10 = (bf16[16,7168]{1,0:T(8,128)(2,1)S(1)}, bf16[16,7168]{1,0:T(8,128)(2,1)S(1)}, u32[]{:S(2)}, u32[]{:S(2)}) collective-permute-start(bf16[16,7168]{1,0:T(8,128)(2,1)S(1)} %get-tuple-element.19), channel_id=1, source_target_pairs={{0,192},{16,208},{32,224},{48,240},{64,128},{80,144},{96,160},{112... | collective-permute-start | bytes 688136 | tf_op jit(solution)/shard_map/ppermute | solution.py:14
  91.0 1.3 collective-permute-start.9
  92.3 2.3 %convolution_add_fusion.3 = f32[64,7168]{1,0:T(8,128)S(1)} fusion(f32[64,7168]{1,0:T(8,128)S(1)} %fusion.35, bf16[7168,128]{1,0:T(8,128)(2,1)} %collective-permute-done.5, bf16[64,256]{1,0:T(8,128)(2,1)S(1)} %get-tuple-element.44), kind=kOutput, calls=%fused_computation.7 | convolution fusion | flops 117899264 | bytes 5521408 | tf_op jit(solution)/shard_map/rd,fd->rf/dot_general | solution.py:71
  94.6 2.3 %convolution_add_fusion.2 = f32[64,7168]{1,0:T(8,128)S(1)} fusion(f32[64,7168]{1,0:T(8,128)S(1)} %convolution_add_fusion.3, bf16[64,256]{1,0:T(8,128)(2,1)S(1)} %get-tuple-element.43, bf16[1,7168,128]{2,1,0:T(8,128)(2,1)} %param.14), kind=kOutput, calls=%fused_computation.6 | convolution fusion | flops 117899264 | bytes 5521408 | tf_op jit(solution)/shard_map/rd,fd->rf/dot_general | solution.py:71
  96.9 2.3 %fusion.3 = bf16[64,7168]{1,0:T(8,128)(2,1)S(1)} fusion(f32[64,7168]{1,0:T(8,128)S(1)} %convolution_add_fusion.2, bf16[7168,128]{1,0:T(8,128)(2,1)} %collective-permute-done.6, bf16[64,256]{1,0:T(8,128)(2,1)S(1)} %get-tuple-element.43), kind=kOutput, calls=%fused_computation.10 | convolution fusion | flops 118358016 | bytes 4603904 | tf_op jit(solution)/shard_map/rd,fd->rf/dot_general | solution.py:71
  99.5 3.6 %collective-permute-start.24 = (bf16[16,7168]{1,0:T(8,128)(2,1)S(1)}, bf16[16,7168]{1,0:T(8,128)(2,1)S(1)}, u32[]{:S(2)}, u32[]{:S(2)}) collective-permute-start(bf16[16,7168]{1,0:T(8,128)(2,1)S(1)} %get-tuple-element.17), channel_id=1, source_target_pairs={{0,128},{16,144},{32,160},{48,176},{64,192},{80,208},{96,224},{112... | collective-permute-start | bytes 688136 | tf_op jit(solution)/shard_map/ppermute | solution.py:14
  103.3 2.7 %collective-permute-start.11 = (bf16[16,7168]{1,0:T(8,128)(2,1)S(1)}, bf16[16,7168]{1,0:T(8,128)(2,1)S(1)}, u32[]{:S(2)}, u32[]{:S(2)}) collective-permute-start(bf16[16,7168]{1,0:T(8,128)(2,1)S(1)} %add_convert_fusion.3), channel_id=1, source_target_pairs={{0,32},{16,48},{32,0},{48,16},{64,96},{80,112},{96,64},{112,80},{1... | collective-permute-start | bytes 688136 | tf_op jit(solution)/shard_map/ppermute | solution.py:14
  106.0 1.3 collective-permute-done.23
  107.3 5.0 %collective-permute-done.24 = bf16[16,7168]{1,0:T(8,128)(2,1)S(1)} collective-permute-done((bf16[16,7168]{1,0:T(8,128)(2,1)S(1)}, bf16[16,7168]{1,0:T(8,128)(2,1)S(1)}, u32[]{:S(2)}, u32[]{:S(2)}) %collective-permute-start.24) | collective-permute-done | bytes 229408 | tf_op jit(solution)/shard_map/ppermute | solution.py:14
  112.4 3.0 %collective-permute-done.25 = bf16[16,7168]{1,0:T(8,128)(2,1)S(1)} collective-permute-done((bf16[16,7168]{1,0:T(8,128)(2,1)S(1)}, bf16[16,7168]{1,0:T(8,128)(2,1)S(1)}, u32[]{:S(2)}, u32[]{:S(2)}) %collective-permute-start.25) | collective-permute-done | bytes 229408 | tf_op jit(solution)/shard_map/ppermute | solution.py:14
  115.5 2.8 %collective-permute-start.26 = (bf16[16,7168]{1,0:T(8,128)(2,1)S(1)}, bf16[16,7168]{1,0:T(8,128)(2,1)S(1)}, u32[]{:S(2)}, u32[]{:S(2)}) collective-permute-start(bf16[16,7168]{1,0:T(8,128)(2,1)S(1)} %add_convert_fusion.1), channel_id=1, source_target_pairs={{0,32},{16,48},{32,0},{48,16},{64,96},{80,112},{96,64},{112,80},{1... | collective-permute-start | bytes 688136 | tf_op jit(solution)/shard_map/ppermute | solution.py:14
  118.3 1.9 collective-permute-start.12
  120.3 2.1 %collective-permute-done.26 = bf16[16,7168]{1,0:T(8,128)(2,1)S(1)} collective-permute-done((bf16[16,7168]{1,0:T(8,128)(2,1)S(1)}, bf16[16,7168]{1,0:T(8,128)(2,1)S(1)}, u32[]{:S(2)}, u32[]{:S(2)}) %collective-permute-start.26) | collective-permute-done | bytes 229408 | tf_op jit(solution)/shard_map/ppermute | solution.py:14
  122.4 2.4 %collective-permute-start.27 = (bf16[8,7168]{1,0:T(8,128)(2,1)S(1)}, bf16[8,7168]{1,0:T(8,128)(2,1)S(1)}, u32[]{:S(2)}, u32[]{:S(2)}) collective-permute-start(bf16[8,7168]{1,0:T(8,128)(2,1)S(1)} %get-tuple-element.30), channel_id=1, source_target_pairs={{0,0},{1,1},{2,2},{3,3},{4,4},{5,5},{6,6},{7,7},{8,8},{9,9},{10,10... | collective-permute-start | bytes 344072 | tf_op jit(solution)/shard_map/ppermute | solution.py:23
  124.8 2.7 %collective-permute-start.28 = (bf16[8,7168]{1,0:T(8,128)(2,1)S(1)}, bf16[8,7168]{1,0:T(8,128)(2,1)S(1)}, u32[]{:S(2)}, u32[]{:S(2)}) collective-permute-start(bf16[8,7168]{1,0:T(8,128)(2,1)S(1)} %get-tuple-element.29), channel_id=1, source_target_pairs={{0,4},{1,5},{2,6},{3,7},{4,0},{5,1},{6,2},{7,3},{8,12},{9,13},{10,... | collective-permute-start | bytes 344072 | tf_op jit(solution)/shard_map/ppermute | solution.py:23
  127.5 3.6 %collective-permute-start.13 = (bf16[8,7168]{1,0:T(8,128)(2,1)S(1)}, bf16[8,7168]{1,0:T(8,128)(2,1)S(1)}, u32[]{:S(2)}, u32[]{:S(2)}) collective-permute-start(bf16[8,7168]{1,0:T(8,128)(2,1)S(1)} %get-tuple-element.39), channel_id=1, source_target_pairs={{0,4},{1,5},{2,6},{3,7},{4,0},{5,1},{6,2},{7,3},{8,12},{9,13},{10,... | collective-permute-start | bytes 344072 | tf_op jit(solution)/shard_map/ppermute | solution.py:23
  131.2 8.7 %collective-permute-done.13 = bf16[8,7168]{1,0:T(8,128)(2,1)S(1)} collective-permute-done((bf16[8,7168]{1,0:T(8,128)(2,1)S(1)}, bf16[8,7168]{1,0:T(8,128)(2,1)S(1)}, u32[]{:S(2)}, u32[]{:S(2)}) %collective-permute-start.13) | collective-permute-done | bytes 114720 | tf_op jit(solution)/shard_map/ppermute | solution.py:23
  140.7 0.7 constant_dynamic-update-slice_fusion.32
  141.4 1.4 collective-permute-start.29
  142.9 2.4 %collective-permute-start.31 = (bf16[16,7168]{1,0:T(8,128)(2,1)S(1)}, bf16[16,7168]{1,0:T(8,128)(2,1)S(1)}, u32[]{:S(2)}, u32[]{:S(2)}) collective-permute-start(bf16[16,7168]{1,0:T(8,128)(2,1)S(1)} %get-tuple-element.48), channel_id=1, source_target_pairs={{0,192},{16,208},{32,224},{48,240},{64,128},{80,144},{96,160},{112... | collective-permute-start | bytes 688136 | tf_op jit(solution)/shard_map/ppermute | solution.py:14
  145.8 2.1 %collective-permute-start.16 = (bf16[16,7168]{1,0:T(8,128)(2,1)S(1)}, bf16[16,7168]{1,0:T(8,128)(2,1)S(1)}, u32[]{:S(2)}, u32[]{:S(2)}) collective-permute-start(bf16[16,7168]{1,0:T(8,128)(2,1)S(1)} %get-tuple-element.58), channel_id=1, source_target_pairs={{0,192},{16,208},{32,224},{48,240},{64,128},{80,144},{96,160},{112... | collective-permute-start | bytes 688136 | tf_op jit(solution)/shard_map/ppermute | solution.py:14
  147.9 10.7 %collective-permute-done.15 = bf16[16,7168]{1,0:T(8,128)(2,1)S(1)} collective-permute-done((bf16[16,7168]{1,0:T(8,128)(2,1)S(1)}, bf16[16,7168]{1,0:T(8,128)(2,1)S(1)}, u32[]{:S(2)}, u32[]{:S(2)}) %collective-permute-start.15) | collective-permute-done | bytes 229408 | tf_op jit(solution)/shard_map/ppermute | solution.py:14
  158.7 6.3 %collective-permute-done.16 = bf16[16,7168]{1,0:T(8,128)(2,1)S(1)} collective-permute-done((bf16[16,7168]{1,0:T(8,128)(2,1)S(1)}, bf16[16,7168]{1,0:T(8,128)(2,1)S(1)}, u32[]{:S(2)}, u32[]{:S(2)}) %collective-permute-start.16) | collective-permute-done | bytes 229408 | tf_op jit(solution)/shard_map/ppermute | solution.py:14
  165.0 1.9 collective-permute-start.17
  167.0 0.7 constant_dynamic-update-slice_fusion.31
  167.7 0.7 constant_dynamic-update-slice_fusion.30
  168.4 0.7 constant_dynamic-update-slice_fusion.29
  169.2 0.7 fusion.17
  170.0 2.0 %fusion.1 = bf16[128,7168]{1,0:T(8,128)(2,1)} fusion(f32[128,7168]{1,0:T(8,128)S(1)} %fusion.17, bf16[128,7168]{1,0:T(8,128)(2,1)S(1)} %constant_dynamic-update-slice_fusion.14, f32[16,128]{1,0:T(8,128)S(1)} %fusion.5, f32[128]{0:T(128)S(1)} %eq.44, f32[16,128]{1,0:T(8,128)S(1)} %fusion.61, pred[16,128]{1,0:T(8,128)(4,1)S(1)} %compare_reduce_fusion), kind=kOutput, calls=%fused_computation.3 | convolution fusion | flops 236765184 | bytes 7358976 | tf_op jit(solution)/shard_map/rt,rd->td/dot_general | solution.py:75
  172.0 1.0 constant_dynamic-update-slice_fusion.34
  173.0 1.1 copy.24
  174.1 5.2 %collective-permute-start.34 = (bf16[448,256]{0,1:T(8,128)(2,1)S(1)}, bf16[448,256]{0,1:T(8,128)(2,1)S(1)}, u32[]{:S(2)}, u32[]{:S(2)}) collective-permute-start(bf16[448,256]{0,1:T(8,128)(2,1)S(1)} %copy.24), channel_id=1, source_target_pairs={{0,240},{16,224},{32,208},{48,192},{64,176},{80,160},{96,144},{112... | collective-permute-start | bytes 688136 | tf_op jit(solution)/shard_map/ppermute | solution.py:93
  179.3 3.5 %convolution_convert_fusion.1 = bf16[128,7168]{1,0:T(8,128)(2,1)} fusion(bf16[128,7168]{1,0:T(8,128)(2,1)} %constant_dynamic-update-slice_fusion.34, f32[128]{0:T(128)S(1)} %eq.44, f32[16,128]{1,0:T(8,128)S(1)} %fusion.61, pred[16,128]{1,0:T(8,128)(4,1)S(1)} %compare_reduce_fusion), kind=kOutput, calls=%fused_computation.4 | convolution fusion | flops 235831296 | bytes 3680768 | tf_op jit(solution)/shard_map/rt,rd->td/dot_general | solution.py:75
  182.7 3.5 %collective-permute-done.34 = bf16[448,256]{0,1:T(8,128)(2,1)S(1)} collective-permute-done((bf16[448,256]{0,1:T(8,128)(2,1)S(1)}, bf16[448,256]{0,1:T(8,128)(2,1)S(1)}, u32[]{:S(2)}, u32[]{:S(2)}) %collective-permute-start.34) | collective-permute-done | bytes 229408 | tf_op jit(solution)/shard_map/ppermute | solution.py:93
  186.4 1.0 copy.22
  (86 shorter events, 5.1 us)
Async XLA Ops:
  7.2 2.6 %copy-start = (bf16[128,7168]{1,0:T(8,128)(2,1)S(1)}, bf16[128,7168]{1,0:T(8,128)(2,1)}, u32[]{:S(2)}) copy-start(bf16[128,7168]{1,0:T(8,128)(2,1)} %param.10) | copy-start | bytes 5505028
  7.2 19.8 %copy-start.3 = (s32[128,8]{0,1:T(8,128)S(1)}, s32[128,8]{0,1:T(8,128)}, u32[]{:S(2)}) copy-start(s32[128,8]{0,1:T(8,128)} %param.11) | copy-start | bytes 12292
  7.2 14.4 %copy-start.2 = (bf16[1,128,512]{2,1,0:T(8,128)(2,1)S(1)}, bf16[1,128,512]{2,1,0:T(8,128)(2,1)}, u32[]{:S(2)}) copy-start(bf16[1,128,512]{2,1,0:T(8,128)(2,1)} %param.17) | copy-start | bytes 393220
  7.2 19.8 %copy-start.4 = (f32[128,8]{0,1:T(8,128)S(1)}, f32[128,8]{0,1:T(8,128)}, u32[]{:S(2)}) copy-start(f32[128,8]{0,1:T(8,128)} %param.12) | copy-start | bytes 12292
  7.2 165.8 %reduce-scatter.4.cloned.1.call-start = ((), (), s32[]{:S(2)}) async-start(), calls=%async_computation.1 | async-start | bytes 3899392
  10.1 30.9 %collective-permute-start = (bf16[8,7168]{1,0:T(8,128)(2,1)S(1)}, bf16[8,7168]{1,0:T(8,128)(2,1)S(1)}, u32[]{:S(2)}, u32[]{:S(2)}) collective-permute-start(bf16[8,7168]{1,0:T(8,128)(2,1)S(1)} %get-tuple-element.42), channel_id=1, source_target_pairs={{0,0},{1,1},{2,2},{3,3},{4,4},{5,5},{6,6},{7,7},{8,8},{9,9},{10,10... | collective-permute-start | bytes 344072 | tf_op jit(solution)/shard_map/ppermute | solution.py:23
  14.2 28.7 %collective-permute-start.1 = (bf16[8,7168]{1,0:T(8,128)(2,1)S(1)}, bf16[8,7168]{1,0:T(8,128)(2,1)S(1)}, u32[]{:S(2)}, u32[]{:S(2)}) collective-permute-start(bf16[8,7168]{1,0:T(8,128)(2,1)S(1)} %get-tuple-element.41), channel_id=1, source_target_pairs={{0,4},{1,5},{2,6},{3,7},{4,0},{5,1},{6,2},{7,3},{8,12},{9,13},{10,... | collective-permute-start | bytes 344072 | tf_op jit(solution)/shard_map/ppermute | solution.py:23
  21.1 59.3 %collective-permute-start.5 = (bf16[7168,128]{1,0:T(8,128)(2,1)}, bf16[7168,128]{1,0:T(8,128)(2,1)}, u32[]{:S(2)}, u32[]{:S(2)}) collective-permute-start(bf16[7168,128]{1,0:T(8,128)(2,1)} %bitcast.4), channel_id=1, source_target_pairs={{0,16},{16,0},{32,48},{48,32},{64,80},{80,64},{96,112},{112,96},{1... | collective-permute-start | bytes 5505032 | tf_op jit(solution)/shard_map/ppermute | solution.py:14
  21.1 61.3 %collective-permute-start.6 = (bf16[7168,128]{1,0:T(8,128)(2,1)}, bf16[7168,128]{1,0:T(8,128)(2,1)}, u32[]{:S(2)}, u32[]{:S(2)}) collective-permute-start(bf16[7168,128]{1,0:T(8,128)(2,1)} %bitcast.5), channel_id=1, source_target_pairs={{0,16},{16,0},{32,48},{48,32},{64,80},{80,64},{96,112},{112,96},{1... | collective-permute-start | bytes 5505032 | tf_op jit(solution)/shard_map/ppermute | solution.py:14
  21.6 7.7 %collective-permute-start.33 = (bf16[128,256]{1,0:T(8,128)(2,1)S(1)}, bf16[128,256]{1,0:T(8,128)(2,1)S(1)}, u32[]{:S(2)}, u32[]{:S(2)}) collective-permute-start(bf16[128,256]{1,0:T(8,128)(2,1)S(1)} %broadcast_select_fusion.2), channel_id=1, source_target_pairs={{0,240},{16,224},{32,208},{48,192},{64,176},{80,160},{96,144},{112... | collective-permute-start | bytes 196616 | tf_op jit(solution)/shard_map/ppermute | solution.py:89
  29.3 13.7 %collective-permute-start.18 = (bf16[8,7168]{1,0:T(8,128)(2,1)S(1)}, bf16[8,7168]{1,0:T(8,128)(2,1)S(1)}, u32[]{:S(2)}, u32[]{:S(2)}) collective-permute-start(bf16[8,7168]{1,0:T(8,128)(2,1)S(1)} %get-tuple-element.32), channel_id=1, source_target_pairs={{0,0},{1,1},{2,2},{3,3},{4,4},{5,5},{6,6},{7,7},{8,8},{9,9},{10,10... | collective-permute-start | bytes 344072 | tf_op jit(solution)/shard_map/ppermute | solution.py:23
  41.1 8.9 %collective-permute-start.19 = (bf16[8,7168]{1,0:T(8,128)(2,1)S(1)}, bf16[8,7168]{1,0:T(8,128)(2,1)S(1)}, u32[]{:S(2)}, u32[]{:S(2)}) collective-permute-start(bf16[8,7168]{1,0:T(8,128)(2,1)S(1)} %get-tuple-element.31), channel_id=1, source_target_pairs={{0,4},{1,5},{2,6},{3,7},{4,0},{5,1},{6,2},{7,3},{8,12},{9,13},{10,... | collective-permute-start | bytes 344072 | tf_op jit(solution)/shard_map/ppermute | solution.py:23
  42.9 41.5 %collective-permute-start.7 = (bf16[128,7168]{1,0:T(8,128)(2,1)}, bf16[128,7168]{1,0:T(8,128)(2,1)S(1)}, u32[]{:S(2)}, u32[]{:S(2)}) collective-permute-start(bf16[128,7168]{1,0:T(8,128)(2,1)} %bitcast.82), channel_id=1, source_target_pairs={{0,16},{16,0},{32,48},{48,32},{64,80},{80,64},{96,112},{112,96},{1... | collective-permute-start | bytes 5505032 | tf_op jit(solution)/shard_map/ppermute | solution.py:14
  43.0 9.0 %collective-permute-start.2 = (bf16[16,7168]{1,0:T(8,128)(2,1)S(1)}, bf16[16,7168]{1,0:T(8,128)(2,1)S(1)}, u32[]{:S(2)}, u32[]{:S(2)}) collective-permute-start(bf16[16,7168]{1,0:T(8,128)(2,1)S(1)} %get-tuple-element.62), channel_id=1, source_target_pairs={{0,64},{16,80},{32,96},{48,112},{64,0},{80,16},{96,32},{112,48},{1... | collective-permute-start | bytes 688136 | tf_op jit(solution)/shard_map/ppermute | solution.py:14
  50.0 8.3 %collective-permute-start.3 = (bf16[16,7168]{1,0:T(8,128)(2,1)S(1)}, bf16[16,7168]{1,0:T(8,128)(2,1)S(1)}, u32[]{:S(2)}, u32[]{:S(2)}) collective-permute-start(bf16[16,7168]{1,0:T(8,128)(2,1)S(1)} %get-tuple-element.62), channel_id=1, source_target_pairs={{0,128},{16,144},{32,160},{48,176},{64,192},{80,208},{96,224},{112... | collective-permute-start | bytes 688136 | tf_op jit(solution)/shard_map/ppermute | solution.py:14
  52.0 12.7 %collective-permute-start.4 = (bf16[16,7168]{1,0:T(8,128)(2,1)S(1)}, bf16[16,7168]{1,0:T(8,128)(2,1)S(1)}, u32[]{:S(2)}, u32[]{:S(2)}) collective-permute-start(bf16[16,7168]{1,0:T(8,128)(2,1)S(1)} %get-tuple-element.62), channel_id=1, source_target_pairs={{0,192},{16,208},{32,224},{48,240},{64,128},{80,144},{96,160},{112... | collective-permute-start | bytes 688136 | tf_op jit(solution)/shard_map/ppermute | solution.py:14
  58.3 8.5 %collective-permute-start.20 = (bf16[16,7168]{1,0:T(8,128)(2,1)S(1)}, bf16[16,7168]{1,0:T(8,128)(2,1)S(1)}, u32[]{:S(2)}, u32[]{:S(2)}) collective-permute-start(bf16[16,7168]{1,0:T(8,128)(2,1)S(1)} %get-tuple-element.52), channel_id=1, source_target_pairs={{0,64},{16,80},{32,96},{48,112},{64,0},{80,16},{96,32},{112,48},{1... | collective-permute-start | bytes 688136 | tf_op jit(solution)/shard_map/ppermute | solution.py:14
  64.8 9.8 %collective-permute-start.21 = (bf16[16,7168]{1,0:T(8,128)(2,1)S(1)}, bf16[16,7168]{1,0:T(8,128)(2,1)S(1)}, u32[]{:S(2)}, u32[]{:S(2)}) collective-permute-start(bf16[16,7168]{1,0:T(8,128)(2,1)S(1)} %get-tuple-element.52), channel_id=1, source_target_pairs={{0,128},{16,144},{32,160},{48,176},{64,192},{80,208},{96,224},{112... | collective-permute-start | bytes 688136 | tf_op jit(solution)/shard_map/ppermute | solution.py:14
  66.8 12.8 %collective-permute-start.22 = (bf16[16,7168]{1,0:T(8,128)(2,1)S(1)}, bf16[16,7168]{1,0:T(8,128)(2,1)S(1)}, u32[]{:S(2)}, u32[]{:S(2)}) collective-permute-start(bf16[16,7168]{1,0:T(8,128)(2,1)S(1)} %get-tuple-element.52), channel_id=1, source_target_pairs={{0,192},{16,208},{32,224},{48,240},{64,128},{80,144},{96,160},{112... | collective-permute-start | bytes 688136 | tf_op jit(solution)/shard_map/ppermute | solution.py:14
  76.6 3.0 %copy-start.1 = (bf16[1,128,7168]{2,1,0:T(8,128)(2,1)S(1)}, bf16[1,128,7168]{2,1,0:T(8,128)(2,1)}, u32[]{:S(2)}) copy-start(bf16[1,128,7168]{2,1,0:T(8,128)(2,1)} %param.15) | copy-start | bytes 5505028
  88.3 14.8 %collective-permute-start.10 = (bf16[16,7168]{1,0:T(8,128)(2,1)S(1)}, bf16[16,7168]{1,0:T(8,128)(2,1)S(1)}, u32[]{:S(2)}, u32[]{:S(2)}) collective-permute-start(bf16[16,7168]{1,0:T(8,128)(2,1)S(1)} %get-tuple-element.19), channel_id=1, source_target_pairs={{0,192},{16,208},{32,224},{48,240},{64,128},{80,144},{96,160},{112... | collective-permute-start | bytes 688136 | tf_op jit(solution)/shard_map/ppermute | solution.py:14
  91.0 12.2 %collective-permute-start.8 = (bf16[16,7168]{1,0:T(8,128)(2,1)S(1)}, bf16[16,7168]{1,0:T(8,128)(2,1)S(1)}, u32[]{:S(2)}, u32[]{:S(2)}) collective-permute-start(bf16[16,7168]{1,0:T(8,128)(2,1)S(1)} %get-tuple-element.18), channel_id=1, source_target_pairs={{0,64},{16,80},{32,96},{48,112},{64,0},{80,16},{96,32},{112,48},{1... | collective-permute-start | bytes 688136 | tf_op jit(solution)/shard_map/ppermute | solution.py:14
  91.0 12.2 %collective-permute-start.9 = (bf16[16,7168]{1,0:T(8,128)(2,1)S(1)}, bf16[16,7168]{1,0:T(8,128)(2,1)S(1)}, u32[]{:S(2)}, u32[]{:S(2)}) collective-permute-start(bf16[16,7168]{1,0:T(8,128)(2,1)S(1)} %get-tuple-element.20), channel_id=1, source_target_pairs={{0,128},{16,144},{32,160},{48,176},{64,192},{80,208},{96,224},{112... | collective-permute-start | bytes 688136 | tf_op jit(solution)/shard_map/ppermute | solution.py:14
  99.2 8.1 %collective-permute-start.23 = (bf16[16,7168]{1,0:T(8,128)(2,1)S(1)}, bf16[16,7168]{1,0:T(8,128)(2,1)S(1)}, u32[]{:S(2)}, u32[]{:S(2)}) collective-permute-start(bf16[16,7168]{1,0:T(8,128)(2,1)S(1)} %get-tuple-element.15), channel_id=1, source_target_pairs={{0,64},{16,80},{32,96},{48,112},{64,0},{80,16},{96,32},{112,48},{1... | collective-permute-start | bytes 688136 | tf_op jit(solution)/shard_map/ppermute | solution.py:14
  99.5 12.9 %collective-permute-start.24 = (bf16[16,7168]{1,0:T(8,128)(2,1)S(1)}, bf16[16,7168]{1,0:T(8,128)(2,1)S(1)}, u32[]{:S(2)}, u32[]{:S(2)}) collective-permute-start(bf16[16,7168]{1,0:T(8,128)(2,1)S(1)} %get-tuple-element.17), channel_id=1, source_target_pairs={{0,128},{16,144},{32,160},{48,176},{64,192},{80,208},{96,224},{112... | collective-permute-start | bytes 688136 | tf_op jit(solution)/shard_map/ppermute | solution.py:14
  103.1 12.3 %collective-permute-start.25 = (bf16[16,7168]{1,0:T(8,128)(2,1)S(1)}, bf16[16,7168]{1,0:T(8,128)(2,1)S(1)}, u32[]{:S(2)}, u32[]{:S(2)}) collective-permute-start(bf16[16,7168]{1,0:T(8,128)(2,1)S(1)} %get-tuple-element.16), channel_id=1, source_target_pairs={{0,192},{16,208},{32,224},{48,240},{64,128},{80,144},{96,160},{112... | collective-permute-start | bytes 688136 | tf_op jit(solution)/shard_map/ppermute | solution.py:14
  103.3 15.0 %collective-permute-start.11 = (bf16[16,7168]{1,0:T(8,128)(2,1)S(1)}, bf16[16,7168]{1,0:T(8,128)(2,1)S(1)}, u32[]{:S(2)}, u32[]{:S(2)}) collective-permute-start(bf16[16,7168]{1,0:T(8,128)(2,1)S(1)} %add_convert_fusion.3), channel_id=1, source_target_pairs={{0,32},{16,48},{32,0},{48,16},{64,96},{80,112},{96,64},{112,80},{1... | collective-permute-start | bytes 688136 | tf_op jit(solution)/shard_map/ppermute | solution.py:14
  115.5 6.9 %collective-permute-start.26 = (bf16[16,7168]{1,0:T(8,128)(2,1)S(1)}, bf16[16,7168]{1,0:T(8,128)(2,1)S(1)}, u32[]{:S(2)}, u32[]{:S(2)}) collective-permute-start(bf16[16,7168]{1,0:T(8,128)(2,1)S(1)} %add_convert_fusion.1), channel_id=1, source_target_pairs={{0,32},{16,48},{32,0},{48,16},{64,96},{80,112},{96,64},{112,80},{1... | collective-permute-start | bytes 688136 | tf_op jit(solution)/shard_map/ppermute | solution.py:14
  118.3 12.8 %collective-permute-start.12 = (bf16[8,7168]{1,0:T(8,128)(2,1)S(1)}, bf16[8,7168]{1,0:T(8,128)(2,1)S(1)}, u32[]{:S(2)}, u32[]{:S(2)}) collective-permute-start(bf16[8,7168]{1,0:T(8,128)(2,1)S(1)} %get-tuple-element.40), channel_id=1, source_target_pairs={{0,0},{1,1},{2,2},{3,3},{4,4},{5,5},{6,6},{7,7},{8,8},{9,9},{10,10... | collective-permute-start | bytes 344072 | tf_op jit(solution)/shard_map/ppermute | solution.py:23
  122.4 17.6 %collective-permute-start.27 = (bf16[8,7168]{1,0:T(8,128)(2,1)S(1)}, bf16[8,7168]{1,0:T(8,128)(2,1)S(1)}, u32[]{:S(2)}, u32[]{:S(2)}) collective-permute-start(bf16[8,7168]{1,0:T(8,128)(2,1)S(1)} %get-tuple-element.30), channel_id=1, source_target_pairs={{0,0},{1,1},{2,2},{3,3},{4,4},{5,5},{6,6},{7,7},{8,8},{9,9},{10,10... | collective-permute-start | bytes 344072 | tf_op jit(solution)/shard_map/ppermute | solution.py:23
  124.8 15.9 %collective-permute-start.28 = (bf16[8,7168]{1,0:T(8,128)(2,1)S(1)}, bf16[8,7168]{1,0:T(8,128)(2,1)S(1)}, u32[]{:S(2)}, u32[]{:S(2)}) collective-permute-start(bf16[8,7168]{1,0:T(8,128)(2,1)S(1)} %get-tuple-element.29), channel_id=1, source_target_pairs={{0,4},{1,5},{2,6},{3,7},{4,0},{5,1},{6,2},{7,3},{8,12},{9,13},{10,... | collective-permute-start | bytes 344072 | tf_op jit(solution)/shard_map/ppermute | solution.py:23
  127.5 12.4 %collective-permute-start.13 = (bf16[8,7168]{1,0:T(8,128)(2,1)S(1)}, bf16[8,7168]{1,0:T(8,128)(2,1)S(1)}, u32[]{:S(2)}, u32[]{:S(2)}) collective-permute-start(bf16[8,7168]{1,0:T(8,128)(2,1)S(1)} %get-tuple-element.39), channel_id=1, source_target_pairs={{0,4},{1,5},{2,6},{3,7},{4,0},{5,1},{6,2},{7,3},{8,12},{9,13},{10,... | collective-permute-start | bytes 344072 | tf_op jit(solution)/shard_map/ppermute | solution.py:23
  140.0 5.9 %collective-permute-start.14 = (bf16[16,7168]{1,0:T(8,128)(2,1)S(1)}, bf16[16,7168]{1,0:T(8,128)(2,1)S(1)}, u32[]{:S(2)}, u32[]{:S(2)}) collective-permute-start(bf16[16,7168]{1,0:T(8,128)(2,1)S(1)} %get-tuple-element.58), channel_id=1, source_target_pairs={{0,64},{16,80},{32,96},{48,112},{64,0},{80,16},{96,32},{112,48},{1... | collective-permute-start | bytes 688136 | tf_op jit(solution)/shard_map/ppermute | solution.py:14
  141.4 25.5 %collective-permute-start.29 = (bf16[16,7168]{1,0:T(8,128)(2,1)S(1)}, bf16[16,7168]{1,0:T(8,128)(2,1)S(1)}, u32[]{:S(2)}, u32[]{:S(2)}) collective-permute-start(bf16[16,7168]{1,0:T(8,128)(2,1)S(1)} %get-tuple-element.48), channel_id=1, source_target_pairs={{0,64},{16,80},{32,96},{48,112},{64,0},{80,16},{96,32},{112,48},{1... | collective-permute-start | bytes 688136 | tf_op jit(solution)/shard_map/ppermute | solution.py:14
  142.9 24.8 %collective-permute-start.30 = (bf16[16,7168]{1,0:T(8,128)(2,1)S(1)}, bf16[16,7168]{1,0:T(8,128)(2,1)S(1)}, u32[]{:S(2)}, u32[]{:S(2)}) collective-permute-start(bf16[16,7168]{1,0:T(8,128)(2,1)S(1)} %get-tuple-element.48), channel_id=1, source_target_pairs={{0,128},{16,144},{32,160},{48,176},{64,192},{80,208},{96,224},{112... | collective-permute-start | bytes 688136 | tf_op jit(solution)/shard_map/ppermute | solution.py:14
  142.9 25.6 %collective-permute-start.31 = (bf16[16,7168]{1,0:T(8,128)(2,1)S(1)}, bf16[16,7168]{1,0:T(8,128)(2,1)S(1)}, u32[]{:S(2)}, u32[]{:S(2)}) collective-permute-start(bf16[16,7168]{1,0:T(8,128)(2,1)S(1)} %get-tuple-element.48), channel_id=1, source_target_pairs={{0,192},{16,208},{32,224},{48,240},{64,128},{80,144},{96,160},{112... | collective-permute-start | bytes 688136 | tf_op jit(solution)/shard_map/ppermute | solution.py:14
  145.3 13.3 %collective-permute-start.15 = (bf16[16,7168]{1,0:T(8,128)(2,1)S(1)}, bf16[16,7168]{1,0:T(8,128)(2,1)S(1)}, u32[]{:S(2)}, u32[]{:S(2)}) collective-permute-start(bf16[16,7168]{1,0:T(8,128)(2,1)S(1)} %get-tuple-element.58), channel_id=1, source_target_pairs={{0,128},{16,144},{32,160},{48,176},{64,192},{80,208},{96,224},{112... | collective-permute-start | bytes 688136 | tf_op jit(solution)/shard_map/ppermute | solution.py:14
  145.8 19.2 %collective-permute-start.16 = (bf16[16,7168]{1,0:T(8,128)(2,1)S(1)}, bf16[16,7168]{1,0:T(8,128)(2,1)S(1)}, u32[]{:S(2)}, u32[]{:S(2)}) collective-permute-start(bf16[16,7168]{1,0:T(8,128)(2,1)S(1)} %get-tuple-element.58), channel_id=1, source_target_pairs={{0,192},{16,208},{32,224},{48,240},{64,128},{80,144},{96,160},{112... | collective-permute-start | bytes 688136 | tf_op jit(solution)/shard_map/ppermute | solution.py:14
  165.0 4.1 %collective-permute-start.17 = (bf16[64,7168]{1,0:T(8,128)(2,1)S(1)}, bf16[64,7168]{1,0:T(8,128)(2,1)S(1)}, u32[]{:S(2)}, u32[]{:S(2)}) collective-permute-start(bf16[64,7168]{1,0:T(8,128)(2,1)S(1)} %get-tuple-element.33), channel_id=1, source_target_pairs={{0,16},{16,0},{32,48},{48,32},{64,80},{80,64},{96,112},{112,96},{1... | collective-permute-start | bytes 2752520 | tf_op jit(solution)/shard_map/ppermute | solution.py:14
  169.2 2.8 %collective-permute-start.32 = (bf16[64,7168]{1,0:T(8,128)(2,1)S(1)}, bf16[64,7168]{1,0:T(8,128)(2,1)S(1)}, u32[]{:S(2)}, u32[]{:S(2)}) collective-permute-start(bf16[64,7168]{1,0:T(8,128)(2,1)S(1)} %get-tuple-element.23), channel_id=1, source_target_pairs={{0,16},{16,0},{32,48},{48,32},{64,80},{80,64},{96,112},{112,96},{1... | collective-permute-start | bytes 2752520 | tf_op jit(solution)/shard_map/ppermute | solution.py:14
  174.1 12.2 %collective-permute-start.34 = (bf16[448,256]{0,1:T(8,128)(2,1)S(1)}, bf16[448,256]{0,1:T(8,128)(2,1)S(1)}, u32[]{:S(2)}, u32[]{:S(2)}) collective-permute-start(bf16[448,256]{0,1:T(8,128)(2,1)S(1)} %copy.24), channel_id=1, source_target_pairs={{0,240},{16,224},{32,208},{48,192},{64,176},{80,160},{96,144},{112... | collective-permute-start | bytes 688136 | tf_op jit(solution)/shard_map/ppermute | solution.py:93
Sparse Core Ops, SparseCore 0:
  41.2 67.4 reduce-scatter.3

commit v2 on v1

v2 whole, which is shorter than its diff:
```python
import functools
import jax
import jax.numpy as jnp
from jax import lax
from jax.experimental import pallas as pl
from jax.experimental.pallas import tpu as pltpu
from jax.sharding import PartitionSpec as P

SLOT = 8
BF = jnp.bfloat16
F32 = jnp.float32
CORE, Y_HI, X_LOW = 1, 2, 4
STEPS = 4


def across(value, mask):
    return lax.ppermute(value, "pipe", [(i, i ^ mask) for i in range(16)])


def delta(p, k):
    return (p & 1) * 8 + (k ^ ((p >> 1) & 1)) * 4 + (p >> 2)


def shifted(value, k, mask=0):
    pairs = [
        (p * 16 + e, (p ^ mask) * 16 + (e ^ delta(p, k))) for p in range(16) for e in range(16)
    ]
    return lax.ppermute(value, ("pipe", "expert"), pairs)


def along_x(value, step):
    pairs = []
    for i in range(16):
        hop = 3 if (i & 1) ^ step else 1
        pairs.append((i, i ^ (X_LOW * hop)))
    return lax.ppermute(value, "pipe", pairs)


def dispatch(first, second):
    block = jnp.concatenate([shifted(first, 0), shifted(second, 1)], axis=0)
    two = jnp.concatenate([block, along_x(block, 0)], axis=0)
    return jnp.concatenate([two, along_x(two, 1)], axis=0)


def add(a, b):
    return (a.astype(F32) + b.astype(F32)).astype(BF)


def collect(kept, sent):
    two = add(kept, along_x(sent, 1))
    size = two.shape[0] // 2
    one = add(two[:size], along_x(two[size:], 0))
    full = add(one[:SLOT], across(one[SLOT:], Y_HI))
    block = jnp.concatenate([shifted(full, 0), shifted(full, 0, Y_HI)], axis=0)
    two = jnp.concatenate([block, along_x(block, 0)], axis=0)
    far = along_x(two, 1)
    return two, far, across(two, CORE), across(far, CORE)


def dot(a, b):
    return jnp.dot(a, b, preferred_element_type=F32)


def tdot(a, b):
    return lax.dot_general(a, b, (((1,), (1,)), ((), ())), preferred_element_type=F32)


def select_kernel(
    where_ref, ids_ref, gates_ref, tok_ref, grad_ref, lat_ref,
    send0, send1, dsend0, dsend1, sel_ref, hi_ref, lo_ref, mine_ref, other_ref,
    pick, weight,
):
    @pl.when(pl.program_id(0) == 0)
    def _():
        p, s = where_ref[0], where_ref[1]
        ids, gates = ids_ref[...], gates_ref[...]
        tok = ids.shape[0]
        row = lax.broadcasted_iota(jnp.int32, (tok, tok), 0)
        lane = lax.broadcasted_iota(jnp.int32, (tok, tok), 1)
        far_core, k = lane >> 6, (lane >> 3) & 1
        ring = (lane >> 4) & 3
        off = ring ^ (ring >> 1)
        off = off ^ (2 * (off & 1) * ((p & 1) ^ far_core))
        base = s ^ ((p & 1) * 8 + ((p >> 1) & 1) * 4 + (p >> 2))
        expert = base ^ (far_core * 8) ^ (k * 4) ^ off
        named = jnp.zeros((tok, tok), F32)
        gate = jnp.zeros((tok, tok), F32)
        for choice in range(ids.shape[1]):
            hit = ids[:, choice : choice + 1] == expert
            named = jnp.where(hit, 1.0, named)
            gate = jnp.where(hit, gates[:, choice : choice + 1], gate)
        earlier = jnp.where(lane < row, 1.0, 0.0).astype(BF)
        before = dot(earlier, named.astype(BF))
        here = jnp.logical_and(named > 0.5, before == (lane & (SLOT - 1)).astype(F32))
        sel = jnp.where(here, 1.0, 0.0)
        mix = jnp.where(here, gate, 0.0)
        sel_ref[...] = sel.astype(BF)
        hi = mix.astype(BF)
        hi_ref[...] = hi
        lo_ref[...] = (mix - hi.astype(F32)).astype(BF)
        pick[...] = sel.T[: 2 * SLOT].astype(BF)
        total = jnp.sum(mix.T[: 2 * SLOT], axis=1, keepdims=True)
        weight[...] = jnp.broadcast_to(total, weight.shape)
        lat = lat_ref[0]
        width = lat.shape[1] // 2
        low = p < 8
        mine_ref[...] = jnp.where(low, lat[:, :width], lat[:, width:])
        other_ref[...] = jnp.where(low, lat[:, width:], lat[:, :width])

    rows = dot(pick[...], tok_ref[...]).astype(BF)
    drows = (dot(pick[...], grad_ref[...]) * weight[:, :1]).astype(BF)
    send0[...] = rows[:SLOT]
    send1[...] = rows[SLOT:]
    dsend0[...] = drows[:SLOT]
    dsend1[...] = drows[SLOT:]


def whole(shape):
    return pl.BlockSpec(shape, lambda i: (0,) * len(shape))


def cost(flops, nbytes):
    return pl.CostEstimate(flops=int(flops), bytes_accessed=int(nbytes), transcendentals=0)


def select(where, ids, gates, tokens, grads, latent):
    tok, d = tokens.shape
    wide = d // STEPS
    width = latent.shape[2] // 2
    col = lambda rows: pl.BlockSpec((rows, wide), lambda i: (0, i))
    chunk = jax.ShapeDtypeStruct((SLOT, d), BF)
    table = jax.ShapeDtypeStruct((tok, tok), BF)
    half = jax.ShapeDtypeStruct((tok, width), BF)
    return pl.pallas_call(
        select_kernel,
        grid=(STEPS,),
        in_specs=[
            pl.BlockSpec(memory_space=pltpu.SMEM),
            whole(ids.shape),
            whole(gates.shape),
            col(tok),
            col(tok),
            whole(latent.shape),
        ],
        out_specs=[col(SLOT)] * 4 + [whole((tok, tok))] * 3 + [whole((tok, width))] * 2,
        out_shape=[chunk] * 4 + [table] * 3 + [half] * 2,
        scratch_shapes=[pltpu.VMEM((2 * SLOT, tok), BF), pltpu.VMEM((2 * SLOT, tok), F32)],
        cost_estimate=cost(4 * 2 * SLOT * tok * d, 4 * tok * d),
        name="select",
    )(where, ids, gates, tokens, grads, latent)


def latent_kernel(tok_ref, mine_ref, got_ref, out_ref):
    both = (mine_ref[...].astype(F32) + got_ref[...].astype(F32)).astype(BF)
    part = lax.dot_general(
        tok_ref[...], both, (((0,), (0,)), ((), ())), preferred_element_type=F32
    )
    out_ref[...] = part.astype(BF)


def latent_part(tokens, mine, got):
    tok, d = tokens.shape
    width = mine.shape[1]
    wide = d // 7
    return pl.pallas_call(
        latent_kernel,
        grid=(7,),
        in_specs=[
            pl.BlockSpec((tok, wide), lambda i: (0, i)),
            whole((tok, width)),
            whole((tok, width)),
        ],
        out_specs=pl.BlockSpec((wide, width), lambda i: (i, 0)),
        out_shape=jax.ShapeDtypeStruct((d, width), BF),
        cost_estimate=cost(2 * tok * d * width, 2 * tok * d + 2 * d * width),
        name="latent_part",
    )(tokens, mine, got)


def forward_kernel(
    rows_ref, wg, wu, wg2, wu2, wd, wd2, kept, sent, fa, fb, acc, hidden
):
    i = pl.program_id(0)
    f = wg.shape[1]

    @pl.when(i == 0)
    def _():
        acc[...] = jnp.zeros_like(acc)

    @pl.when(i < STEPS)
    def _():
        rows = rows_ref[...]
        acc[:, :f] += dot(rows, wg[...])
        acc[:, f : 2 * f] += dot(rows, wg2[...])
        acc[:, 2 * f : 3 * f] += dot(rows, wu[...])
        acc[:, 3 * f :] += dot(rows, wu2[...])

    @pl.when(i == STEPS - 1)
    def _():
        gate, up = acc[:, : 2 * f], acc[:, 2 * f :]
        sg = jax.nn.sigmoid(gate)
        hidden[...] = (gate * sg * up).astype(BF)
        fa[...] = up * sg * (1.0 + gate * (1.0 - sg))
        fb[...] = gate * sg

    @pl.when(i >= STEPS)
    def _():
        out = dot(hidden[:, :f], wd[...]) + dot(hidden[:, f:], wd2[...])
        out = out.astype(BF)
        half = out.shape[0] // 2
        kept[...] = out[:half]
        sent[...] = out[half:]


def forward(rows, wg, wu, wg2, wu2, wd, wd2):
    n, d = rows.shape
    f = wg.shape[1]
    wide = d // STEPS
    early = lambda i: jnp.minimum(i, STEPS - 1)
    late = lambda i: jnp.maximum(i - STEPS, 0)
    weight = pl.BlockSpec((wide, f), lambda i: (early(i), 0))
    down = pl.BlockSpec((f, wide), lambda i: (0, late(i)))
    out = pl.BlockSpec((n // 2, wide), lambda i: (0, late(i)))
    return pl.pallas_call(
        forward_kernel,
        grid=(2 * STEPS,),
        in_specs=[pl.BlockSpec((n, wide), lambda i: (0, early(i)))] + [weight] * 4 + [down] * 2,
        out_specs=[out] * 2 + [whole((n, 2 * f))] * 2,
        out_shape=[jax.ShapeDtypeStruct((n // 2, d), BF)] * 2
        + [jax.ShapeDtypeStruct((n, 2 * f), F32)] * 2,
        scratch_shapes=[pltpu.VMEM((n, 4 * f), F32), pltpu.VMEM((n, 2 * f), BF)],
        cost_estimate=cost(12 * n * d * f, 12 * d * f + 4 * n * d),
        name="forward",
    )(rows, wg, wu, wg2, wu2, wd, wd2)


def backward_kernel(
    rows_ref, fa, fb, wd, wd2, wg, wu, wg2, wu2, kept, sent, acc, gate_grad, up_grad
):
    i = pl.program_id(0)
    f = wg.shape[1]

    @pl.when(i == 0)
    def _():
        acc[...] = jnp.zeros_like(acc)

    @pl.when(i < STEPS)
    def _():
        rows = rows_ref[...]
        acc[:, :f] += tdot(rows, wd[...])
        acc[:, f:] += tdot(rows, wd2[...])

    @pl.when(i == STEPS - 1)
    def _():
        gate_grad[...] = (acc[...] * fa[...]).astype(BF)
        up_grad[...] = (acc[...] * fb[...]).astype(BF)

    @pl.when(i >= STEPS)
    def _():
        out = tdot(gate_grad[:, :f], wg[...]) + tdot(gate_grad[:, f:], wg2[...])
        out = out + tdot(up_grad[:, :f], wu[...]) + tdot(up_grad[:, f:], wu2[...])
        out = out.astype(BF)
        half = out.shape[0] // 2
        kept[...] = out[:half]
        sent[...] = out[half:]


def backward(rows, fa, fb, wd, wd2, wg, wu, wg2, wu2):
    n, d = rows.shape
    f = wg.shape[1]
    wide = d // STEPS
    early = lambda i: jnp.minimum(i, STEPS - 1)
    late = lambda i: jnp.maximum(i - STEPS, 0)
    weight = pl.BlockSpec((wide, f), lambda i: (late(i), 0))
    down = pl.BlockSpec((f, wide), lambda i: (0, early(i)))
    out = pl.BlockSpec((n // 2, wide), lambda i: (0, late(i)))
    return pl.pallas_call(
        backward_kernel,
        grid=(2 * STEPS,),
        in_specs=[pl.BlockSpec((n, wide), lambda i: (0, early(i)))]
        + [whole((n, 2 * f))] * 2
        + [down] * 2
        + [weight] * 4,
        out_specs=[out] * 2,
        out_shape=[jax.ShapeDtypeStruct((n // 2, d), BF)] * 2,
        scratch_shapes=[
            pltpu.VMEM((n, 2 * f), F32),
            pltpu.VMEM((n, 2 * f), BF),
            pltpu.VMEM((n, 2 * f), BF),
        ],
        cost_estimate=cost(12 * n * d * f, 12 * d * f + 4 * n * d),
        name="backward",
    )(rows, fa, fb, wd, wd2, wg, wu, wg2, wu2)


def combine_kernel(n_tables, *refs):
    tables, parts, out = refs[:n_tables], refs[n_tables:-1], refs[-1]
    back = jnp.concatenate([part[...] for part in parts], axis=0)
    total = dot(tables[0][...], back)
    for table in tables[1:]:
        total = total + dot(table[...], back)
    out[...] = total.astype(BF)


def combine(tables, parts):
    tok = tables[0].shape[0]
    d = parts[0].shape[1]
    wide = d // STEPS
    col = lambda rows: pl.BlockSpec((rows, wide), lambda i: (0, i))
    return pl.pallas_call(
        functools.partial(combine_kernel, len(tables)),
        grid=(STEPS,),
        in_specs=[whole((tok, tok))] * len(tables) + [col(part.shape[0]) for part in parts],
        out_specs=col(tok),
        out_shape=jax.ShapeDtypeStruct((tok, d), BF),
        cost_estimate=cost(2 * tok * tok * d * len(tables), 4 * tok * d),
        name="combine",
    )(*tables, *parts)


def per_device(tokens, route_ids, route_gates, w_gate, w_up, w_down, out_grad, latent_grad):
    p = lax.axis_index("pipe")
    s = lax.axis_index("expert")
    where = jnp.stack([p, s]).astype(jnp.int32)
    wg, wu, wd = w_gate[0], w_up[0], w_down[0]
    wg2, wu2, wd2 = across(wg, CORE), across(wu, CORE), across(wd, CORE)
    mirror = [(i, 15 - i) for i in range(16)]

    send0, send1, dsend0, dsend1, sel, hi, lo, mine, other = select(
        where, route_ids, route_gates, tokens, out_grad, latent_grad
    )
    got = lax.ppermute(other, "pipe", mirror)
    part = latent_part(tokens, mine, got)
    share = lax.psum_scatter(part, "expert", scatter_dimension=0, tiled=True)
    theirs = lax.ppermute(share, "pipe", mirror)
    low = p < 8
    kv_grad = jnp.concatenate(
        [jnp.where(low, share, theirs), jnp.where(low, theirs, share)], axis=1
    )[None]

    rows = dispatch(send0, send1)
    drows = dispatch(dsend0, dsend1)
    kept, sent, fa, fb = forward(rows, wg, wu, wg2, wu2, wd, wd2)
    routed = combine([hi, lo], collect(kept, sent))
    dkept, dsent = backward(drows, fa, fb, wd, wd2, wg, wu, wg2, wu2)
    token_grad = combine([sel], collect(dkept, dsent))
    return routed, token_grad, kv_grad


def solution(mesh):
    return jax.shard_map(
        per_device,
        mesh=mesh,
        in_specs=(
            P("expert", None),
            P("expert", None),
            P("expert", None),
            P("expert", None, "pipe"),
            P("expert", None, "pipe"),
            P("expert", "pipe", None),
            P("expert", None),
            P("pipe", "expert", None),
        ),
        out_specs=(P("expert", None), P("expert", None), P("pipe", "expert", None)),
        check_vma=False,
    )
```

time: 195 us -> 176 us (0.903)
  Pallas kernels: 0 us -> 39.2 us
  matrix products: 31.7 us -> 0 us
  waiting for transfers between devices: 60.9 us -> 39.5 us
  local copies, waits for them, and re-layouts: 13.2 us -> 5.12 us
    pallas_call x0 -> x6, Pallas kernels: none -> 39.2 us  [the longest x1 10.1 us: backward(): pl.pallas_call(backward_kernel, grid=(2 * STEPS,), in_specs=[pl.BlockSpec...]
    ppermute x25 -> x9, waiting for transfers between devices: 41.7 us -> 6.02 us  [across(): return lax.ppermute(value, 'pipe', [(i, i ^ mask) for i in range(16)])]
    dot_general x19 -> x0, matrix products: 31.7 us -> none  [the longest x8 11 us: rdot(): return jnp.dot(a, b, preferred_element_type=F32)]
    ppermute x2 -> x14, waiting for transfers between devices: 3.52 us -> 27.2 us  [the longest x12 27 us: along_x(): return lax.ppermute(value, 'pipe', pairs)]
    ppermute x25 -> x9, starting transfers between devices: 34.7 us -> 23.5 us  [across(): return lax.ppermute(value, 'pipe', [(i, i ^ mask) for i in range(16)])]
    ppermute x2 -> x14, starting transfers between devices: 10.6 us -> 21.7 us  [the longest x12 15.9 us: along_x(): return lax.ppermute(value, 'pipe', pairs)]
    ppermute x8, waiting for transfers between devices: 15.6 us -> 6.2 us  [shifted(): return lax.ppermute(value, ('pipe', 'expert'), pairs)]
    unnamed x27 -> x30, local copies, waits for them, and re-layouts: 11 us -> 5.03 us
  transfers between devices with their start and end apart: 36 -> 32, of which waited for: 14 -> 11; matrix products, arithmetic and copies ran while one was open for 22% -> 1% of each run, Pallas kernels for 0% -> 20%
where the time goes in v2:
time: 176 us; the launch traced here: 175 us
  starting transfers between devices  72.8 us (41%)
  waiting for transfers between devices  39.5 us (22%)
  Pallas kernels  39.2 us (22%)
  between operations  14.5 us (8%)
  local copies, waits for them, and re-layouts  5.12 us (3%)
  other arithmetic  3.93 us (2%)
    ppermute x8, starting transfers between devices, shifted(): return lax.ppermute(value, ('pipe', 'expert'), pairs)  27.6 us
    ppermute x12, waiting for transfers between devices, along_x(): return lax.ppermute(value, 'pipe', pairs)  27 us
    ppermute x9, starting transfers between devices, across(): return lax.ppermute(value, 'pipe', [(i, i ^ mask) for i in range(16)])  23.5 us
    ppermute x12, starting transfers between devices, along_x(): return lax.ppermute(value, 'pipe', pairs)  15.9 us
    pallas_call x1, Pallas kernels, backward(): pl.pallas_call(backward_kernel, grid=(2 * STEPS,), in_specs=[pl.BlockSpec...  10.1 us
    pallas_call x1, Pallas kernels, forward(): pl.pallas_call(forward_kernel, grid=(2 * STEPS,), in_specs=[pl.BlockSpec(...  8.89 us
    pallas_call x2, Pallas kernels, combine(): pl.pallas_call(functools.partial(combine_kernel, len(tables)), grid=(STEP...  8.72 us
    pallas_call x1, Pallas kernels, latent_part(): pl.pallas_call(latent_kernel, grid=(7,), in_specs=[pl.BlockSpec((tok, wid...  6.58 us
  transfers between devices with their start and end apart: 32, of which 11 were waited for; matrix products, arithmetic and copies ran while one was open for 1% of the time, Pallas kernels for 20%

profile of v2, /device:TPU:1, one launch (start us, length us, event | category | flops | bytes accessed | tf_op | source)
XLA Modules:
  0.0 174.9 jit_solution(15539028061010486202)
XLA Ops:
  7.2 0.0 reduce-scatter.2.cloned.1.call-start
  7.2 1.4 copy.11.ids_ref
  8.6 1.4 copy.12.gates_ref
  10.0 0.6 pad_add_fusion.where_ref
  10.6 4.9 %select.1 = (bf16[8,7168]{1,0:T(8,128)(2,1)}, bf16[8,7168]{1,0:T(8,128)(2,1)}, bf16[8,7168]{1,0:T(8,128)(2,1)}, bf16[8,7168]{1,0:T(8,128)(2,1)}, bf16[128,128]{1...) custom-call(s32[2]{0:T(128)} %pad_add_fusion.where_ref, ...), custom_call_target="tpu_custom_call" | custom-call | flops 58720256 | bytes 3670016 | tf_op jit(solution)/shard_map/select/pallas_call | solution.py:134
  15.5 4.0 %collective-permute-start = (bf16[8,7168]{1,0:T(8,128)(2,1)}, bf16[8,7168]{1,0:T(8,128)(2,1)S(1)}, u32[]{:S(2)}, u32[]{:S(2)}) collective-permute-start(bf16[8,7168]{1,0:T(8,128)(2,1)} %get-tuple-element.20), channel_id=1, source_target_pairs={{0,0},{1,1},{2,2},{3,3},{4,4},{5,5},{6,6},{7,7},{8,8},{9,9},{10,10... | collective-permute-start | bytes 344072 | tf_op jit(solution)/shard_map/ppermute | solution.py:28
  19.6 8.7 %collective-permute-start.1 = (bf16[8,7168]{1,0:T(8,128)(2,1)}, bf16[8,7168]{1,0:T(8,128)(2,1)S(1)}, u32[]{:S(2)}, u32[]{:S(2)}) collective-permute-start(bf16[8,7168]{1,0:T(8,128)(2,1)} %get-tuple-element.21), channel_id=1, source_target_pairs={{0,4},{1,5},{2,6},{3,7},{4,0},{5,1},{6,2},{7,3},{8,12},{9,13},{10,... | collective-permute-start | bytes 344072 | tf_op jit(solution)/shard_map/ppermute | solution.py:28
  28.3 5.4 %collective-permute-start.29 = (bf16[128,256]{1,0:T(8,128)(2,1)}, bf16[128,256]{1,0:T(8,128)(2,1)S(1)}, u32[]{:S(2)}, u32[]{:S(2)}) collective-permute-start(bf16[128,256]{1,0:T(8,128)(2,1)} %get-tuple-element.32), channel_id=1, source_target_pairs={{0,240},{16,224},{32,208},{48,192},{64,176},{80,160},{96,144},{112... | collective-permute-start | bytes 196616 | tf_op jit(solution)/shard_map/ppermute | solution.py:332
  33.7 2.3 %collective-permute-start.16 = (bf16[8,7168]{1,0:T(8,128)(2,1)}, bf16[8,7168]{1,0:T(8,128)(2,1)S(1)}, u32[]{:S(2)}, u32[]{:S(2)}) collective-permute-start(bf16[8,7168]{1,0:T(8,128)(2,1)} %get-tuple-element.25), channel_id=1, source_target_pairs={{0,0},{1,1},{2,2},{3,3},{4,4},{5,5},{6,6},{7,7},{8,8},{9,9},{10,10... | collective-permute-start | bytes 344072 | tf_op jit(solution)/shard_map/ppermute | solution.py:28
  36.0 3.8 %collective-permute-start.17 = (bf16[8,7168]{1,0:T(8,128)(2,1)}, bf16[8,7168]{1,0:T(8,128)(2,1)S(1)}, u32[]{:S(2)}, u32[]{:S(2)}) collective-permute-start(bf16[8,7168]{1,0:T(8,128)(2,1)} %get-tuple-element.26), channel_id=1, source_target_pairs={{0,4},{1,5},{2,6},{3,7},{4,0},{5,1},{6,2},{7,3},{8,12},{9,13},{10,... | collective-permute-start | bytes 344072 | tf_op jit(solution)/shard_map/ppermute | solution.py:28
  39.8 0.1 collective-permute-start.4
  39.9 0.5 copy-done.11
  40.4 6.6 %latent_part.1 = bf16[7168,256]{1,0:T(8,128)(2,1)} custom-call(bf16[128,7168]{1,0:T(8,128)(2,1)} %tok_ref.3, bf16[128,256]{1,0:T(8,128)(2,1)} %get-tuple-element.31.mine_ref, bf16[128,256]{1,0:T(8,128)(2,1)} %copy-done.11), custom_call_target="tpu_custom_call" | custom-call | flops 469762048 | bytes 5505024 | tf_op jit(solution)/shard_map/latent_part/pallas_call | solution.py:165
  47.0 0.0 reduce-scatter.2.cloned.1.call-update
  47.1 0.1 collective-permute-start.5
  47.2 0.5 collective-permute-start.6
  47.7 0.1 collective-permute-start.2
  47.8 2.7 %collective-permute-start.18 = (bf16[16,7168]{1,0:T(8,128)(2,1)S(1)}, bf16[16,7168]{1,0:T(8,128)(2,1)S(1)}, u32[]{:S(2)}, u32[]{:S(2)}) collective-permute-start(bf16[16,7168]{1,0:T(8,128)(2,1)S(1)} %pad_maximum_fusion.6), channel_id=1, source_target_pairs={{0,64},{16,208},{32,96},{48,240},{64,0},{80,144},{96,32},{112,176}... | collective-permute-start | bytes 688136 | tf_op jit(solution)/shard_map/ppermute | solution.py:36
  50.6 3.3 %collective-permute-done.2 = bf16[16,7168]{1,0:T(8,128)(2,1)S(1)} collective-permute-done((bf16[16,7168]{1,0:T(8,128)(2,1)S(1)}, bf16[16,7168]{1,0:T(8,128)(2,1)S(1)}, u32[]{:S(2)}, u32[]{:S(2)}) %collective-permute-start.2) | collective-permute-done | bytes 229408 | tf_op jit(solution)/shard_map/ppermute | solution.py:36
  53.9 0.1 collective-permute-start.3
  54.0 2.3 %collective-permute-done.18 = bf16[16,7168]{1,0:T(8,128)(2,1)S(1)} collective-permute-done((bf16[16,7168]{1,0:T(8,128)(2,1)S(1)}, bf16[16,7168]{1,0:T(8,128)(2,1)S(1)}, u32[]{:S(2)}, u32[]{:S(2)}) %collective-permute-start.18) | collective-permute-done | bytes 229408 | tf_op jit(solution)/shard_map/ppermute | solution.py:36
  56.3 0.1 collective-permute-start.19
  56.4 5.3 %collective-permute-done.3 = bf16[32,7168]{1,0:T(8,128)(2,1)S(1)} collective-permute-done((bf16[32,7168]{1,0:T(8,128)(2,1)S(1)}, bf16[32,7168]{1,0:T(8,128)(2,1)S(1)}, u32[]{:S(2)}, u32[]{:S(2)}) %collective-permute-start.3) | collective-permute-done | bytes 458784 | tf_op jit(solution)/shard_map/ppermute | solution.py:36
  61.7 1.0 pad_maximum_fusion.rows_ref
  62.7 8.9 %forward.1 = (bf16[32,7168]{1,0:T(8,128)(2,1)}, bf16[32,7168]{1,0:T(8,128)(2,1)}, f32[64,256]{1,0:T(8,128)}, f32[64,256]{1,0:T(8,128)}) custom-call(bf16[64,7168]{1,0:T(8,128)(2,1)} %pad_maximum_fusion.rows_ref, bf16[7168,128]{1,0:T(8,128)(2,1)} %bitcast.7, bf16[7168,128]{1,0:T(8,128)(2,1)} %bitcast.11, bf16[7168,128]{1,0:T(8,128)(2,1)} %collective-permute-done.4.wg2, ...), custom_call_target="tpu_custom_call" | custom-call | flops 704643072 | bytes 12845056 | tf_op jit(solution)/shard_map/forward/pallas_call | solution.py:224
  71.6 0.1 collective-permute-start.7
  71.7 1.0 pad_maximum_fusion.1.rows_ref
  72.7 10.1 %backward.1 = (bf16[32,7168]{1,0:T(8,128)(2,1)}, bf16[32,7168]{1,0:T(8,128)(2,1)}) custom-call(bf16[64,7168]{1,0:T(8,128)(2,1)} %pad_maximum_fusion.1.rows_ref, f32[64,256]{1,0:T(8,128)} %get-tuple-element.27.fa, f32[64,256]{1,0:T(8,128)} %get-tuple-element.28.fb, bf16[128,7168]{1,0:T(8,128)(2,1)} %bitcast.15, bf16[128,7168]{1,0:T(8,128)(2,1)} %collective-permute-done.6.wd2, ...), custom_call_target="tpu_custom_call" | custom-call | flops 704643072 | bytes 12845056 | tf_op jit(solution)/shard_map/backward/pallas_call | solution.py:277
  82.7 1.5 collective-permute-start.20
  84.3 0.1 add_convert_fusion.1
  84.4 0.1 collective-permute-start.8
  84.5 6.4 %collective-permute-done.20 = bf16[32,7168]{1,0:T(8,128)(2,1)S(1)} collective-permute-done((bf16[32,7168]{1,0:T(8,128)(2,1)}, bf16[32,7168]{1,0:T(8,128)(2,1)S(1)}, u32[]{:S(2)}, u32[]{:S(2)}) %collective-permute-start.20) | collective-permute-done | bytes 458784 | tf_op jit(solution)/shard_map/ppermute | solution.py:36
  90.9 0.1 add_convert_fusion
  91.1 0.2 collective-permute-start.21
  91.2 1.0 collective-permute-done.8
  92.2 0.1 add_convert_fusion.3
  92.3 0.7 collective-permute-start.9
  93.0 5.4 %collective-permute-done.21 = bf16[16,7168]{1,0:T(8,128)(2,1)S(1)} collective-permute-done((bf16[16,7168]{1,0:T(8,128)(2,1)S(1)}, bf16[16,7168]{1,0:T(8,128)(2,1)S(1)}, u32[]{:S(2)}, u32[]{:S(2)}) %collective-permute-start.21) | collective-permute-done | bytes 229408 | tf_op jit(solution)/shard_map/ppermute | solution.py:36
  98.4 0.1 add_convert_fusion.2
  98.5 0.7 collective-permute-start.22
  99.2 2.3 %collective-permute-done.9 = bf16[8,7168]{1,0:T(8,128)(2,1)S(1)} collective-permute-done((bf16[8,7168]{1,0:T(8,128)(2,1)S(1)}, bf16[8,7168]{1,0:T(8,128)(2,1)S(1)}, u32[]{:S(2)}, u32[]{:S(2)}) %collective-permute-start.9) | collective-permute-done | bytes 114720 | tf_op jit(solution)/shard_map/ppermute | solution.py:17
  101.5 0.5 collective-permute-start.11
  102.0 1.9 %collective-permute-start.10 = (bf16[8,7168]{1,0:T(8,128)(2,1)S(1)}, bf16[8,7168]{1,0:T(8,128)(2,1)S(1)}, u32[]{:S(2)}, u32[]{:S(2)}) collective-permute-start(bf16[8,7168]{1,0:T(8,128)(2,1)S(1)} %add_convert_fusion.5), channel_id=1, source_target_pairs={{0,0},{1,1},{2,2},{3,3},{4,4},{5,5},{6,6},{7,7},{8,8},{9,9},{10,10... | collective-permute-start | bytes 344072 | tf_op jit(solution)/shard_map/ppermute | solution.py:28
  103.9 3.7 %collective-permute-done.22 = bf16[8,7168]{1,0:T(8,128)(2,1)S(1)} collective-permute-done((bf16[8,7168]{1,0:T(8,128)(2,1)S(1)}, bf16[8,7168]{1,0:T(8,128)(2,1)S(1)}, u32[]{:S(2)}, u32[]{:S(2)}) %collective-permute-start.22) | collective-permute-done | bytes 114720 | tf_op jit(solution)/shard_map/ppermute | solution.py:17
  107.6 3.6 %collective-permute-start.24 = (bf16[8,7168]{1,0:T(8,128)(2,1)S(1)}, bf16[8,7168]{1,0:T(8,128)(2,1)S(1)}, u32[]{:S(2)}, u32[]{:S(2)}) collective-permute-start(bf16[8,7168]{1,0:T(8,128)(2,1)S(1)} %add_convert_fusion.4), channel_id=1, source_target_pairs={{0,32},{1,33},{2,34},{3,35},{4,36},{5,37},{6,38},{7,39},{8,40},{9,... | collective-permute-start | bytes 344072 | tf_op jit(solution)/shard_map/ppermute | solution.py:28
  111.2 2.8 %collective-permute-start.23 = (bf16[8,7168]{1,0:T(8,128)(2,1)S(1)}, bf16[8,7168]{1,0:T(8,128)(2,1)S(1)}, u32[]{:S(2)}, u32[]{:S(2)}) collective-permute-start(bf16[8,7168]{1,0:T(8,128)(2,1)S(1)} %add_convert_fusion.4), channel_id=1, source_target_pairs={{0,0},{1,1},{2,2},{3,3},{4,4},{5,5},{6,6},{7,7},{8,8},{9,9},{10,10... | collective-permute-start | bytes 344072 | tf_op jit(solution)/shard_map/ppermute | solution.py:28
  114.1 3.1 %collective-permute-start.12 = (bf16[16,7168]{1,0:T(8,128)(2,1)S(1)}, bf16[16,7168]{1,0:T(8,128)(2,1)S(1)}, u32[]{:S(2)}, u32[]{:S(2)}) collective-permute-start(bf16[16,7168]{1,0:T(8,128)(2,1)S(1)} %pad_maximum_fusion.5), channel_id=1, source_target_pairs={{0,64},{16,208},{32,96},{48,240},{64,0},{80,144},{96,32},{112,176}... | collective-permute-start | bytes 688136 | tf_op jit(solution)/shard_map/ppermute | solution.py:36
  117.2 6.2 %collective-permute-done.24 = bf16[8,7168]{1,0:T(8,128)(2,1)S(1)} collective-permute-done((bf16[8,7168]{1,0:T(8,128)(2,1)S(1)}, bf16[8,7168]{1,0:T(8,128)(2,1)S(1)}, u32[]{:S(2)}, u32[]{:S(2)}) %collective-permute-start.24) | collective-permute-done | bytes 114720 | tf_op jit(solution)/shard_map/ppermute | solution.py:28
  123.4 6.3 %collective-permute-start.25 = (bf16[16,7168]{1,0:T(8,128)(2,1)S(1)}, bf16[16,7168]{1,0:T(8,128)(2,1)S(1)}, u32[]{:S(2)}, u32[]{:S(2)}) collective-permute-start(bf16[16,7168]{1,0:T(8,128)(2,1)S(1)} %pad_maximum_fusion.7), channel_id=1, source_target_pairs={{0,64},{16,208},{32,96},{48,240},{64,0},{80,144},{96,32},{112,176}... | collective-permute-start | bytes 688136 | tf_op jit(solution)/shard_map/ppermute | solution.py:36
  129.7 3.3 %collective-permute-done.25 = bf16[16,7168]{1,0:T(8,128)(2,1)S(1)} collective-permute-done((bf16[16,7168]{1,0:T(8,128)(2,1)S(1)}, bf16[16,7168]{1,0:T(8,128)(2,1)S(1)}, u32[]{:S(2)}, u32[]{:S(2)}) %collective-permute-start.25) | collective-permute-done | bytes 229408 | tf_op jit(solution)/shard_map/ppermute | solution.py:36
  133.1 0.0 copy-start.1
  133.1 0.1 collective-permute-start.26
  133.2 1.5 collective-permute-start.13
  134.8 10.1 %collective-permute-start.27 = (bf16[32,7168]{1,0:T(8,128)(2,1)S(1)}, bf16[32,7168]{1,0:T(8,128)(2,1)S(1)}, u32[]{:S(2)}, u32[]{:S(2)}) collective-permute-start(bf16[32,7168]{1,0:T(8,128)(2,1)S(1)} %constant_dynamic-update-slice_fusion.3.refs_1_), channel_id=1, source_target_pairs={{0,16},{16,0},{32,48},{48,32},{64,80},{80,64},{96,112},{112,96},{1... | collective-permute-start | bytes 1376264 | tf_op jit(solution)/shard_map/ppermute | solution.py:17
  144.8 6.3 %collective-permute-start.28 = (bf16[32,7168]{1,0:T(8,128)(2,1)S(1)}, bf16[32,7168]{1,0:T(8,128)(2,1)}, u32[]{:S(2)}, u32[]{:S(2)}) collective-permute-start(bf16[32,7168]{1,0:T(8,128)(2,1)S(1)} %collective-permute-done.26.refs_2_), channel_id=1, source_target_pairs={{0,16},{16,0},{32,48},{48,32},{64,80},{80,64},{96,112},{112,96},{1... | collective-permute-start | bytes 1376264 | tf_op jit(solution)/shard_map/ppermute | solution.py:17
  151.2 4.9 %collective-permute-start.15 = (bf16[32,7168]{1,0:T(8,128)(2,1)S(1)}, bf16[32,7168]{1,0:T(8,128)(2,1)S(1)}, u32[]{:S(2)}, u32[]{:S(2)}) collective-permute-start(bf16[32,7168]{1,0:T(8,128)(2,1)S(1)} %collective-permute-done.13.refs_3_), channel_id=1, source_target_pairs={{0,16},{16,0},{32,48},{48,32},{64,80},{80,64},{96,112},{112,96},{1... | collective-permute-start | bytes 1376264 | tf_op jit(solution)/shard_map/ppermute | solution.py:17
  156.1 0.4 collective-permute-start.30
  156.5 0.7 copy-done.6
  157.2 4.2 %combine.3 = bf16[128,7168]{1,0:T(8,128)(2,1)} custom-call(bf16[128,128]{1,0:T(8,128)(2,1)} %get-tuple-element.24.refs_0_, bf16[32,7168]{1,0:T(8,128)(2,1)} %copy-done.1, bf16[32,7168]{1,0:T(8,128)(2,1)} %copy-done.4, bf16[32,7168]{1,0:T(8,128)(2,1)} %copy-done.6, bf16[32,7168]{1,0:T(8,128)(2,1)} %collective-permute-done.28.refs_4_), custom_call_target="tpu_custom_call" | custom-call | flops 234881024 | bytes 3670016 | tf_op jit(solution)/shard_map/combine/pallas_call | solution.py:310
  161.5 0.7 copy-done.5
  162.3 0.2 copy-done.7
  162.4 4.5 %combine.2 = bf16[128,7168]{1,0:T(8,128)(2,1)} custom-call(bf16[128,128]{1,0:T(8,128)(2,1)} %get-tuple-element.18.refs_0_, bf16[128,128]{1,0:T(8,128)(2,1)} %get-tuple-element.19.refs_1_, bf16[32,7168]{1,0:T(8,128)(2,1)} %copy-done.2, bf16[32,7168]{1,0:T(8,128)(2,1)} %copy-done.3, bf16[32,7168]{1,0:T(8,128)(2,1)} %copy-done.5, bf16[32,7168]{1,0:T(8,128)(2,1)} %copy-done.7), custom_call_target="tpu_custom_call" | custom-call | flops 469762048 | bytes 3670016 | tf_op jit(solution)/shard_map/combine/pallas_call | solution.py:310
  166.9 0.3 collective-permute-done.30
  167.3 0.8 maximum_bitcast_fusion
  (60 shorter events, 0.4 us)
Async XLA Ops:
  7.2 148.9 %reduce-scatter.2.cloned.1.call-start = ((), (), s32[]{:S(2)}) async-start(), calls=%async_computation.1 | async-start | bytes 3899392 | tf_op jit(solution)/shard_map/reduce_scatter | solution.py:334
  10.6 29.2 %copy-start = (bf16[1,7168,128]{2,1,0:T(8,128)(2,1)S(1)}, bf16[1,7168,128]{2,1,0:T(8,128)(2,1)}, u32[]{:S(2)}) copy-start(bf16[1,7168,128]{2,1,0:T(8,128)(2,1)} %param.11) | copy-start | bytes 5505028
  15.5 31.5 %collective-permute-start = (bf16[8,7168]{1,0:T(8,128)(2,1)}, bf16[8,7168]{1,0:T(8,128)(2,1)S(1)}, u32[]{:S(2)}, u32[]{:S(2)}) collective-permute-start(bf16[8,7168]{1,0:T(8,128)(2,1)} %get-tuple-element.20), channel_id=1, source_target_pairs={{0,0},{1,1},{2,2},{3,3},{4,4},{5,5},{6,6},{7,7},{8,8},{9,9},{10,10... | collective-permute-start | bytes 344072 | tf_op jit(solution)/shard_map/ppermute | solution.py:28
  19.6 27.6 %collective-permute-start.1 = (bf16[8,7168]{1,0:T(8,128)(2,1)}, bf16[8,7168]{1,0:T(8,128)(2,1)S(1)}, u32[]{:S(2)}, u32[]{:S(2)}) collective-permute-start(bf16[8,7168]{1,0:T(8,128)(2,1)} %get-tuple-element.21), channel_id=1, source_target_pairs={{0,4},{1,5},{2,6},{3,7},{4,0},{5,1},{6,2},{7,3},{8,12},{9,13},{10,... | collective-permute-start | bytes 344072 | tf_op jit(solution)/shard_map/ppermute | solution.py:28
  28.3 11.5 %collective-permute-start.29 = (bf16[128,256]{1,0:T(8,128)(2,1)}, bf16[128,256]{1,0:T(8,128)(2,1)S(1)}, u32[]{:S(2)}, u32[]{:S(2)}) collective-permute-start(bf16[128,256]{1,0:T(8,128)(2,1)} %get-tuple-element.32), channel_id=1, source_target_pairs={{0,240},{16,224},{32,208},{48,192},{64,176},{80,160},{96,144},{112... | collective-permute-start | bytes 196616 | tf_op jit(solution)/shard_map/ppermute | solution.py:332
  33.7 14.0 %collective-permute-start.16 = (bf16[8,7168]{1,0:T(8,128)(2,1)}, bf16[8,7168]{1,0:T(8,128)(2,1)S(1)}, u32[]{:S(2)}, u32[]{:S(2)}) collective-permute-start(bf16[8,7168]{1,0:T(8,128)(2,1)} %get-tuple-element.25), channel_id=1, source_target_pairs={{0,0},{1,1},{2,2},{3,3},{4,4},{5,5},{6,6},{7,7},{8,8},{9,9},{10,10... | collective-permute-start | bytes 344072 | tf_op jit(solution)/shard_map/ppermute | solution.py:28
  36.0 11.8 %collective-permute-start.17 = (bf16[8,7168]{1,0:T(8,128)(2,1)}, bf16[8,7168]{1,0:T(8,128)(2,1)S(1)}, u32[]{:S(2)}, u32[]{:S(2)}) collective-permute-start(bf16[8,7168]{1,0:T(8,128)(2,1)} %get-tuple-element.26), channel_id=1, source_target_pairs={{0,4},{1,5},{2,6},{3,7},{4,0},{5,1},{6,2},{7,3},{8,12},{9,13},{10,... | collective-permute-start | bytes 344072 | tf_op jit(solution)/shard_map/ppermute | solution.py:28
  39.8 0.6 copy-start.11
  39.8 22.9 %collective-permute-start.4 = (bf16[7168,128]{1,0:T(8,128)(2,1)S(1)}, bf16[7168,128]{1,0:T(8,128)(2,1)}, u32[]{:S(2)}, u32[]{:S(2)}) collective-permute-start(bf16[7168,128]{1,0:T(8,128)(2,1)S(1)} %bitcast.9), channel_id=1, source_target_pairs={{0,16},{16,0},{32,48},{48,32},{64,80},{80,64},{96,112},{112,96},{1... | collective-permute-start | bytes 5505032 | tf_op jit(solution)/shard_map/ppermute | solution.py:17
  47.1 15.6 %collective-permute-start.5 = (bf16[7168,128]{1,0:T(8,128)(2,1)}, bf16[7168,128]{1,0:T(8,128)(2,1)}, u32[]{:S(2)}, u32[]{:S(2)}) collective-permute-start(bf16[7168,128]{1,0:T(8,128)(2,1)} %bitcast.10), channel_id=1, source_target_pairs={{0,16},{16,0},{32,48},{48,32},{64,80},{80,64},{96,112},{112,96},{1... | collective-permute-start | bytes 5505032 | tf_op jit(solution)/shard_map/ppermute | solution.py:17
  47.2 15.5 %collective-permute-start.6 = (bf16[128,7168]{1,0:T(8,128)(2,1)}, bf16[128,7168]{1,0:T(8,128)(2,1)}, u32[]{:S(2)}, u32[]{:S(2)}) collective-permute-start(bf16[128,7168]{1,0:T(8,128)(2,1)} %bitcast.13), channel_id=1, source_target_pairs={{0,16},{16,0},{32,48},{48,32},{64,80},{80,64},{96,112},{112,96},{1... | collective-permute-start | bytes 5505032 | tf_op jit(solution)/shard_map/ppermute | solution.py:17
  47.7 6.2 %collective-permute-start.2 = (bf16[16,7168]{1,0:T(8,128)(2,1)S(1)}, bf16[16,7168]{1,0:T(8,128)(2,1)S(1)}, u32[]{:S(2)}, u32[]{:S(2)}) collective-permute-start(bf16[16,7168]{1,0:T(8,128)(2,1)S(1)} %pad_maximum_fusion.4), channel_id=1, source_target_pairs={{0,64},{16,208},{32,96},{48,240},{64,0},{80,144},{96,32},{112,176}... | collective-permute-start | bytes 688136 | tf_op jit(solution)/shard_map/ppermute | solution.py:36
  47.8 8.5 %collective-permute-start.18 = (bf16[16,7168]{1,0:T(8,128)(2,1)S(1)}, bf16[16,7168]{1,0:T(8,128)(2,1)S(1)}, u32[]{:S(2)}, u32[]{:S(2)}) collective-permute-start(bf16[16,7168]{1,0:T(8,128)(2,1)S(1)} %pad_maximum_fusion.6), channel_id=1, source_target_pairs={{0,64},{16,208},{32,96},{48,240},{64,0},{80,144},{96,32},{112,176}... | collective-permute-start | bytes 688136 | tf_op jit(solution)/shard_map/ppermute | solution.py:36
  53.9 7.8 %collective-permute-start.3 = (bf16[32,7168]{1,0:T(8,128)(2,1)S(1)}, bf16[32,7168]{1,0:T(8,128)(2,1)S(1)}, u32[]{:S(2)}, u32[]{:S(2)}) collective-permute-start(bf16[32,7168]{1,0:T(8,128)(2,1)S(1)} %pad_maximum_fusion.2), channel_id=1, source_target_pairs={{0,192},{16,80},{32,224},{48,112},{64,128},{80,16},{96,160},{112,4... | collective-permute-start | bytes 1376264 | tf_op jit(solution)/shard_map/ppermute | solution.py:36
  56.3 15.3 %collective-permute-start.19 = (bf16[32,7168]{1,0:T(8,128)(2,1)S(1)}, bf16[32,7168]{1,0:T(8,128)(2,1)S(1)}, u32[]{:S(2)}, u32[]{:S(2)}) collective-permute-start(bf16[32,7168]{1,0:T(8,128)(2,1)S(1)} %pad_maximum_fusion.3), channel_id=1, source_target_pairs={{0,192},{16,80},{32,224},{48,112},{64,128},{80,16},{96,160},{112,4... | collective-permute-start | bytes 1376264 | tf_op jit(solution)/shard_map/ppermute | solution.py:36
  71.6 12.7 %collective-permute-start.7 = (bf16[32,7168]{1,0:T(8,128)(2,1)}, bf16[32,7168]{1,0:T(8,128)(2,1)S(1)}, u32[]{:S(2)}, u32[]{:S(2)}) collective-permute-start(bf16[32,7168]{1,0:T(8,128)(2,1)} %get-tuple-element.23), channel_id=1, source_target_pairs={{0,192},{16,80},{32,224},{48,112},{64,128},{80,16},{96,160},{112,4... | collective-permute-start | bytes 1376264 | tf_op jit(solution)/shard_map/ppermute | solution.py:36
  72.7 11.6 %copy-start.8 = (bf16[32,7168]{1,0:T(8,128)(2,1)S(1)}, bf16[32,7168]{1,0:T(8,128)(2,1)}, u32[]{:S(2)}) copy-start(bf16[32,7168]{1,0:T(8,128)(2,1)} %get-tuple-element.22) | copy-start | bytes 1376260
  82.7 8.2 %copy-start.9 = (bf16[32,7168]{1,0:T(8,128)(2,1)S(1)}, bf16[32,7168]{1,0:T(8,128)(2,1)}, u32[]{:S(2)}) copy-start(bf16[32,7168]{1,0:T(8,128)(2,1)} %get-tuple-element.29) | copy-start | bytes 1376260
  82.7 8.2 %collective-permute-start.20 = (bf16[32,7168]{1,0:T(8,128)(2,1)}, bf16[32,7168]{1,0:T(8,128)(2,1)S(1)}, u32[]{:S(2)}, u32[]{:S(2)}) collective-permute-start(bf16[32,7168]{1,0:T(8,128)(2,1)} %get-tuple-element.30), channel_id=1, source_target_pairs={{0,192},{16,80},{32,224},{48,112},{64,128},{80,16},{96,160},{112,4... | collective-permute-start | bytes 1376264 | tf_op jit(solution)/shard_map/ppermute | solution.py:36
  84.4 7.8 %collective-permute-start.8 = (bf16[16,7168]{1,0:T(8,128)(2,1)S(1)}, bf16[16,7168]{1,0:T(8,128)(2,1)S(1)}, u32[]{:S(2)}, u32[]{:S(2)}) collective-permute-start(bf16[16,7168]{1,0:T(8,128)(2,1)S(1)} %slice.33), channel_id=1, source_target_pairs={{0,64},{16,208},{32,96},{48,240},{64,0},{80,144},{96,32},{112,176}... | collective-permute-start | bytes 688136 | tf_op jit(solution)/shard_map/ppermute | solution.py:36
  91.1 7.3 %collective-permute-start.21 = (bf16[16,7168]{1,0:T(8,128)(2,1)S(1)}, bf16[16,7168]{1,0:T(8,128)(2,1)S(1)}, u32[]{:S(2)}, u32[]{:S(2)}) collective-permute-start(bf16[16,7168]{1,0:T(8,128)(2,1)S(1)} %slice.37), channel_id=1, source_target_pairs={{0,64},{16,208},{32,96},{48,240},{64,0},{80,144},{96,32},{112,176}... | collective-permute-start | bytes 688136 | tf_op jit(solution)/shard_map/ppermute | solution.py:36
  92.3 9.2 %collective-permute-start.9 = (bf16[8,7168]{1,0:T(8,128)(2,1)S(1)}, bf16[8,7168]{1,0:T(8,128)(2,1)S(1)}, u32[]{:S(2)}, u32[]{:S(2)}) collective-permute-start(bf16[8,7168]{1,0:T(8,128)(2,1)S(1)} %slice.35), channel_id=1, source_target_pairs={{0,32},{16,48},{32,0},{48,16},{64,96},{80,112},{96,64},{112,80},{1... | collective-permute-start | bytes 344072 | tf_op jit(solution)/shard_map/ppermute | solution.py:17
  98.5 9.2 %collective-permute-start.22 = (bf16[8,7168]{1,0:T(8,128)(2,1)S(1)}, bf16[8,7168]{1,0:T(8,128)(2,1)S(1)}, u32[]{:S(2)}, u32[]{:S(2)}) collective-permute-start(bf16[8,7168]{1,0:T(8,128)(2,1)S(1)} %slice.39), channel_id=1, source_target_pairs={{0,32},{16,48},{32,0},{48,16},{64,96},{80,112},{96,64},{112,80},{1... | collective-permute-start | bytes 344072 | tf_op jit(solution)/shard_map/ppermute | solution.py:17
  101.5 12.5 %collective-permute-start.11 = (bf16[8,7168]{1,0:T(8,128)(2,1)S(1)}, bf16[8,7168]{1,0:T(8,128)(2,1)S(1)}, u32[]{:S(2)}, u32[]{:S(2)}) collective-permute-start(bf16[8,7168]{1,0:T(8,128)(2,1)S(1)} %add_convert_fusion.5), channel_id=1, source_target_pairs={{0,32},{1,33},{2,34},{3,35},{4,36},{5,37},{6,38},{7,39},{8,40},{9,... | collective-permute-start | bytes 344072 | tf_op jit(solution)/shard_map/ppermute | solution.py:28
  102.0 12.1 %collective-permute-start.10 = (bf16[8,7168]{1,0:T(8,128)(2,1)S(1)}, bf16[8,7168]{1,0:T(8,128)(2,1)S(1)}, u32[]{:S(2)}, u32[]{:S(2)}) collective-permute-start(bf16[8,7168]{1,0:T(8,128)(2,1)S(1)} %add_convert_fusion.5), channel_id=1, source_target_pairs={{0,0},{1,1},{2,2},{3,3},{4,4},{5,5},{6,6},{7,7},{8,8},{9,9},{10,10... | collective-permute-start | bytes 344072 | tf_op jit(solution)/shard_map/ppermute | solution.py:28
  107.6 15.7 %collective-permute-start.24 = (bf16[8,7168]{1,0:T(8,128)(2,1)S(1)}, bf16[8,7168]{1,0:T(8,128)(2,1)S(1)}, u32[]{:S(2)}, u32[]{:S(2)}) collective-permute-start(bf16[8,7168]{1,0:T(8,128)(2,1)S(1)} %add_convert_fusion.4), channel_id=1, source_target_pairs={{0,32},{1,33},{2,34},{3,35},{4,36},{5,37},{6,38},{7,39},{8,40},{9,... | collective-permute-start | bytes 344072 | tf_op jit(solution)/shard_map/ppermute | solution.py:28
  111.2 12.1 %collective-permute-start.23 = (bf16[8,7168]{1,0:T(8,128)(2,1)S(1)}, bf16[8,7168]{1,0:T(8,128)(2,1)S(1)}, u32[]{:S(2)}, u32[]{:S(2)}) collective-permute-start(bf16[8,7168]{1,0:T(8,128)(2,1)S(1)} %add_convert_fusion.4), channel_id=1, source_target_pairs={{0,0},{1,1},{2,2},{3,3},{4,4},{5,5},{6,6},{7,7},{8,8},{9,9},{10,10... | collective-permute-start | bytes 344072 | tf_op jit(solution)/shard_map/ppermute | solution.py:28
  114.1 19.1 %collective-permute-start.12 = (bf16[16,7168]{1,0:T(8,128)(2,1)S(1)}, bf16[16,7168]{1,0:T(8,128)(2,1)S(1)}, u32[]{:S(2)}, u32[]{:S(2)}) collective-permute-start(bf16[16,7168]{1,0:T(8,128)(2,1)S(1)} %pad_maximum_fusion.5), channel_id=1, source_target_pairs={{0,64},{16,208},{32,96},{48,240},{64,0},{80,144},{96,32},{112,176}... | collective-permute-start | bytes 688136 | tf_op jit(solution)/shard_map/ppermute | solution.py:36
  123.4 9.7 %collective-permute-start.25 = (bf16[16,7168]{1,0:T(8,128)(2,1)S(1)}, bf16[16,7168]{1,0:T(8,128)(2,1)S(1)}, u32[]{:S(2)}, u32[]{:S(2)}) collective-permute-start(bf16[16,7168]{1,0:T(8,128)(2,1)S(1)} %pad_maximum_fusion.7), channel_id=1, source_target_pairs={{0,64},{16,208},{32,96},{48,240},{64,0},{80,144},{96,32},{112,176}... | collective-permute-start | bytes 688136 | tf_op jit(solution)/shard_map/ppermute | solution.py:36
  133.1 23.4 %copy-start.1 = (bf16[32,7168]{1,0:T(8,128)(2,1)}, bf16[32,7168]{1,0:T(8,128)(2,1)S(1)}, u32[]{:S(2)}) copy-start(bf16[32,7168]{1,0:T(8,128)(2,1)S(1)} %constant_dynamic-update-slice_fusion.3.refs_1_) | copy-start | bytes 1376260
  133.1 11.7 %collective-permute-start.26 = (bf16[32,7168]{1,0:T(8,128)(2,1)S(1)}, bf16[32,7168]{1,0:T(8,128)(2,1)S(1)}, u32[]{:S(2)}, u32[]{:S(2)}) collective-permute-start(bf16[32,7168]{1,0:T(8,128)(2,1)S(1)} %constant_dynamic-update-slice_fusion.3.refs_1_), channel_id=1, source_target_pairs={{0,192},{16,80},{32,224},{48,112},{64,128},{80,16},{96,160},{112,4... | collective-permute-start | bytes 1376264 | tf_op jit(solution)/shard_map/ppermute | solution.py:36
  133.2 28.2 %copy-start.2 = (bf16[32,7168]{1,0:T(8,128)(2,1)}, bf16[32,7168]{1,0:T(8,128)(2,1)S(1)}, u32[]{:S(2)}) copy-start(bf16[32,7168]{1,0:T(8,128)(2,1)S(1)} %constant_dynamic-update-slice_fusion.refs_2_) | copy-start | bytes 1376260
  133.2 17.9 %collective-permute-start.13 = (bf16[32,7168]{1,0:T(8,128)(2,1)S(1)}, bf16[32,7168]{1,0:T(8,128)(2,1)S(1)}, u32[]{:S(2)}, u32[]{:S(2)}) collective-permute-start(bf16[32,7168]{1,0:T(8,128)(2,1)S(1)} %constant_dynamic-update-slice_fusion.refs_2_), channel_id=1, source_target_pairs={{0,192},{16,80},{32,224},{48,112},{64,128},{80,16},{96,160},{112,4... | collective-permute-start | bytes 1376264 | tf_op jit(solution)/shard_map/ppermute | solution.py:36
  134.8 21.7 %collective-permute-start.27 = (bf16[32,7168]{1,0:T(8,128)(2,1)S(1)}, bf16[32,7168]{1,0:T(8,128)(2,1)S(1)}, u32[]{:S(2)}, u32[]{:S(2)}) collective-permute-start(bf16[32,7168]{1,0:T(8,128)(2,1)S(1)} %constant_dynamic-update-slice_fusion.3.refs_1_), channel_id=1, source_target_pairs={{0,16},{16,0},{32,48},{48,32},{64,80},{80,64},{96,112},{112,96},{1... | collective-permute-start | bytes 1376264 | tf_op jit(solution)/shard_map/ppermute | solution.py:17
  144.8 11.7 %copy-start.4 = (bf16[32,7168]{1,0:T(8,128)(2,1)}, bf16[32,7168]{1,0:T(8,128)(2,1)S(1)}, u32[]{:S(2)}) copy-start(bf16[32,7168]{1,0:T(8,128)(2,1)S(1)} %collective-permute-done.26.refs_2_) | copy-start | bytes 1376260
  144.8 11.6 %collective-permute-start.28 = (bf16[32,7168]{1,0:T(8,128)(2,1)S(1)}, bf16[32,7168]{1,0:T(8,128)(2,1)}, u32[]{:S(2)}, u32[]{:S(2)}) collective-permute-start(bf16[32,7168]{1,0:T(8,128)(2,1)S(1)} %collective-permute-done.26.refs_2_), channel_id=1, source_target_pairs={{0,16},{16,0},{32,48},{48,32},{64,80},{80,64},{96,112},{112,96},{1... | collective-permute-start | bytes 1376264 | tf_op jit(solution)/shard_map/ppermute | solution.py:17
  151.2 10.3 %collective-permute-start.14 = (bf16[32,7168]{1,0:T(8,128)(2,1)S(1)}, bf16[32,7168]{1,0:T(8,128)(2,1)S(1)}, u32[]{:S(2)}, u32[]{:S(2)}) collective-permute-start(bf16[32,7168]{1,0:T(8,128)(2,1)S(1)} %constant_dynamic-update-slice_fusion.refs_2_), channel_id=1, source_target_pairs={{0,16},{16,0},{32,48},{48,32},{64,80},{80,64},{96,112},{112,96},{1... | collective-permute-start | bytes 1376264 | tf_op jit(solution)/shard_map/ppermute | solution.py:17
  151.2 10.3 %copy-start.3 = (bf16[32,7168]{1,0:T(8,128)(2,1)}, bf16[32,7168]{1,0:T(8,128)(2,1)S(1)}, u32[]{:S(2)}) copy-start(bf16[32,7168]{1,0:T(8,128)(2,1)S(1)} %collective-permute-done.13.refs_3_) | copy-start | bytes 1376260
  151.2 10.3 %collective-permute-start.15 = (bf16[32,7168]{1,0:T(8,128)(2,1)S(1)}, bf16[32,7168]{1,0:T(8,128)(2,1)S(1)}, u32[]{:S(2)}, u32[]{:S(2)}) collective-permute-start(bf16[32,7168]{1,0:T(8,128)(2,1)S(1)} %collective-permute-done.13.refs_3_), channel_id=1, source_target_pairs={{0,16},{16,0},{32,48},{48,32},{64,80},{80,64},{96,112},{112,96},{1... | collective-permute-start | bytes 1376264 | tf_op jit(solution)/shard_map/ppermute | solution.py:17
  156.1 11.1 %collective-permute-start.30 = (bf16[448,256]{1,0:T(8,128)(2,1)}, bf16[448,256]{1,0:T(8,128)(2,1)S(1)}, u32[]{:S(2)}, u32[]{:S(2)}) collective-permute-start(bf16[448,256]{1,0:T(8,128)(2,1)} %reduce-scatter.2.cloned.1.call-done), channel_id=1, source_target_pairs={{0,240},{16,224},{32,208},{48,192},{64,176},{80,160},{96,144},{112... | collective-permute-start | bytes 688136 | tf_op jit(solution)/shard_map/ppermute | solution.py:335
  156.5 0.8 copy-start.6
  161.5 0.8 copy-start.5
  161.5 0.9 copy-start.7
  162.4 4.8 %copy-start.10 = (bf16[448,256]{1,0:T(8,128)(2,1)S(1)}, bf16[448,256]{1,0:T(8,128)(2,1)}, u32[]{:S(2)}) copy-start(bf16[448,256]{1,0:T(8,128)(2,1)} %reduce-scatter.2.cloned.1.call-done) | copy-start | bytes 688132
Sparse Core Ops, SparseCore 0:
  47.2 64.5 reduce-scatter.1

commit v3 on v2

v3 whole, which is shorter than its diff:
```python
import functools
import jax
import jax.numpy as jnp
from jax import lax
from jax.experimental import pallas as pl
from jax.experimental.pallas import tpu as pltpu
from jax.sharding import PartitionSpec as P

SLOT = 8
BF = jnp.bfloat16
F32 = jnp.float32
CORE, Y_HI, X_LOW = 1, 2, 4
STEPS = 4


def across(value, mask):
    return lax.ppermute(value, "pipe", [(i, i ^ mask) for i in range(16)])


def delta(p, k):
    return (p & 1) * 8 + (k ^ ((p >> 1) & 1)) * 4 + (p >> 2)


def shifted(value, k, mask=0):
    pairs = [
        (p * 16 + e, (p ^ mask) * 16 + (e ^ delta(p, k))) for p in range(16) for e in range(16)
    ]
    return lax.ppermute(value, ("pipe", "expert"), pairs)


def along_x(value, step):
    pairs = []
    for i in range(16):
        hop = 3 if (i & 1) ^ step else 1
        pairs.append((i, i ^ (X_LOW * hop)))
    return lax.ppermute(value, "pipe", pairs)


def dispatch(first, second):
    block = jnp.concatenate([shifted(first, 0), shifted(second, 1)], axis=0)
    two = jnp.concatenate([block, along_x(block, 0)], axis=0)
    return jnp.concatenate([two, along_x(two, 1)], axis=0)


def add(a, b):
    return (a.astype(F32) + b.astype(F32)).astype(BF)


def collect(kept, sent, after=None):
    two = add(kept, along_x(sent, 1))
    size = two.shape[0] // 2
    one = add(two[:size], along_x(two[size:], 0))
    full = add(one[:SLOT], across(one[SLOT:], Y_HI))
    block = jnp.concatenate([shifted(full, 0), shifted(full, 0, Y_HI)], axis=0)
    two = block, along_x(block, 0)
    two = jnp.concatenate(two, axis=0) if after is None else join(*two, after)
    rest = along_x(two, 1)
    return two, rest, across(two, CORE), across(rest, CORE)


def dot(a, b):
    return jnp.dot(a, b, preferred_element_type=F32)


def tdot(a, b):
    return lax.dot_general(a, b, (((1,), (1,)), ((), ())), preferred_element_type=F32)


def far(value):
    return pltpu.with_memory_space_constraint(value, pltpu.HBM)


def near(value):
    return pltpu.with_memory_space_constraint(value, pltpu.VMEM)


def cost(flops, nbytes):
    return pl.CostEstimate(flops=int(flops), bytes_accessed=int(nbytes), transcendentals=0)


def tables(p, s, ids, gates, rows):
    tok = ids.shape[1]
    row = lax.broadcasted_iota(jnp.int32, (rows, tok), 0)
    far_core, k = row >> 6, (row >> 3) & 1
    ring = (row >> 4) & 3
    off = ring ^ (ring >> 1)
    off = off ^ (2 * (off & 1) * ((p & 1) ^ far_core))
    base = s ^ ((p & 1) * 8 + ((p >> 1) & 1) * 4 + (p >> 2))
    expert = base ^ (far_core * 8) ^ (k * 4) ^ off
    named = jnp.zeros((rows, tok), F32)
    gate = jnp.zeros((rows, tok), F32)
    for choice in range(ids.shape[0]):
        hit = ids[choice : choice + 1, :] == expert
        named = jnp.where(hit, 1.0, named)
        gate = jnp.where(hit, gates[choice : choice + 1, :], gate)
    first = lax.broadcasted_iota(jnp.int32, (tok, tok), 0)
    second = lax.broadcasted_iota(jnp.int32, (tok, tok), 1)
    earlier = jnp.where(first < second, 1.0, 0.0).astype(BF)
    before = dot(named.astype(BF), earlier)
    slot = (row & (SLOT - 1)).astype(F32)
    here = jnp.logical_and(named > 0.5, before == slot)
    return jnp.where(here, 1.0, 0.0), jnp.where(here, gate, 0.0)


def select_kernel(
    p_ref, s_ref, ids_ref, gates_ref, tok_ref, grad_ref, lat_ref,
    send0, send1, dsend0, dsend1, mine_ref, other_ref, pick, weight,
):
    @pl.when(pl.program_id(0) == 0)
    def _():
        p, s = p_ref[0], s_ref[0]
        sel, mix = tables(p, s, ids_ref[...], gates_ref[...], 2 * SLOT)
        pick[...] = sel.astype(BF)
        total = jnp.sum(mix, axis=1, keepdims=True)
        weight[...] = jnp.broadcast_to(total, weight.shape)
        lat = lat_ref[0]
        width = lat.shape[1] // 2
        low = p < 8
        mine_ref[...] = jnp.where(low, lat[:, :width], lat[:, width:])
        other_ref[...] = jnp.where(low, lat[:, width:], lat[:, :width])

    rows = dot(pick[...], tok_ref[...]).astype(BF)
    drows = (dot(pick[...], grad_ref[...]) * weight[:, :1]).astype(BF)
    send0[...] = rows[:SLOT]
    send1[...] = rows[SLOT:]
    dsend0[...] = drows[:SLOT]
    dsend1[...] = drows[SLOT:]


def whole(shape):
    return pl.BlockSpec(shape, lambda i: (0,) * len(shape))


SCALAR = pl.BlockSpec(memory_space=pltpu.SMEM)


def select(p, s, ids, gates, tokens, grads, latent):
    tok, d = tokens.shape
    wide = d // STEPS
    width = latent.shape[2] // 2
    col = lambda rows: pl.BlockSpec((rows, wide), lambda i: (0, i))
    chunk = jax.ShapeDtypeStruct((SLOT, d), BF)
    half = jax.ShapeDtypeStruct((tok, width), BF)
    return pl.pallas_call(
        select_kernel,
        grid=(STEPS,),
        in_specs=[
            SCALAR,
            SCALAR,
            whole(ids.shape),
            whole(gates.shape),
            col(tok),
            col(tok),
            whole(latent.shape),
        ],
        out_specs=[col(SLOT)] * 4 + [whole((tok, width))] * 2,
        out_shape=[chunk] * 4 + [half] * 2,
        scratch_shapes=[pltpu.VMEM((2 * SLOT, tok), BF), pltpu.VMEM((2 * SLOT, tok), F32)],
        cost_estimate=cost(4 * 2 * SLOT * tok * d, 4 * tok * d),
        compiler_params=pltpu.CompilerParams(vmem_limit_bytes=16 << 20),
        name="select",
    )(p, s, ids, gates, far(tokens), far(grads), far(latent))


def latent_kernel(
    p_ref, s_ref, ids_ref, gates_ref, mine_ref, got_ref, tok_ref,
    out_ref, sel_ref, hi_ref, lo_ref, turned,
):
    i = pl.program_id(0)

    @pl.when(i == 0)
    def _():
        tok = ids_ref.shape[1]
        sel, mix = tables(p_ref[0], s_ref[0], ids_ref[...], gates_ref[...], tok)
        sel_ref[...] = sel.T.astype(BF)
        mix = mix.T
        hi = mix.astype(BF)
        hi_ref[...] = hi
        lo_ref[...] = (mix - hi.astype(F32)).astype(BF)
        turned[...] = (mine_ref[...].astype(F32) + got_ref[...].astype(F32)).astype(BF)

    part = lax.dot_general(tok_ref[...], turned[...], (((0,), (0,)), ((), ())), preferred_element_type=F32)
    out_ref[...] = part.astype(BF)


def latent_part(p, s, ids, gates, mine, got, tokens):
    tok, d = tokens.shape
    width = mine.shape[1]
    n = 16
    group = 4
    table = jax.ShapeDtypeStruct((tok, tok), BF)
    return pl.pallas_call(
        latent_kernel,
        grid=(n // group,),
        in_specs=[
            SCALAR,
            SCALAR,
            whole(ids.shape),
            whole(gates.shape),
            whole(mine.shape),
            whole(got.shape),
            pl.BlockSpec((tok, d // n * group), lambda i: (0, i)),
        ],
        out_specs=[pl.BlockSpec((d // n * group, width), lambda i: (i, 0))]
        + [whole((tok, tok))] * 3,
        out_shape=[pltpu.HBM((d, width), BF)] + [table] * 3,
        scratch_shapes=[pltpu.VMEM((tok, width), BF)],
        cost_estimate=cost(2 * tok * d * width, 2 * tok * d + 2 * d * width),
        compiler_params=pltpu.CompilerParams(vmem_limit_bytes=16 << 20),
        name="latent_part",
    )(p, s, ids, gates, mine, got, tokens)


def finish_kernel(p_ref, share_ref, theirs_ref, out_ref):
    low = p_ref[0] < 8
    share, theirs = share_ref[...], theirs_ref[...]
    width = share.shape[1]
    out_ref[0, :, :width] = jnp.where(low, share, theirs)
    out_ref[0, :, width:] = jnp.where(low, theirs, share)


def finish(p, share, theirs):
    rows, width = share.shape
    return pl.pallas_call(
        finish_kernel,
        in_specs=[SCALAR] + [pl.BlockSpec(memory_space=pltpu.VMEM)] * 2,
        out_specs=pl.BlockSpec(memory_space=pltpu.VMEM),
        out_shape=jax.ShapeDtypeStruct((1, rows, 2 * width), BF),
        cost_estimate=cost(0, 8 * width * rows),
        compiler_params=pltpu.CompilerParams(vmem_limit_bytes=8 << 20),
        name="finish",
    )(p, share, theirs)


def join_kernel(a, b, _, out):
    size = a.shape[0]
    out[:size] = a[...]
    out[size:] = b[...]


def join(a, b, after):
    vmem = pl.BlockSpec(memory_space=pltpu.VMEM)
    return pl.pallas_call(
        join_kernel,
        in_specs=[vmem] * 2 + [pl.BlockSpec(memory_space=pl.ANY)],
        out_specs=vmem,
        out_shape=pltpu.VMEM((2 * a.shape[0], a.shape[1]), a.dtype),
        cost_estimate=cost(0, 8 * a.size),
        compiler_params=pltpu.CompilerParams(vmem_limit_bytes=8 << 20),
        name="join",
    )(near(a), near(b), after)


PIECES = 7


def forward_kernel(rows, wg, wu, wg2, wu2, wd, wd2, _, kept, sent, fa, fb):
    n, d = rows.shape
    f = wg.shape[1]
    wide = d // PIECES
    acc = jnp.zeros((n, 4 * f), F32)
    for i in range(PIECES):
        at = pl.ds(i * wide, wide)
        weights = jnp.concatenate([wg[at, :], wg2[at, :], wu[at, :], wu2[at, :]], axis=1)
        acc = acc + dot(rows[:, at], weights)
    gate, up = acc[:, : 2 * f], acc[:, 2 * f :]
    sg = jax.nn.sigmoid(gate)
    hidden = (gate * sg * up).astype(BF)
    fa[...] = up * sg * (1.0 + gate * (1.0 - sg))
    fb[...] = gate * sg
    for i in range(PIECES):
        at = pl.ds(i * wide, wide)
        out = dot(hidden, jnp.concatenate([wd[:, at], wd2[:, at]], axis=0)).astype(BF)
        kept[:, at] = out[: n // 2]
        sent[:, at] = out[n // 2 :]


def forward(rows, wg, wu, wg2, wu2, wd, wd2, after):
    n, d = rows.shape
    f = wg.shape[1]
    vmem = pl.BlockSpec(memory_space=pltpu.VMEM)
    return pl.pallas_call(
        forward_kernel,
        in_specs=[vmem] * 7 + [pl.BlockSpec(memory_space=pl.ANY)],
        out_specs=[vmem] * 4,
        out_shape=[pltpu.VMEM((n // 2, d), BF)] * 2 + [pltpu.VMEM((n, 2 * f), F32)] * 2,
        cost_estimate=cost(12 * n * d * f, 12 * d * f + 4 * n * d),
        compiler_params=pltpu.CompilerParams(vmem_limit_bytes=12 << 20),
        name="forward",
    )(*map(near, (rows, wg, wu, wg2, wu2, wd, wd2)), after)


def backward_kernel(rows, fa, fb, wd, wd2, wg, wu, wg2, wu2, kept, sent):
    n, d = rows.shape
    f = wg.shape[1]
    wide = d // PIECES
    acc = jnp.zeros((n, 2 * f), F32)
    for i in range(PIECES):
        at = pl.ds(i * wide, wide)
        acc = acc + tdot(rows[:, at], jnp.concatenate([wd[:, at], wd2[:, at]], axis=0))
    grads = jnp.concatenate([(acc * fa[...]).astype(BF), (acc * fb[...]).astype(BF)], axis=1)
    for i in range(PIECES):
        at = pl.ds(i * wide, wide)
        weights = jnp.concatenate([wg[at, :], wg2[at, :], wu[at, :], wu2[at, :]], axis=1)
        out = tdot(grads, weights).astype(BF)
        kept[:, at] = out[: n // 2]
        sent[:, at] = out[n // 2 :]


def backward(rows, fa, fb, wd, wd2, wg, wu, wg2, wu2):
    n, d = rows.shape
    f = wg.shape[1]
    vmem = pl.BlockSpec(memory_space=pltpu.VMEM)
    return pl.pallas_call(
        backward_kernel,
        in_specs=[vmem] * 9,
        out_specs=[vmem] * 2,
        out_shape=[pltpu.VMEM((n // 2, d), BF)] * 2,
        cost_estimate=cost(12 * n * d * f, 12 * d * f + 4 * n * d),
        compiler_params=pltpu.CompilerParams(vmem_limit_bytes=12 << 20),
        name="backward",
    )(*map(near, (rows, fa, fb, wd, wd2, wg, wu, wg2, wu2)))


def combine_kernel(n_tables, *refs):
    mixing, parts, out, buf, sems = refs[:n_tables], refs[n_tables:-3], *refs[-3:]
    d = out.shape[1]
    wide = d // PIECES
    copies = []
    for i in range(PIECES):
        at = pl.ds(i * wide, wide)
        back = jnp.concatenate([part[:, at] for part in parts], axis=0)
        total = dot(mixing[0][...], back)
        for table in mixing[1:]:
            total = total + dot(table[...], back)
        buf[:, at] = total.astype(BF)
        copy = pltpu.make_async_copy(buf.at[:, at], out.at[:, at], sems.at[i])
        copy.start()
        copies.append(copy)
    for copy in copies:
        copy.wait()


def combine(mixing, parts):
    tok = mixing[0].shape[0]
    d = parts[0].shape[1]
    vmem = pl.BlockSpec(memory_space=pltpu.VMEM)
    return pl.pallas_call(
        functools.partial(combine_kernel, len(mixing)),
        in_specs=[vmem] * (len(mixing) + len(parts)),
        out_specs=pl.BlockSpec(memory_space=pl.ANY),
        out_shape=jax.ShapeDtypeStruct((tok, d), BF),
        scratch_shapes=[pltpu.VMEM((tok, d), BF), pltpu.SemaphoreType.DMA((PIECES,))],
        cost_estimate=cost(2 * tok * tok * d * len(mixing), 4 * tok * d),
        compiler_params=pltpu.CompilerParams(vmem_limit_bytes=12 << 20),
        name="combine",
    )(*map(near, mixing), *map(near, parts))


def per_device(tokens, route_ids, route_gates, w_gate, w_up, w_down, out_grad, latent_grad):
    p = lax.axis_index("pipe").reshape(1).astype(jnp.int32)
    s = lax.axis_index("expert").reshape(1).astype(jnp.int32)
    ids, gates = route_ids.T, route_gates.T
    wg, wu, wd = w_gate[0], w_up[0], w_down[0]
    wg2, wu2, wd2 = across(wg, CORE), across(wu, CORE), across(wd, CORE)
    mirror = [(i, 15 - i) for i in range(16)]

    send0, send1, dsend0, dsend1, mine, other = select(
        p, s, ids, gates, tokens, out_grad, latent_grad
    )
    got = lax.ppermute(other, "pipe", mirror)
    part, sel, hi, lo = latent_part(p, s, ids, gates, mine, got, tokens)
    share = lax.psum_scatter(part, "expert", scatter_dimension=0, tiled=True)
    theirs = lax.ppermute(share, "pipe", mirror)
    kv_grad = finish(p, share, theirs)

    rows = dispatch(send0, send1)
    drows = dispatch(dsend0, dsend1)
    kept, sent, fa, fb = forward(rows, wg, wu, wg2, wu2, wd, wd2, hi)
    routed = combine([hi, lo], collect(kept, sent))
    dkept, dsent = backward(drows, fa, fb, wd, wd2, wg, wu, wg2, wu2)
    token_grad = combine([sel], collect(dkept, dsent, share))
    return routed, token_grad, kv_grad


def solution(mesh):
    return jax.shard_map(
        per_device,
        mesh=mesh,
        in_specs=(
            P("expert", None),
            P("expert", None),
            P("expert", None),
            P("expert", None, "pipe"),
            P("expert", None, "pipe"),
            P("expert", "pipe", None),
            P("expert", None),
            P("pipe", "expert", None),
        ),
        out_specs=(P("expert", None), P("expert", None), P("pipe", "expert", None)),
        check_vma=False,
    )
```

time: 176 us -> 159 us (0.903)
  Pallas kernels: 39.2 us -> 22.5 us
  waiting for transfers between devices: 39.5 us -> 44.9 us
  local copies, waits for them, and re-layouts: 5.12 us -> 1.49 us
  other arithmetic: 3.93 us -> 0.62 us
  starting transfers between devices: 72.8 us -> 74.7 us
    pallas_call x6 -> x8, Pallas kernels: 39.2 us -> 22.5 us  [the longest x1 6.63 us: backward(): pl.pallas_call(backward_kernel, in_specs=[vmem] * 9, out_specs=[vmem] * 2...]
    ppermute x8, waiting for transfers between devices: 6.2 us -> 14.3 us  [shifted(): return lax.ppermute(value, ('pipe', 'expert'), pairs)]
    ppermute x1, starting transfers between devices: 0.39 us -> 5.42 us  [per_device(): theirs = lax.ppermute(share, 'pipe', mirror)]
    ppermute x12, starting transfers between devices: 15.9 us -> 11.4 us  [along_x(): return lax.ppermute(value, 'pipe', pairs)]
    ppermute x1, waiting for transfers between devices: 0.27 us -> 4.42 us  [per_device(): theirs = lax.ppermute(share, 'pipe', mirror)]
    unnamed x30 -> x15, local copies, waits for them, and re-layouts: 5.03 us -> 1.41 us
    ppermute x9, waiting for transfers between devices: 6.02 us -> 2.47 us  [across(): return lax.ppermute(value, 'pipe', [(i, i ^ mask) for i in range(16)])]
    ppermute x12, waiting for transfers between devices: 27 us -> 23.7 us  [along_x(): return lax.ppermute(value, 'pipe', pairs)]
  transfers between devices with their start and end apart: 32 -> 32, of which waited for: 11 -> 13; matrix products, arithmetic and copies ran while one was open for 1% -> 0% of each run, Pallas kernels for 20% -> 11%
where the time goes in v3:
time: 159 us
  starting transfers between devices  74.7 us (47%)
  waiting for transfers between devices  44.9 us (28%)
  Pallas kernels  22.5 us (14%)
  between operations  14.4 us (9%)
    ppermute x8, starting transfers between devices, shifted(): return lax.ppermute(value, ('pipe', 'expert'), pairs)  29.7 us
    ppermute x12, waiting for transfers between devices, along_x(): return lax.ppermute(value, 'pipe', pairs)  23.7 us
    ppermute x9, starting transfers between devices, across(): return lax.ppermute(value, 'pipe', [(i, i ^ mask) for i in range(16)])  22.7 us
    ppermute x8, waiting for transfers between devices, shifted(): return lax.ppermute(value, ('pipe', 'expert'), pairs)  14.3 us
    ppermute x12, starting transfers between devices, along_x(): return lax.ppermute(value, 'pipe', pairs)  11.4 us
    pallas_call x1, Pallas kernels, backward(): pl.pallas_call(backward_kernel, in_specs=[vmem] * 9, out_specs=[vmem] * 2...  6.63 us
    ppermute x1, starting transfers between devices, per_device(): theirs = lax.ppermute(share, 'pipe', mirror)  5.42 us
    ppermute x1, starting transfers between devices, per_device(): got = lax.ppermute(other, 'pipe', mirror)  5.42 us
  transfers between devices with their start and end apart: 32, of which 13 were waited for; matrix products, arithmetic and copies ran while one was open for 0% of the time, Pallas kernels for 11%

profile of v3, /device:TPU:1, one launch (start us, length us, event | category | flops | bytes accessed | tf_op | source)
XLA Modules:
  0.0 158.7 jit_solution(8620633203691953387)
XLA Ops:
  7.2 0.0 reduce-scatter.2.cloned.1.call-start
  7.2 0.7 copy-done.4
  7.9 0.7 copy-done.5
  8.6 3.5 %select.1 = (bf16[8,7168]{1,0:T(8,128)(2,1)S(1)}, bf16[8,7168]{1,0:T(8,128)(2,1)S(1)}, bf16[8,7168]{1,0:T(8,128)(2,1)S(1)}, bf16[8,7168]{1,0:T(8,128)(2,1)S(1)},...) custom-call(s32[1]{0:T(128)} %bitcast.p_ref, s32[1]{0:T(128)} %bitcast.1.s_ref, s32[8,128]{1,0:T(8,128)S(1)} %bitcast.16, ...), custom_call_target="tpu_custom_call" | custom-call | flops 58720256 | bytes 3670016 | tf_op jit(solution)/shard_map/select/pallas_call | solution.py:144
  12.1 4.0 %collective-permute-start.1 = (bf16[8,7168]{1,0:T(8,128)(2,1)S(1)}, bf16[8,7168]{1,0:T(8,128)(2,1)S(1)}, u32[]{:S(2)}, u32[]{:S(2)}) collective-permute-start(bf16[8,7168]{1,0:T(8,128)(2,1)S(1)} %get-tuple-element.23), channel_id=1, source_target_pairs={{0,0},{1,1},{2,2},{3,3},{4,4},{5,5},{6,6},{7,7},{8,8},{9,9},{10,10... | collective-permute-start | bytes 344072 | tf_op jit(solution)/shard_map/ppermute | solution.py:28
  16.2 8.7 %collective-permute-start.2 = (bf16[8,7168]{1,0:T(8,128)(2,1)S(1)}, bf16[8,7168]{1,0:T(8,128)(2,1)S(1)}, u32[]{:S(2)}, u32[]{:S(2)}) collective-permute-start(bf16[8,7168]{1,0:T(8,128)(2,1)S(1)} %get-tuple-element.24), channel_id=1, source_target_pairs={{0,4},{1,5},{2,6},{3,7},{4,0},{5,1},{6,2},{7,3},{8,12},{9,13},{10,... | collective-permute-start | bytes 344072 | tf_op jit(solution)/shard_map/ppermute | solution.py:28
  24.9 5.4 %collective-permute-start = (bf16[128,256]{1,0:T(8,128)(2,1)S(1)}, bf16[128,256]{1,0:T(8,128)(2,1)S(1)}, u32[]{:S(2)}, u32[]{:S(2)}) collective-permute-start(bf16[128,256]{1,0:T(8,128)(2,1)S(1)} %get-tuple-element.20), channel_id=1, source_target_pairs={{0,240},{16,224},{32,208},{48,192},{64,176},{80,160},{96,144},{112... | collective-permute-start | bytes 196616 | tf_op jit(solution)/shard_map/ppermute | solution.py:371
  30.3 2.3 %collective-permute-start.17 = (bf16[8,7168]{1,0:T(8,128)(2,1)S(1)}, bf16[8,7168]{1,0:T(8,128)(2,1)S(1)}, u32[]{:S(2)}, u32[]{:S(2)}) collective-permute-start(bf16[8,7168]{1,0:T(8,128)(2,1)S(1)} %get-tuple-element.28), channel_id=1, source_target_pairs={{0,0},{1,1},{2,2},{3,3},{4,4},{5,5},{6,6},{7,7},{8,8},{9,9},{10,10... | collective-permute-start | bytes 344072 | tf_op jit(solution)/shard_map/ppermute | solution.py:28
  32.6 3.8 %collective-permute-start.18 = (bf16[8,7168]{1,0:T(8,128)(2,1)S(1)}, bf16[8,7168]{1,0:T(8,128)(2,1)S(1)}, u32[]{:S(2)}, u32[]{:S(2)}) collective-permute-start(bf16[8,7168]{1,0:T(8,128)(2,1)S(1)} %get-tuple-element.29), channel_id=1, source_target_pairs={{0,4},{1,5},{2,6},{3,7},{4,0},{5,1},{6,2},{7,3},{8,12},{9,13},{10,... | collective-permute-start | bytes 344072 | tf_op jit(solution)/shard_map/ppermute | solution.py:28
  36.4 0.0 collective-permute-done.got_ref
  36.4 0.1 collective-permute-start.5
  36.5 3.6 %latent_part.1 = (bf16[7168,256]{1,0:T(8,128)(2,1)}, bf16[128,128]{1,0:T(8,128)(2,1)S(1)}, bf16[128,128]{1,0:T(8,128)(2,1)S(1)}, bf16[128,128]{1,0:T(8,128)(2,1)S(1)}) custom-call(s32[1]{0:T(128)} %bitcast.p_ref, s32[1]{0:T(128)} %bitcast.1.s_ref, s32[8,128]{1,0:T(8,128)S(1)} %bitcast.17, f32[8,128]{1,0:T(8,128)S(1)} %bitcast.19, ...), custom_call_target="tpu_custom_call" | custom-call | flops 469762048 | bytes 5505024 | tf_op jit(solution)/shard_map/latent_part/pallas_call | solution.py:192
  40.1 0.0 reduce-scatter.2.cloned.1.call-update
  40.2 0.6 collective-permute-start.6
  40.7 0.1 collective-permute-start.7
  40.9 0.1 collective-permute-start.3
  41.0 2.9 %collective-permute-done.18 = bf16[8,7168]{1,0:T(8,128)(2,1)S(1)} collective-permute-done((bf16[8,7168]{1,0:T(8,128)(2,1)S(1)}, bf16[8,7168]{1,0:T(8,128)(2,1)S(1)}, u32[]{:S(2)}, u32[]{:S(2)}) %collective-permute-start.18) | collective-permute-done | bytes 114720 | tf_op jit(solution)/shard_map/ppermute | solution.py:28
  43.9 0.0 copy-start.2
  43.9 0.0 copy-start.3
  43.9 0.1 collective-permute-start.19
  44.0 3.0 %collective-permute-done.3 = bf16[16,7168]{1,0:T(8,128)(2,1)S(1)} collective-permute-done((bf16[16,7168]{1,0:T(8,128)(2,1)S(1)}, bf16[16,7168]{1,0:T(8,128)(2,1)S(1)}, u32[]{:S(2)}, u32[]{:S(2)}) %collective-permute-start.3) | collective-permute-done | bytes 229408 | tf_op jit(solution)/shard_map/ppermute | solution.py:36
  47.1 0.1 collective-permute-start.4
  47.2 2.9 %collective-permute-done.19 = bf16[16,7168]{1,0:T(8,128)(2,1)S(1)} collective-permute-done((bf16[16,7168]{1,0:T(8,128)(2,1)S(1)}, bf16[16,7168]{1,0:T(8,128)(2,1)S(1)}, u32[]{:S(2)}, u32[]{:S(2)}) %collective-permute-start.19) | collective-permute-done | bytes 229408 | tf_op jit(solution)/shard_map/ppermute | solution.py:36
  50.1 0.1 collective-permute-start.20
  50.2 4.7 %collective-permute-done.4 = bf16[32,7168]{1,0:T(8,128)(2,1)S(1)} collective-permute-done((bf16[32,7168]{1,0:T(8,128)(2,1)S(1)}, bf16[32,7168]{1,0:T(8,128)(2,1)S(1)}, u32[]{:S(2)}, u32[]{:S(2)}) %collective-permute-start.4) | collective-permute-done | bytes 458784 | tf_op jit(solution)/shard_map/ppermute | solution.py:36
  54.9 0.1 pad_maximum_fusion.rows
  55.0 3.6 %forward.1 = (bf16[32,7168]{1,0:T(8,128)(2,1)S(1)}, bf16[32,7168]{1,0:T(8,128)(2,1)S(1)}, f32[64,256]{1,0:T(8,128)S(1)}, f32[64,256]{1,0:T(8,128)S(1)}) custom-call(bf16[64,7168]{1,0:T(8,128)(2,1)S(1)} %pad_maximum_fusion.rows, bf16[7168,128]{1,0:T(8,128)(2,1)S(1)} %bitcast.8, bf16[7168,128]{1,0:T(8,128)(2,1)S(1)} %bitcast.11, ...), custom_call_target="tpu_custom_call" | custom-call | flops 704643072 | bytes 12845056 | tf_op jit(solution)/shard_map/forward/pallas_call | solution.py:282
  58.7 0.8 collective-permute-start.8
  59.4 0.3 collective-permute-done.20
  59.7 0.1 pad_maximum_fusion.1.rows
  59.8 6.6 %backward.1 = (bf16[32,7168]{1,0:T(8,128)(2,1)S(1)}, bf16[32,7168]{1,0:T(8,128)(2,1)S(1)}) custom-call(bf16[64,7168]{1,0:T(8,128)(2,1)S(1)} %pad_maximum_fusion.1.rows, f32[64,256]{1,0:T(8,128)S(1)} %get-tuple-element.30.fa, f32[64,256]{1,0:T(8,128)S(1)} %get-tuple-element.31.fb, bf16[128,7168]{1,0:T(8,128)(2,1)S(1)} %bitcast.15, ...), custom_call_target="tpu_custom_call" | custom-call | flops 704643072 | bytes 12845056 | tf_op jit(solution)/shard_map/backward/pallas_call | solution.py:314
  66.4 0.9 collective-permute-start.21
  67.3 0.1 add_convert_fusion.1
  67.4 0.1 collective-permute-start.9
  67.5 6.7 %collective-permute-done.21 = bf16[32,7168]{1,0:T(8,128)(2,1)S(1)} collective-permute-done((bf16[32,7168]{1,0:T(8,128)(2,1)S(1)}, bf16[32,7168]{1,0:T(8,128)(2,1)S(1)}, u32[]{:S(2)}, u32[]{:S(2)}) %collective-permute-start.21) | collective-permute-done | bytes 458784 | tf_op jit(solution)/shard_map/ppermute | solution.py:36
  74.2 0.1 add_convert_fusion
  74.4 0.3 collective-permute-start.22
  74.7 0.1 add_convert_fusion.3
  74.8 2.1 %collective-permute-start.10 = (bf16[8,7168]{1,0:T(8,128)(2,1)S(1)}, bf16[8,7168]{1,0:T(8,128)(2,1)S(1)}, u32[]{:S(2)}, u32[]{:S(2)}) collective-permute-start(bf16[8,7168]{1,0:T(8,128)(2,1)S(1)} %slice.35), channel_id=1, source_target_pairs={{0,32},{16,48},{32,0},{48,16},{64,96},{80,112},{96,64},{112,80},{1... | collective-permute-start | bytes 344072 | tf_op jit(solution)/shard_map/ppermute | solution.py:17
  76.9 4.5 %collective-permute-done.22 = bf16[16,7168]{1,0:T(8,128)(2,1)S(1)} collective-permute-done((bf16[16,7168]{1,0:T(8,128)(2,1)S(1)}, bf16[16,7168]{1,0:T(8,128)(2,1)S(1)}, u32[]{:S(2)}, u32[]{:S(2)}) %collective-permute-start.22) | collective-permute-done | bytes 229408 | tf_op jit(solution)/shard_map/ppermute | solution.py:36
  81.4 0.1 add_convert_fusion.2
  81.4 1.8 %collective-permute-start.23 = (bf16[8,7168]{1,0:T(8,128)(2,1)S(1)}, bf16[8,7168]{1,0:T(8,128)(2,1)S(1)}, u32[]{:S(2)}, u32[]{:S(2)}) collective-permute-start(bf16[8,7168]{1,0:T(8,128)(2,1)S(1)} %slice.39), channel_id=1, source_target_pairs={{0,32},{16,48},{32,0},{48,16},{64,96},{80,112},{96,64},{112,80},{1... | collective-permute-start | bytes 344072 | tf_op jit(solution)/shard_map/ppermute | solution.py:17
  83.2 4.1 %collective-permute-start.12 = (bf16[8,7168]{1,0:T(8,128)(2,1)S(1)}, bf16[8,7168]{1,0:T(8,128)(2,1)S(1)}, u32[]{:S(2)}, u32[]{:S(2)}) collective-permute-start(bf16[8,7168]{1,0:T(8,128)(2,1)S(1)} %add_convert_fusion.5), channel_id=1, source_target_pairs={{0,32},{1,33},{2,34},{3,35},{4,36},{5,37},{6,38},{7,39},{8,40},{9,... | collective-permute-start | bytes 344072 | tf_op jit(solution)/shard_map/ppermute | solution.py:28
  87.4 1.9 %collective-permute-start.11 = (bf16[8,7168]{1,0:T(8,128)(2,1)S(1)}, bf16[8,7168]{1,0:T(8,128)(2,1)S(1)}, u32[]{:S(2)}, u32[]{:S(2)}) collective-permute-start(bf16[8,7168]{1,0:T(8,128)(2,1)S(1)} %add_convert_fusion.5), channel_id=1, source_target_pairs={{0,0},{1,1},{2,2},{3,3},{4,4},{5,5},{6,6},{7,7},{8,8},{9,9},{10,10... | collective-permute-start | bytes 344072 | tf_op jit(solution)/shard_map/ppermute | solution.py:28
  89.3 2.4 %collective-permute-done.23 = bf16[8,7168]{1,0:T(8,128)(2,1)S(1)} collective-permute-done((bf16[8,7168]{1,0:T(8,128)(2,1)S(1)}, bf16[8,7168]{1,0:T(8,128)(2,1)S(1)}, u32[]{:S(2)}, u32[]{:S(2)}) %collective-permute-start.23) | collective-permute-done | bytes 114720 | tf_op jit(solution)/shard_map/ppermute | solution.py:17
  91.8 1.7 %collective-permute-start.25 = (bf16[8,7168]{1,0:T(8,128)(2,1)S(1)}, bf16[8,7168]{1,0:T(8,128)(2,1)S(1)}, u32[]{:S(2)}, u32[]{:S(2)}) collective-permute-start(bf16[8,7168]{1,0:T(8,128)(2,1)S(1)} %add_convert_fusion.4), channel_id=1, source_target_pairs={{0,32},{1,33},{2,34},{3,35},{4,36},{5,37},{6,38},{7,39},{8,40},{9,... | collective-permute-start | bytes 344072 | tf_op jit(solution)/shard_map/ppermute | solution.py:28
  93.5 3.2 %collective-permute-start.24 = (bf16[8,7168]{1,0:T(8,128)(2,1)S(1)}, bf16[8,7168]{1,0:T(8,128)(2,1)S(1)}, u32[]{:S(2)}, u32[]{:S(2)}) collective-permute-start(bf16[8,7168]{1,0:T(8,128)(2,1)S(1)} %add_convert_fusion.4), channel_id=1, source_target_pairs={{0,0},{1,1},{2,2},{3,3},{4,4},{5,5},{6,6},{7,7},{8,8},{9,9},{10,10... | collective-permute-start | bytes 344072 | tf_op jit(solution)/shard_map/ppermute | solution.py:28
  96.7 2.9 %collective-permute-done.11 = bf16[8,7168]{1,0:T(8,128)(2,1)S(1)} collective-permute-done((bf16[8,7168]{1,0:T(8,128)(2,1)S(1)}, bf16[8,7168]{1,0:T(8,128)(2,1)S(1)}, u32[]{:S(2)}, u32[]{:S(2)}) %collective-permute-start.11) | collective-permute-done | bytes 114720 | tf_op jit(solution)/shard_map/ppermute | solution.py:28
  99.6 0.1 collective-permute-start.13
  99.7 3.5 %collective-permute-done.24 = bf16[8,7168]{1,0:T(8,128)(2,1)S(1)} collective-permute-done((bf16[8,7168]{1,0:T(8,128)(2,1)S(1)}, bf16[8,7168]{1,0:T(8,128)(2,1)S(1)}, u32[]{:S(2)}, u32[]{:S(2)}) %collective-permute-start.24) | collective-permute-done | bytes 114720 | tf_op jit(solution)/shard_map/ppermute | solution.py:28
  103.3 5.0 %collective-permute-done.25 = bf16[8,7168]{1,0:T(8,128)(2,1)S(1)} collective-permute-done((bf16[8,7168]{1,0:T(8,128)(2,1)S(1)}, bf16[8,7168]{1,0:T(8,128)(2,1)S(1)}, u32[]{:S(2)}, u32[]{:S(2)}) %collective-permute-start.25) | collective-permute-done | bytes 114720 | tf_op jit(solution)/shard_map/ppermute | solution.py:28
  108.3 5.1 %collective-permute-start.26 = (bf16[16,7168]{1,0:T(8,128)(2,1)S(1)}, bf16[16,7168]{1,0:T(8,128)(2,1)S(1)}, u32[]{:S(2)}, u32[]{:S(2)}) collective-permute-start(bf16[16,7168]{1,0:T(8,128)(2,1)S(1)} %constant_dynamic-update-slice_fusion.3.a), channel_id=1, source_target_pairs={{0,64},{16,208},{32,96},{48,240},{64,0},{80,144},{96,32},{112,176}... | collective-permute-start | bytes 688136 | tf_op jit(solution)/shard_map/ppermute | solution.py:36
  113.4 2.0 %collective-permute-start.14 = (bf16[32,7168]{1,0:T(8,128)(2,1)S(1)}, bf16[32,7168]{1,0:T(8,128)(2,1)S(1)}, u32[]{:S(2)}, u32[]{:S(2)}) collective-permute-start(bf16[32,7168]{1,0:T(8,128)(2,1)S(1)} %constant_dynamic-update-slice_fusion.refs_2_), channel_id=1, source_target_pairs={{0,192},{16,80},{32,224},{48,112},{64,128},{80,16},{96,160},{112,4... | collective-permute-start | bytes 1376264 | tf_op jit(solution)/shard_map/ppermute | solution.py:36
  115.5 1.6 %collective-permute-done.26.b = bf16[16,7168]{1,0:T(8,128)(2,1)S(1)} collective-permute-done((bf16[16,7168]{1,0:T(8,128)(2,1)S(1)}, bf16[16,7168]{1,0:T(8,128)(2,1)S(1)}, u32[]{:S(2)}, u32[]{:S(2)}) %collective-permute-start.26) | collective-permute-done | bytes 229408 | tf_op jit(solution)/shard_map/ppermute | solution.py:36
  117.1 1.7 %collective-permute-start.27 = (bf16[32,7168]{1,0:T(8,128)(2,1)S(1)}, bf16[32,7168]{1,0:T(8,128)(2,1)S(1)}, u32[]{:S(2)}, u32[]{:S(2)}) collective-permute-start(bf16[32,7168]{1,0:T(8,128)(2,1)S(1)} %join.1.refs_1_), channel_id=1, source_target_pairs={{0,192},{16,80},{32,224},{48,112},{64,128},{80,16},{96,160},{112,4... | collective-permute-start | bytes 1376264 | tf_op jit(solution)/shard_map/ppermute | solution.py:36
  118.9 11.6 %collective-permute-start.15 = (bf16[32,7168]{1,0:T(8,128)(2,1)S(1)}, bf16[32,7168]{1,0:T(8,128)(2,1)S(1)}, u32[]{:S(2)}, u32[]{:S(2)}) collective-permute-start(bf16[32,7168]{1,0:T(8,128)(2,1)S(1)} %constant_dynamic-update-slice_fusion.refs_2_), channel_id=1, source_target_pairs={{0,16},{16,0},{32,48},{48,32},{64,80},{80,64},{96,112},{112,96},{1... | collective-permute-start | bytes 1376264 | tf_op jit(solution)/shard_map/ppermute | solution.py:17
  130.5 0.0 collective-permute-start.16
  130.5 0.5 collective-permute-start.28
  131.0 5.9 %collective-permute-start.29 = (bf16[32,7168]{1,0:T(8,128)(2,1)S(1)}, bf16[32,7168]{1,0:T(8,128)(2,1)S(1)}, u32[]{:S(2)}, u32[]{:S(2)}) collective-permute-start(bf16[32,7168]{1,0:T(8,128)(2,1)S(1)} %collective-permute-done.27.refs_2_), channel_id=1, source_target_pairs={{0,16},{16,0},{32,48},{48,32},{64,80},{80,64},{96,112},{112,96},{1... | collective-permute-start | bytes 1376264 | tf_op jit(solution)/shard_map/ppermute | solution.py:17
  136.9 5.4 %collective-permute-start.30 = (bf16[448,256]{1,0:T(8,128)(2,1)}, bf16[448,256]{1,0:T(8,128)(2,1)S(1)}, u32[]{:S(2)}, u32[]{:S(2)}) collective-permute-start(bf16[448,256]{1,0:T(8,128)(2,1)} %reduce-scatter.2.cloned.1.call-done._.share_ref), channel_id=1, source_target_pairs={{0,240},{16,224},{32,208},{48,192},{64,176},{80,160},{96,144},{112... | collective-permute-start | bytes 688136 | tf_op jit(solution)/shard_map/ppermute | solution.py:374
  142.3 1.9 %combine.2 = bf16[128,7168]{1,0:T(8,128)(2,1)} custom-call(bf16[128,128]{1,0:T(8,128)(2,1)S(1)} %get-tuple-element.21._.refs_0_, bf16[128,128]{1,0:T(8,128)(2,1)S(1)} %get-tuple-element.22.refs_1_, bf16[32,7168]{1,0:T(8,128)(2,1)S(1)} %constant_dynamic-update-slice_fusion.refs_2_, bf16[32,7168]{1,0:T(8,128)(2,1)S(1)} %collective-permute-done.14.refs_3_, ...), custom_call_target="tpu_custom_call" | custom-call | flops 469762048 | bytes 3670016 | tf_op jit(solution)/shard_map/combine/pallas_call | solution.py:348
  144.2 4.4 %collective-permute-done.30.theirs_ref = bf16[448,256]{1,0:T(8,128)(2,1)S(1)} collective-permute-done((bf16[448,256]{1,0:T(8,128)(2,1)}, bf16[448,256]{1,0:T(8,128)(2,1)S(1)}, u32[]{:S(2)}, u32[]{:S(2)}) %collective-permute-start.30) | collective-permute-done | bytes 229408 | tf_op jit(solution)/shard_map/ppermute | solution.py:374
  148.6 1.7 %finish.1 = bf16[1,448,512]{2,1,0:T(8,128)(2,1)} custom-call(s32[1]{0:T(128)} %bitcast.p_ref, bf16[448,256]{1,0:T(8,128)(2,1)} %reduce-scatter.2.cloned.1.call-done._.share_ref, bf16[448,256]{1,0:T(8,128)(2,1)S(1)} %collective-permute-done.30.theirs_ref), custom_call_target="tpu_custom_call" | custom-call | bytes 917504 | tf_op jit(solution)/shard_map/finish/pallas_call | solution.py:224
  150.4 1.5 combine.3
  (43 shorter events, 0.4 us)
Async XLA Ops:
  7.2 109.9 %reduce-scatter.2.cloned.1.call-start = ((), (), s32[]{:S(2)}) async-start(), calls=%async_computation.1 | async-start | bytes 3899392 | tf_op jit(solution)/shard_map/reduce_scatter | solution.py:373
  7.2 0.7 copy-start.4
  7.9 0.7 copy-start.5
  8.6 27.8 %copy-start.1 = (bf16[1,7168,128]{2,1,0:T(8,128)(2,1)S(1)}, bf16[1,7168,128]{2,1,0:T(8,128)(2,1)}, u32[]{:S(2)}) copy-start(bf16[1,7168,128]{2,1,0:T(8,128)(2,1)} %param.11) | copy-start | bytes 5505028
  8.6 27.9 %copy-start = (bf16[128,7168]{1,0:T(8,128)(2,1)S(1)}, bf16[128,7168]{1,0:T(8,128)(2,1)}, u32[]{:S(2)}) copy-start(bf16[128,7168]{1,0:T(8,128)(2,1)} %tok_ref.3) | copy-start | bytes 5505028
  12.1 28.0 %collective-permute-start.1 = (bf16[8,7168]{1,0:T(8,128)(2,1)S(1)}, bf16[8,7168]{1,0:T(8,128)(2,1)S(1)}, u32[]{:S(2)}, u32[]{:S(2)}) collective-permute-start(bf16[8,7168]{1,0:T(8,128)(2,1)S(1)} %get-tuple-element.23), channel_id=1, source_target_pairs={{0,0},{1,1},{2,2},{3,3},{4,4},{5,5},{6,6},{7,7},{8,8},{9,9},{10,10... | collective-permute-start | bytes 344072 | tf_op jit(solution)/shard_map/ppermute | solution.py:28
  16.2 24.6 %collective-permute-start.2 = (bf16[8,7168]{1,0:T(8,128)(2,1)S(1)}, bf16[8,7168]{1,0:T(8,128)(2,1)S(1)}, u32[]{:S(2)}, u32[]{:S(2)}) collective-permute-start(bf16[8,7168]{1,0:T(8,128)(2,1)S(1)} %get-tuple-element.24), channel_id=1, source_target_pairs={{0,4},{1,5},{2,6},{3,7},{4,0},{5,1},{6,2},{7,3},{8,12},{9,13},{10,... | collective-permute-start | bytes 344072 | tf_op jit(solution)/shard_map/ppermute | solution.py:28
  24.9 11.5 %collective-permute-start = (bf16[128,256]{1,0:T(8,128)(2,1)S(1)}, bf16[128,256]{1,0:T(8,128)(2,1)S(1)}, u32[]{:S(2)}, u32[]{:S(2)}) collective-permute-start(bf16[128,256]{1,0:T(8,128)(2,1)S(1)} %get-tuple-element.20), channel_id=1, source_target_pairs={{0,240},{16,224},{32,208},{48,192},{64,176},{80,160},{96,144},{112... | collective-permute-start | bytes 196616 | tf_op jit(solution)/shard_map/ppermute | solution.py:371
  30.3 10.6 %collective-permute-start.17 = (bf16[8,7168]{1,0:T(8,128)(2,1)S(1)}, bf16[8,7168]{1,0:T(8,128)(2,1)S(1)}, u32[]{:S(2)}, u32[]{:S(2)}) collective-permute-start(bf16[8,7168]{1,0:T(8,128)(2,1)S(1)} %get-tuple-element.28), channel_id=1, source_target_pairs={{0,0},{1,1},{2,2},{3,3},{4,4},{5,5},{6,6},{7,7},{8,8},{9,9},{10,10... | collective-permute-start | bytes 344072 | tf_op jit(solution)/shard_map/ppermute | solution.py:28
  32.6 11.3 %collective-permute-start.18 = (bf16[8,7168]{1,0:T(8,128)(2,1)S(1)}, bf16[8,7168]{1,0:T(8,128)(2,1)S(1)}, u32[]{:S(2)}, u32[]{:S(2)}) collective-permute-start(bf16[8,7168]{1,0:T(8,128)(2,1)S(1)} %get-tuple-element.29), channel_id=1, source_target_pairs={{0,4},{1,5},{2,6},{3,7},{4,0},{5,1},{6,2},{7,3},{8,12},{9,13},{10,... | collective-permute-start | bytes 344072 | tf_op jit(solution)/shard_map/ppermute | solution.py:28
  36.4 18.5 %collective-permute-start.5 = (bf16[7168,128]{1,0:T(8,128)(2,1)S(1)}, bf16[7168,128]{1,0:T(8,128)(2,1)}, u32[]{:S(2)}, u32[]{:S(2)}) collective-permute-start(bf16[7168,128]{1,0:T(8,128)(2,1)S(1)} %bitcast.7), channel_id=1, source_target_pairs={{0,16},{16,0},{32,48},{48,32},{64,80},{80,64},{96,112},{112,96},{1... | collective-permute-start | bytes 5505032 | tf_op jit(solution)/shard_map/ppermute | solution.py:17
  40.2 14.8 %collective-permute-start.6 = (bf16[7168,128]{1,0:T(8,128)(2,1)}, bf16[7168,128]{1,0:T(8,128)(2,1)S(1)}, u32[]{:S(2)}, u32[]{:S(2)}) collective-permute-start(bf16[7168,128]{1,0:T(8,128)(2,1)} %bitcast.10), channel_id=1, source_target_pairs={{0,16},{16,0},{32,48},{48,32},{64,80},{80,64},{96,112},{112,96},{1... | collective-permute-start | bytes 5505032 | tf_op jit(solution)/shard_map/ppermute | solution.py:17
  40.7 14.2 %collective-permute-start.7 = (bf16[128,7168]{1,0:T(8,128)(2,1)}, bf16[128,7168]{1,0:T(8,128)(2,1)S(1)}, u32[]{:S(2)}, u32[]{:S(2)}) collective-permute-start(bf16[128,7168]{1,0:T(8,128)(2,1)} %bitcast.13), channel_id=1, source_target_pairs={{0,16},{16,0},{32,48},{48,32},{64,80},{80,64},{96,112},{112,96},{1... | collective-permute-start | bytes 5505032 | tf_op jit(solution)/shard_map/ppermute | solution.py:17
  40.9 6.2 %collective-permute-start.3 = (bf16[16,7168]{1,0:T(8,128)(2,1)S(1)}, bf16[16,7168]{1,0:T(8,128)(2,1)S(1)}, u32[]{:S(2)}, u32[]{:S(2)}) collective-permute-start(bf16[16,7168]{1,0:T(8,128)(2,1)S(1)} %pad_maximum_fusion.4), channel_id=1, source_target_pairs={{0,64},{16,208},{32,96},{48,240},{64,0},{80,144},{96,32},{112,176}... | collective-permute-start | bytes 688136 | tf_op jit(solution)/shard_map/ppermute | solution.py:36
  43.9 11.1 %copy-start.2 = (bf16[1,7168,128]{2,1,0:T(8,128)(2,1)S(1)}, bf16[1,7168,128]{2,1,0:T(8,128)(2,1)}, u32[]{:S(2)}) copy-start(bf16[1,7168,128]{2,1,0:T(8,128)(2,1)} %param.12) | copy-start | bytes 5505028
  43.9 11.1 %copy-start.3 = (bf16[1,128,7168]{2,1,0:T(8,128)(2,1)S(1)}, bf16[1,128,7168]{2,1,0:T(8,128)(2,1)}, u32[]{:S(2)}) copy-start(bf16[1,128,7168]{2,1,0:T(8,128)(2,1)} %param.13) | copy-start | bytes 5505028
  43.9 6.2 %collective-permute-start.19 = (bf16[16,7168]{1,0:T(8,128)(2,1)S(1)}, bf16[16,7168]{1,0:T(8,128)(2,1)S(1)}, u32[]{:S(2)}, u32[]{:S(2)}) collective-permute-start(bf16[16,7168]{1,0:T(8,128)(2,1)S(1)} %pad_maximum_fusion.6), channel_id=1, source_target_pairs={{0,64},{16,208},{32,96},{48,240},{64,0},{80,144},{96,32},{112,176}... | collective-permute-start | bytes 688136 | tf_op jit(solution)/shard_map/ppermute | solution.py:36
  47.1 7.8 %collective-permute-start.4 = (bf16[32,7168]{1,0:T(8,128)(2,1)S(1)}, bf16[32,7168]{1,0:T(8,128)(2,1)S(1)}, u32[]{:S(2)}, u32[]{:S(2)}) collective-permute-start(bf16[32,7168]{1,0:T(8,128)(2,1)S(1)} %pad_maximum_fusion.2), channel_id=1, source_target_pairs={{0,192},{16,80},{32,224},{48,112},{64,128},{80,16},{96,160},{112,4... | collective-permute-start | bytes 1376264 | tf_op jit(solution)/shard_map/ppermute | solution.py:36
  50.1 9.6 %collective-permute-start.20 = (bf16[32,7168]{1,0:T(8,128)(2,1)S(1)}, bf16[32,7168]{1,0:T(8,128)(2,1)S(1)}, u32[]{:S(2)}, u32[]{:S(2)}) collective-permute-start(bf16[32,7168]{1,0:T(8,128)(2,1)S(1)} %pad_maximum_fusion.3), channel_id=1, source_target_pairs={{0,192},{16,80},{32,224},{48,112},{64,128},{80,16},{96,160},{112,4... | collective-permute-start | bytes 1376264 | tf_op jit(solution)/shard_map/ppermute | solution.py:36
  58.7 8.6 %collective-permute-start.8 = (bf16[32,7168]{1,0:T(8,128)(2,1)S(1)}, bf16[32,7168]{1,0:T(8,128)(2,1)S(1)}, u32[]{:S(2)}, u32[]{:S(2)}) collective-permute-start(bf16[32,7168]{1,0:T(8,128)(2,1)S(1)} %get-tuple-element.26), channel_id=1, source_target_pairs={{0,192},{16,80},{32,224},{48,112},{64,128},{80,16},{96,160},{112,4... | collective-permute-start | bytes 1376264 | tf_op jit(solution)/shard_map/ppermute | solution.py:36
  66.4 7.8 %collective-permute-start.21 = (bf16[32,7168]{1,0:T(8,128)(2,1)S(1)}, bf16[32,7168]{1,0:T(8,128)(2,1)S(1)}, u32[]{:S(2)}, u32[]{:S(2)}) collective-permute-start(bf16[32,7168]{1,0:T(8,128)(2,1)S(1)} %get-tuple-element.33), channel_id=1, source_target_pairs={{0,192},{16,80},{32,224},{48,112},{64,128},{80,16},{96,160},{112,4... | collective-permute-start | bytes 1376264 | tf_op jit(solution)/shard_map/ppermute | solution.py:36
  67.4 7.3 %collective-permute-start.9 = (bf16[16,7168]{1,0:T(8,128)(2,1)S(1)}, bf16[16,7168]{1,0:T(8,128)(2,1)S(1)}, u32[]{:S(2)}, u32[]{:S(2)}) collective-permute-start(bf16[16,7168]{1,0:T(8,128)(2,1)S(1)} %slice.33), channel_id=1, source_target_pairs={{0,64},{16,208},{32,96},{48,240},{64,0},{80,144},{96,32},{112,176}... | collective-permute-start | bytes 688136 | tf_op jit(solution)/shard_map/ppermute | solution.py:36
  74.4 7.0 %collective-permute-start.22 = (bf16[16,7168]{1,0:T(8,128)(2,1)S(1)}, bf16[16,7168]{1,0:T(8,128)(2,1)S(1)}, u32[]{:S(2)}, u32[]{:S(2)}) collective-permute-start(bf16[16,7168]{1,0:T(8,128)(2,1)S(1)} %slice.37), channel_id=1, source_target_pairs={{0,64},{16,208},{32,96},{48,240},{64,0},{80,144},{96,32},{112,176}... | collective-permute-start | bytes 688136 | tf_op jit(solution)/shard_map/ppermute | solution.py:36
  74.8 8.4 %collective-permute-start.10 = (bf16[8,7168]{1,0:T(8,128)(2,1)S(1)}, bf16[8,7168]{1,0:T(8,128)(2,1)S(1)}, u32[]{:S(2)}, u32[]{:S(2)}) collective-permute-start(bf16[8,7168]{1,0:T(8,128)(2,1)S(1)} %slice.35), channel_id=1, source_target_pairs={{0,32},{16,48},{32,0},{48,16},{64,96},{80,112},{96,64},{112,80},{1... | collective-permute-start | bytes 344072 | tf_op jit(solution)/shard_map/ppermute | solution.py:17
  81.4 10.3 %collective-permute-start.23 = (bf16[8,7168]{1,0:T(8,128)(2,1)S(1)}, bf16[8,7168]{1,0:T(8,128)(2,1)S(1)}, u32[]{:S(2)}, u32[]{:S(2)}) collective-permute-start(bf16[8,7168]{1,0:T(8,128)(2,1)S(1)} %slice.39), channel_id=1, source_target_pairs={{0,32},{16,48},{32,0},{48,16},{64,96},{80,112},{96,64},{112,80},{1... | collective-permute-start | bytes 344072 | tf_op jit(solution)/shard_map/ppermute | solution.py:17
  83.2 13.4 %collective-permute-start.12 = (bf16[8,7168]{1,0:T(8,128)(2,1)S(1)}, bf16[8,7168]{1,0:T(8,128)(2,1)S(1)}, u32[]{:S(2)}, u32[]{:S(2)}) collective-permute-start(bf16[8,7168]{1,0:T(8,128)(2,1)S(1)} %add_convert_fusion.5), channel_id=1, source_target_pairs={{0,32},{1,33},{2,34},{3,35},{4,36},{5,37},{6,38},{7,39},{8,40},{9,... | collective-permute-start | bytes 344072 | tf_op jit(solution)/shard_map/ppermute | solution.py:28
  87.4 12.2 %collective-permute-start.11 = (bf16[8,7168]{1,0:T(8,128)(2,1)S(1)}, bf16[8,7168]{1,0:T(8,128)(2,1)S(1)}, u32[]{:S(2)}, u32[]{:S(2)}) collective-permute-start(bf16[8,7168]{1,0:T(8,128)(2,1)S(1)} %add_convert_fusion.5), channel_id=1, source_target_pairs={{0,0},{1,1},{2,2},{3,3},{4,4},{5,5},{6,6},{7,7},{8,8},{9,9},{10,10... | collective-permute-start | bytes 344072 | tf_op jit(solution)/shard_map/ppermute | solution.py:28
  91.8 16.5 %collective-permute-start.25 = (bf16[8,7168]{1,0:T(8,128)(2,1)S(1)}, bf16[8,7168]{1,0:T(8,128)(2,1)S(1)}, u32[]{:S(2)}, u32[]{:S(2)}) collective-permute-start(bf16[8,7168]{1,0:T(8,128)(2,1)S(1)} %add_convert_fusion.4), channel_id=1, source_target_pairs={{0,32},{1,33},{2,34},{3,35},{4,36},{5,37},{6,38},{7,39},{8,40},{9,... | collective-permute-start | bytes 344072 | tf_op jit(solution)/shard_map/ppermute | solution.py:28
  93.5 9.8 %collective-permute-start.24 = (bf16[8,7168]{1,0:T(8,128)(2,1)S(1)}, bf16[8,7168]{1,0:T(8,128)(2,1)S(1)}, u32[]{:S(2)}, u32[]{:S(2)}) collective-permute-start(bf16[8,7168]{1,0:T(8,128)(2,1)S(1)} %add_convert_fusion.4), channel_id=1, source_target_pairs={{0,0},{1,1},{2,2},{3,3},{4,4},{5,5},{6,6},{7,7},{8,8},{9,9},{10,10... | collective-permute-start | bytes 344072 | tf_op jit(solution)/shard_map/ppermute | solution.py:28
  99.6 13.8 %collective-permute-start.13 = (bf16[16,7168]{1,0:T(8,128)(2,1)S(1)}, bf16[16,7168]{1,0:T(8,128)(2,1)S(1)}, u32[]{:S(2)}, u32[]{:S(2)}) collective-permute-start(bf16[16,7168]{1,0:T(8,128)(2,1)S(1)} %pad_maximum_fusion.5), channel_id=1, source_target_pairs={{0,64},{16,208},{32,96},{48,240},{64,0},{80,144},{96,32},{112,176}... | collective-permute-start | bytes 688136 | tf_op jit(solution)/shard_map/ppermute | solution.py:36
  108.3 8.8 %collective-permute-start.26 = (bf16[16,7168]{1,0:T(8,128)(2,1)S(1)}, bf16[16,7168]{1,0:T(8,128)(2,1)S(1)}, u32[]{:S(2)}, u32[]{:S(2)}) collective-permute-start(bf16[16,7168]{1,0:T(8,128)(2,1)S(1)} %constant_dynamic-update-slice_fusion.3.a), channel_id=1, source_target_pairs={{0,64},{16,208},{32,96},{48,240},{64,0},{80,144},{96,32},{112,176}... | collective-permute-start | bytes 688136 | tf_op jit(solution)/shard_map/ppermute | solution.py:36
  113.4 17.0 %collective-permute-start.14 = (bf16[32,7168]{1,0:T(8,128)(2,1)S(1)}, bf16[32,7168]{1,0:T(8,128)(2,1)S(1)}, u32[]{:S(2)}, u32[]{:S(2)}) collective-permute-start(bf16[32,7168]{1,0:T(8,128)(2,1)S(1)} %constant_dynamic-update-slice_fusion.refs_2_), channel_id=1, source_target_pairs={{0,192},{16,80},{32,224},{48,112},{64,128},{80,16},{96,160},{112,4... | collective-permute-start | bytes 1376264 | tf_op jit(solution)/shard_map/ppermute | solution.py:36
  117.1 13.9 %collective-permute-start.27 = (bf16[32,7168]{1,0:T(8,128)(2,1)S(1)}, bf16[32,7168]{1,0:T(8,128)(2,1)S(1)}, u32[]{:S(2)}, u32[]{:S(2)}) collective-permute-start(bf16[32,7168]{1,0:T(8,128)(2,1)S(1)} %join.1.refs_1_), channel_id=1, source_target_pairs={{0,192},{16,80},{32,224},{48,112},{64,128},{80,16},{96,160},{112,4... | collective-permute-start | bytes 1376264 | tf_op jit(solution)/shard_map/ppermute | solution.py:36
  118.9 23.5 %collective-permute-start.15 = (bf16[32,7168]{1,0:T(8,128)(2,1)S(1)}, bf16[32,7168]{1,0:T(8,128)(2,1)S(1)}, u32[]{:S(2)}, u32[]{:S(2)}) collective-permute-start(bf16[32,7168]{1,0:T(8,128)(2,1)S(1)} %constant_dynamic-update-slice_fusion.refs_2_), channel_id=1, source_target_pairs={{0,16},{16,0},{32,48},{48,32},{64,80},{80,64},{96,112},{112,96},{1... | collective-permute-start | bytes 1376264 | tf_op jit(solution)/shard_map/ppermute | solution.py:17
  130.5 11.9 %collective-permute-start.16 = (bf16[32,7168]{1,0:T(8,128)(2,1)S(1)}, bf16[32,7168]{1,0:T(8,128)(2,1)S(1)}, u32[]{:S(2)}, u32[]{:S(2)}) collective-permute-start(bf16[32,7168]{1,0:T(8,128)(2,1)S(1)} %collective-permute-done.14.refs_3_), channel_id=1, source_target_pairs={{0,16},{16,0},{32,48},{48,32},{64,80},{80,64},{96,112},{112,96},{1... | collective-permute-start | bytes 1376264 | tf_op jit(solution)/shard_map/ppermute | solution.py:17
  130.5 19.9 %collective-permute-start.28 = (bf16[32,7168]{1,0:T(8,128)(2,1)S(1)}, bf16[32,7168]{1,0:T(8,128)(2,1)S(1)}, u32[]{:S(2)}, u32[]{:S(2)}) collective-permute-start(bf16[32,7168]{1,0:T(8,128)(2,1)S(1)} %join.1.refs_1_), channel_id=1, source_target_pairs={{0,16},{16,0},{32,48},{48,32},{64,80},{80,64},{96,112},{112,96},{1... | collective-permute-start | bytes 1376264 | tf_op jit(solution)/shard_map/ppermute | solution.py:17
  131.0 19.4 %collective-permute-start.29 = (bf16[32,7168]{1,0:T(8,128)(2,1)S(1)}, bf16[32,7168]{1,0:T(8,128)(2,1)S(1)}, u32[]{:S(2)}, u32[]{:S(2)}) collective-permute-start(bf16[32,7168]{1,0:T(8,128)(2,1)S(1)} %collective-permute-done.27.refs_2_), channel_id=1, source_target_pairs={{0,16},{16,0},{32,48},{48,32},{64,80},{80,64},{96,112},{112,96},{1... | collective-permute-start | bytes 1376264 | tf_op jit(solution)/shard_map/ppermute | solution.py:17
  136.9 11.7 %collective-permute-start.30 = (bf16[448,256]{1,0:T(8,128)(2,1)}, bf16[448,256]{1,0:T(8,128)(2,1)S(1)}, u32[]{:S(2)}, u32[]{:S(2)}) collective-permute-start(bf16[448,256]{1,0:T(8,128)(2,1)} %reduce-scatter.2.cloned.1.call-done._.share_ref), channel_id=1, source_target_pairs={{0,240},{16,224},{32,208},{48,192},{64,176},{80,160},{96,144},{112... | collective-permute-start | bytes 688136 | tf_op jit(solution)/shard_map/ppermute | solution.py:374
Sparse Core Ops, SparseCore 0:
  40.3 64.7 reduce-scatter.1

commit v4 on v3

--- a/solution.py
+++ b/solution.py
@@ -18,13 +18,11 @@
 
 
 def delta(p, k):
-    return (p & 1) * 8 + (k ^ ((p >> 1) & 1)) * 4 + (p >> 2)
-
-
-def shifted(value, k, mask=0):
-    pairs = [
-        (p * 16 + e, (p ^ mask) * 16 + (e ^ delta(p, k))) for p in range(16) for e in range(16)
-    ]
+    return (p & 1) * 8 + (k ^ ((p ^ (p >> 1)) & 1)) * 4 + (p >> 2)
+
+
+def shifted(value, k):
+    pairs = [(p * 16 + e, p * 16 + (e ^ delta(p, k))) for p in range(16) for e in range(16)]
     return lax.ppermute(value, ("pipe", "expert"), pairs)
 
 
@@ -46,15 +44,18 @@
     return (a.astype(F32) + b.astype(F32)).astype(BF)
 
 
-def collect(kept, sent, after=None):
+def collect(kept, sent, after=None, last=None):
     two = add(kept, along_x(sent, 1))
     size = two.shape[0] // 2
     one = add(two[:size], along_x(two[size:], 0))
     full = add(one[:SLOT], across(one[SLOT:], Y_HI))
-    block = jnp.concatenate([shifted(full, 0), shifted(full, 0, Y_HI)], axis=0)
+    chunk = shifted(full, 0)
+    block = jnp.concatenate([chunk, across(chunk, Y_HI)], axis=0)
     two = block, along_x(block, 0)
     two = jnp.concatenate(two, axis=0) if after is None else join(*two, after)
     rest = along_x(two, 1)
+    if last is not None:
+        rest = later(rest, last)
     return two, rest, across(two, CORE), across(rest, CORE)
 
 
@@ -85,8 +86,7 @@
     ring = (row >> 4) & 3
     off = ring ^ (ring >> 1)
     off = off ^ (2 * (off & 1) * ((p & 1) ^ far_core))
-    base = s ^ ((p & 1) * 8 + ((p >> 1) & 1) * 4 + (p >> 2))
-    expert = base ^ (far_core * 8) ^ (k * 4) ^ off
+    expert = s ^ delta(p, 0) ^ (far_core * 12) ^ (k * 4) ^ off
     named = jnp.zeros((rows, tok), F32)
     gate = jnp.zeros((rows, tok), F32)
     for choice in range(ids.shape[0]):
@@ -103,8 +103,8 @@
 
 
 def select_kernel(
-    p_ref, s_ref, ids_ref, gates_ref, tok_ref, grad_ref, lat_ref,
-    send0, send1, dsend0, dsend1, mine_ref, other_ref, pick, weight,
+    p_ref, s_ref, ids_ref, gates_ref, tok_ref, grad_ref,
+    send0, send1, dsend0, dsend1, pick, weight,
 ):
     @pl.when(pl.program_id(0) == 0)
     def _():
@@ -113,12 +113,6 @@
         pick[...] = sel.astype(BF)
         total = jnp.sum(mix, axis=1, keepdims=True)
         weight[...] = jnp.broadcast_to(total, weight.shape)
-        lat = lat_ref[0]
-        width = lat.shape[1] // 2
-        low = p < 8
-        mine_ref[...] = jnp.where(low, lat[:, :width], lat[:, width:])
-        other_ref[...] = jnp.where(low, lat[:, width:], lat[:, :width])
-
     rows = dot(pick[...], tok_ref[...]).astype(BF)
     drows = (dot(pick[...], grad_ref[...]) * weight[:, :1]).astype(BF)
     send0[...] = rows[:SLOT]
@@ -134,13 +128,11 @@
 SCALAR = pl.BlockSpec(memory_space=pltpu.SMEM)
 
 
-def select(p, s, ids, gates, tokens, grads, latent):
+def select(p, s, ids, gates, tokens, grads):
     tok, d = tokens.shape
     wide = d // STEPS
-    width = latent.shape[2] // 2
     col = lambda rows: pl.BlockSpec((rows, wide), lambda i: (0, i))
     chunk = jax.ShapeDtypeStruct((SLOT, d), BF)
-    half = jax.ShapeDtypeStruct((tok, width), BF)
     return pl.pallas_call(
         select_kernel,
         grid=(STEPS,),
@@ -151,19 +143,18 @@
             whole(gates.shape),
             col(tok),
             col(tok),
-            whole(latent.shape),
         ],
-        out_specs=[col(SLOT)] * 4 + [whole((tok, width))] * 2,
-        out_shape=[chunk] * 4 + [half] * 2,
+        out_specs=[col(SLOT)] * 4,
+        out_shape=[chunk] * 4,
         scratch_shapes=[pltpu.VMEM((2 * SLOT, tok), BF), pltpu.VMEM((2 * SLOT, tok), F32)],
         cost_estimate=cost(4 * 2 * SLOT * tok * d, 4 * tok * d),
         compiler_params=pltpu.CompilerParams(vmem_limit_bytes=16 << 20),
         name="select",
-    )(p, s, ids, gates, far(tokens), far(grads), far(latent))
+    )(p, s, ids, gates, far(tokens), far(grads))
 
 
 def latent_kernel(
-    p_ref, s_ref, ids_ref, gates_ref, mine_ref, got_ref, tok_ref,
+    p_ref, s_ref, ids_ref, gates_ref, lat_ref, got_ref, tok_ref,
     out_ref, sel_ref, hi_ref, lo_ref, turned,
 ):
     i = pl.program_id(0)
@@ -177,15 +168,17 @@
         hi = mix.astype(BF)
         hi_ref[...] = hi
         lo_ref[...] = (mix - hi.astype(F32)).astype(BF)
-        turned[...] = (mine_ref[...].astype(F32) + got_ref[...].astype(F32)).astype(BF)
+        width = got_ref.shape[1]
+        mine = jnp.where(p_ref[0] < 8, lat_ref[0, :, :width], lat_ref[0, :, width:])
+        turned[...] = (mine.astype(F32) + got_ref[...].astype(F32)).astype(BF)
 
     part = lax.dot_general(tok_ref[...], turned[...], (((0,), (0,)), ((), ())), preferred_element_type=F32)
     out_ref[...] = part.astype(BF)
 
 
-def latent_part(p, s, ids, gates, mine, got, tokens):
+def latent_part(p, s, ids, gates, latent, got, tokens):
     tok, d = tokens.shape
-    width = mine.shape[1]
+    width = got.shape[1]
     n = 16
     group = 4
     table = jax.ShapeDtypeStruct((tok, tok), BF)
@@ -197,7 +190,7 @@
             SCALAR,
             whole(ids.shape),
             whole(gates.shape),
-            whole(mine.shape),
+            whole(latent.shape),
             whole(got.shape),
             pl.BlockSpec((tok, d // n * group), lambda i: (0, i)),
         ],
@@ -208,7 +201,7 @@
         cost_estimate=cost(2 * tok * d * width, 2 * tok * d + 2 * d * width),
         compiler_params=pltpu.CompilerParams(vmem_limit_bytes=16 << 20),
         name="latent_part",
-    )(p, s, ids, gates, mine, got, tokens)
+    )(p, s, ids, gates, latent, got, tokens)
 
 
 def finish_kernel(p_ref, share_ref, theirs_ref, out_ref):
@@ -236,6 +229,23 @@
     size = a.shape[0]
     out[:size] = a[...]
     out[size:] = b[...]
+
+
+def pass_kernel(a, _, out):
+    out[...] = a[...]
+
+
+def later(a, after):
+    vmem = pl.BlockSpec(memory_space=pltpu.VMEM)
+    return pl.pallas_call(
+        pass_kernel,
+        in_specs=[vmem, pl.BlockSpec(memory_space=pl.ANY)],
+        out_specs=vmem,
+        out_shape=pltpu.VMEM(a.shape, a.dtype),
+        cost_estimate=cost(0, 4 * a.size),
+        compiler_params=pltpu.CompilerParams(vmem_limit_bytes=8 << 20),
+        name="later",
+    )(near(a), after)
 
 
 def join(a, b, after):
@@ -365,11 +375,13 @@
     wg2, wu2, wd2 = across(wg, CORE), across(wu, CORE), across(wd, CORE)
     mirror = [(i, 15 - i) for i in range(16)]
 
-    send0, send1, dsend0, dsend1, mine, other = select(
-        p, s, ids, gates, tokens, out_grad, latent_grad
-    )
+    send0, send1, dsend0, dsend1 = select(p, s, ids, gates, tokens, out_grad)
+    latent = latent_grad[0]
+    width = latent.shape[1] // 2
+    other = jnp.where(p[0] < 8, latent[:, width:], latent[:, :width])
     got = lax.ppermute(other, "pipe", mirror)
-    part, sel, hi, lo = latent_part(p, s, ids, gates, mine, got, tokens)
+    send0 = later(send0, got)
+    part, sel, hi, lo = latent_part(p, s, ids, gates, latent_grad, got, tokens)
     share = lax.psum_scatter(part, "expert", scatter_dimension=0, tiled=True)
     theirs = lax.ppermute(share, "pipe", mirror)
     kv_grad = finish(p, share, theirs)
@@ -379,7 +391,7 @@
     kept, sent, fa, fb = forward(rows, wg, wu, wg2, wu2, wd, wd2, hi)
     routed = combine([hi, lo], collect(kept, sent))
     dkept, dsent = backward(drows, fa, fb, wd, wd2, wg, wu, wg2, wu2)
-    token_grad = combine([sel], collect(dkept, dsent, share))
+    token_grad = combine([sel], collect(dkept, dsent, share, theirs))
     return routed, token_grad, kv_grad
 
 

time: 159 us -> 153 us (0.962)
  starting transfers between devices: 74.7 us -> 53.8 us
  waiting for transfers between devices: 44.9 us -> 58.6 us
    ppermute x9 -> x11, starting transfers between devices: 22.7 us -> 2.85 us  [across(): return lax.ppermute(value, 'pipe', [(i, i ^ mask) for i in range(16)])]
    ppermute x8 -> x6, starting transfers between devices: 29.7 us -> 23 us  [shifted(): return lax.ppermute(value, ('pipe', 'expert'), pairs)]
    ppermute x9 -> x11, waiting for transfers between devices: 2.47 us -> 8.99 us  [across(): return lax.ppermute(value, 'pipe', [(i, i ^ mask) for i in range(16)])]
    ppermute x1, waiting for transfers between devices: 4.42 us -> 10.6 us  [per_device(): theirs = lax.ppermute(share, 'pipe', mirror)]
    ppermute x12, waiting for transfers between devices: 23.7 us -> 28.4 us  [along_x(): return lax.ppermute(value, 'pipe', pairs)]
    ppermute x8 -> x6, waiting for transfers between devices: 14.3 us -> 10.6 us  [shifted(): return lax.ppermute(value, ('pipe', 'expert'), pairs)]
    ppermute x1, starting transfers between devices: 5.42 us -> 8.77 us  [per_device(): theirs = lax.ppermute(share, 'pipe', mirror)]
  transfers between devices with their start and end apart: 32 -> 32, of which waited for: 13 -> 15; matrix products, arithmetic and copies ran while one was open for 0% -> 0% of each run, Pallas kernels for 11% -> 13%
where the time goes in v4:
time: 153 us; the launch traced here: 152 us
  waiting for transfers between devices  58.6 us (38%)
  starting transfers between devices  53.8 us (35%)
  Pallas kernels  21.6 us (14%)
  between operations  14.5 us (9%)
  local copies, waits for them, and re-layouts  2.44 us (2%)
    ppermute x12, waiting for transfers between devices, along_x(): return lax.ppermute(value, 'pipe', pairs)  28.4 us
    ppermute x6, starting transfers between devices, shifted(): return lax.ppermute(value, ('pipe', 'expert'), pairs)  23 us
    ppermute x12, starting transfers between devices, along_x(): return lax.ppermute(value, 'pipe', pairs)  12.6 us
    ppermute x6, waiting for transfers between devices, shifted(): return lax.ppermute(value, ('pipe', 'expert'), pairs)  10.6 us
    ppermute x1, waiting for transfers between devices, per_device(): theirs = lax.ppermute(share, 'pipe', mirror)  10.6 us
    ppermute x11, waiting for transfers between devices, across(): return lax.ppermute(value, 'pipe', [(i, i ^ mask) for i in range(16)])  8.99 us
    ppermute x1, starting transfers between devices, per_device(): theirs = lax.ppermute(share, 'pipe', mirror)  8.77 us
    pallas_call x1, Pallas kernels, backward(): pl.pallas_call(backward_kernel, in_specs=[vmem] * 9, out_specs=[vmem] * 2...  6.62 us
  transfers between devices with their start and end apart: 32, of which 15 were waited for; matrix products, arithmetic and copies ran while one was open for 0% of the time, Pallas kernels for 13%

profile of v4, /device:TPU:1, one launch (start us, length us, event | category | flops | bytes accessed | tf_op | source)
XLA Modules:
  0.0 152.4 jit_solution(6853100912184594267)
XLA Ops:
  7.2 0.0 reduce-scatter.2.cloned.1.call-start
  7.2 0.9 slice_select_fusion
  8.1 6.6 %collective-permute-start = (bf16[128,256]{1,0:T(8,128)(2,1)S(1)}, bf16[128,256]{1,0:T(8,128)(2,1)S(1)}, u32[]{:S(2)}, u32[]{:S(2)}) collective-permute-start(bf16[128,256]{1,0:T(8,128)(2,1)S(1)} %slice_select_fusion), channel_id=1, source_target_pairs={{0,240},{16,224},{32,208},{48,192},{64,176},{80,160},{96,144},{112... | collective-permute-start | bytes 196616 | tf_op jit(solution)/shard_map/ppermute | solution.py:382
  14.7 0.7 copy-done.7
  15.4 0.7 copy-done.8
  16.1 3.5 %select.1 = (bf16[8,7168]{1,0:T(8,128)(2,1)S(1)}, bf16[8,7168]{1,0:T(8,128)(2,1)S(1)}, bf16[8,7168]{1,0:T(8,128)(2,1)S(1)}, bf16[8,7168]{1,0:T(8,128)(2,1)S(1)}) custom-call(s32[1]{0:T(128)} %bitcast.p_ref, s32[1]{0:T(128)} %bitcast.1.s_ref, s32[8,128]{1,0:T(8,128)S(1)} %bitcast.18, f32[8,128]{1,0:T(8,128)S(1)} %bitcast.20, bf16[128,7168]{1,0:T(8,128)(2,1)} %tok_ref.3, ...), custom_call_target="tpu_custom_call" | custom-call | flops 58720256 | bytes 3670016 | tf_op jit(solution)/shard_map/select/pallas_call | solution.py:136
  19.6 2.3 %collective-permute-start.2 = (bf16[8,7168]{1,0:T(8,128)(2,1)S(1)}, bf16[8,7168]{1,0:T(8,128)(2,1)S(1)}, u32[]{:S(2)}, u32[]{:S(2)}) collective-permute-start(bf16[8,7168]{1,0:T(8,128)(2,1)S(1)} %get-tuple-element.20), channel_id=1, source_target_pairs={{0,4},{1,5},{2,6},{3,7},{4,0},{5,1},{6,2},{7,3},{8,12},{9,13},{10,... | collective-permute-start | bytes 344072 | tf_op jit(solution)/shard_map/ppermute | solution.py:26
  21.9 9.6 %collective-permute-start.1 = (bf16[8,7168]{1,0:T(8,128)(2,1)S(1)}, bf16[8,7168]{1,0:T(8,128)(2,1)S(1)}, u32[]{:S(2)}, u32[]{:S(2)}) collective-permute-start(bf16[8,7168]{1,0:T(8,128)(2,1)S(1)} %later.2), channel_id=1, source_target_pairs={{0,0},{1,1},{2,2},{3,3},{4,4},{5,5},{6,6},{7,7},{8,8},{9,9},{10,10... | collective-permute-start | bytes 344072 | tf_op jit(solution)/shard_map/ppermute | solution.py:26
  31.5 1.9 %collective-permute-start.17 = (bf16[8,7168]{1,0:T(8,128)(2,1)S(1)}, bf16[8,7168]{1,0:T(8,128)(2,1)S(1)}, u32[]{:S(2)}, u32[]{:S(2)}) collective-permute-start(bf16[8,7168]{1,0:T(8,128)(2,1)S(1)} %get-tuple-element.24), channel_id=1, source_target_pairs={{0,0},{1,1},{2,2},{3,3},{4,4},{5,5},{6,6},{7,7},{8,8},{9,9},{10,10... | collective-permute-start | bytes 344072 | tf_op jit(solution)/shard_map/ppermute | solution.py:26
  33.4 2.3 %collective-permute-start.18 = (bf16[8,7168]{1,0:T(8,128)(2,1)S(1)}, bf16[8,7168]{1,0:T(8,128)(2,1)S(1)}, u32[]{:S(2)}, u32[]{:S(2)}) collective-permute-start(bf16[8,7168]{1,0:T(8,128)(2,1)S(1)} %get-tuple-element.25), channel_id=1, source_target_pairs={{0,4},{1,5},{2,6},{3,7},{4,0},{5,1},{6,2},{7,3},{8,12},{9,13},{10,... | collective-permute-start | bytes 344072 | tf_op jit(solution)/shard_map/ppermute | solution.py:26
  35.8 0.1 collective-permute-start.5
  35.9 3.6 %latent_part.1 = (bf16[7168,256]{1,0:T(8,128)(2,1)}, bf16[128,128]{1,0:T(8,128)(2,1)S(1)}, bf16[128,128]{1,0:T(8,128)(2,1)S(1)}, bf16[128,128]{1,0:T(8,128)(2,1)S(1)}) custom-call(s32[1]{0:T(128)} %bitcast.p_ref, s32[1]{0:T(128)} %bitcast.1.s_ref, s32[8,128]{1,0:T(8,128)S(1)} %bitcast.19, f32[8,128]{1,0:T(8,128)S(1)} %bitcast.21, ...), custom_call_target="tpu_custom_call" | custom-call | flops 469762048 | bytes 5505024 | tf_op jit(solution)/shard_map/latent_part/pallas_call | solution.py:185
  39.5 0.0 reduce-scatter.2.cloned.1.call-update
  39.5 0.5 collective-permute-start.6
  40.1 0.1 collective-permute-start.7
  40.2 1.7 %collective-permute-done.17 = bf16[8,7168]{1,0:T(8,128)(2,1)S(1)} collective-permute-done((bf16[8,7168]{1,0:T(8,128)(2,1)S(1)}, bf16[8,7168]{1,0:T(8,128)(2,1)S(1)}, u32[]{:S(2)}, u32[]{:S(2)}) %collective-permute-start.17) | collective-permute-done | bytes 114720 | tf_op jit(solution)/shard_map/ppermute | solution.py:26
  41.9 0.0 copy-start.2
  42.0 0.0 copy-start.3
  42.0 2.8 %collective-permute-start.19 = (bf16[16,7168]{1,0:T(8,128)(2,1)S(1)}, bf16[16,7168]{1,0:T(8,128)(2,1)S(1)}, u32[]{:S(2)}, u32[]{:S(2)}) collective-permute-start(bf16[16,7168]{1,0:T(8,128)(2,1)S(1)} %pad_maximum_fusion.6), channel_id=1, source_target_pairs={{0,64},{16,208},{32,96},{48,240},{64,0},{80,144},{96,32},{112,176}... | collective-permute-start | bytes 688136 | tf_op jit(solution)/shard_map/ppermute | solution.py:34
  44.7 3.3 %collective-permute-done.3 = bf16[16,7168]{1,0:T(8,128)(2,1)S(1)} collective-permute-done((bf16[16,7168]{1,0:T(8,128)(2,1)S(1)}, bf16[16,7168]{1,0:T(8,128)(2,1)S(1)}, u32[]{:S(2)}, u32[]{:S(2)}) %collective-permute-start.3) | collective-permute-done | bytes 229408 | tf_op jit(solution)/shard_map/ppermute | solution.py:34
  48.0 0.1 collective-permute-start.4
  48.1 2.3 %collective-permute-done.19 = bf16[16,7168]{1,0:T(8,128)(2,1)S(1)} collective-permute-done((bf16[16,7168]{1,0:T(8,128)(2,1)S(1)}, bf16[16,7168]{1,0:T(8,128)(2,1)S(1)}, u32[]{:S(2)}, u32[]{:S(2)}) %collective-permute-start.19) | collective-permute-done | bytes 229408 | tf_op jit(solution)/shard_map/ppermute | solution.py:34
  50.5 0.1 collective-permute-start.20
  50.6 5.3 %collective-permute-done.4 = bf16[32,7168]{1,0:T(8,128)(2,1)S(1)} collective-permute-done((bf16[32,7168]{1,0:T(8,128)(2,1)S(1)}, bf16[32,7168]{1,0:T(8,128)(2,1)S(1)}, u32[]{:S(2)}, u32[]{:S(2)}) %collective-permute-start.4) | collective-permute-done | bytes 458784 | tf_op jit(solution)/shard_map/ppermute | solution.py:34
  55.9 0.1 pad_maximum_fusion.rows
  56.0 3.6 %forward.1 = (bf16[32,7168]{1,0:T(8,128)(2,1)S(1)}, bf16[32,7168]{1,0:T(8,128)(2,1)S(1)}, f32[64,256]{1,0:T(8,128)S(1)}, f32[64,256]{1,0:T(8,128)S(1)}) custom-call(bf16[64,7168]{1,0:T(8,128)(2,1)S(1)} %pad_maximum_fusion.rows, bf16[7168,128]{1,0:T(8,128)(2,1)S(1)} %bitcast.9, bf16[7168,128]{1,0:T(8,128)(2,1)S(1)} %bitcast.12, ...), custom_call_target="tpu_custom_call" | custom-call | flops 704643072 | bytes 12845056 | tf_op jit(solution)/shard_map/forward/pallas_call | solution.py:292
  59.6 0.1 collective-permute-start.8
  59.7 1.1 collective-permute-done.20
  60.8 0.1 pad_maximum_fusion.1.rows
  60.8 6.6 %backward.1 = (bf16[32,7168]{1,0:T(8,128)(2,1)S(1)}, bf16[32,7168]{1,0:T(8,128)(2,1)S(1)}) custom-call(bf16[64,7168]{1,0:T(8,128)(2,1)S(1)} %pad_maximum_fusion.1.rows, f32[64,256]{1,0:T(8,128)S(1)} %get-tuple-element.26.fa, f32[64,256]{1,0:T(8,128)S(1)} %get-tuple-element.27.fb, bf16[128,7168]{1,0:T(8,128)(2,1)S(1)} %bitcast.16, ...), custom_call_target="tpu_custom_call" | custom-call | flops 704643072 | bytes 12845056 | tf_op jit(solution)/shard_map/backward/pallas_call | solution.py:324
  67.5 0.5 collective-permute-start.21
  68.0 0.1 add_convert_fusion.1
  68.1 0.1 collective-permute-start.9
  68.2 8.4 %collective-permute-done.21 = bf16[32,7168]{1,0:T(8,128)(2,1)S(1)} collective-permute-done((bf16[32,7168]{1,0:T(8,128)(2,1)S(1)}, bf16[32,7168]{1,0:T(8,128)(2,1)S(1)}, u32[]{:S(2)}, u32[]{:S(2)}) %collective-permute-start.21) | collective-permute-done | bytes 458784 | tf_op jit(solution)/shard_map/ppermute | solution.py:34
  76.6 0.1 add_convert_fusion
  76.7 0.1 collective-permute-start.22
  76.8 0.1 add_convert_fusion.3
  76.9 0.5 collective-permute-start.10
  77.4 5.5 %collective-permute-done.22 = bf16[16,7168]{1,0:T(8,128)(2,1)S(1)} collective-permute-done((bf16[16,7168]{1,0:T(8,128)(2,1)S(1)}, bf16[16,7168]{1,0:T(8,128)(2,1)S(1)}, u32[]{:S(2)}, u32[]{:S(2)}) %collective-permute-start.22) | collective-permute-done | bytes 229408 | tf_op jit(solution)/shard_map/ppermute | solution.py:34
  82.9 0.1 add_convert_fusion.2
  83.0 0.1 collective-permute-start.23
  83.1 2.1 %collective-permute-done.10 = bf16[8,7168]{1,0:T(8,128)(2,1)S(1)} collective-permute-done((bf16[8,7168]{1,0:T(8,128)(2,1)S(1)}, bf16[8,7168]{1,0:T(8,128)(2,1)S(1)}, u32[]{:S(2)}, u32[]{:S(2)}) %collective-permute-start.10) | collective-permute-done | bytes 114720 | tf_op jit(solution)/shard_map/ppermute | solution.py:17
  85.2 4.5 %collective-permute-start.11 = (bf16[8,7168]{1,0:T(8,128)(2,1)S(1)}, bf16[8,7168]{1,0:T(8,128)(2,1)S(1)}, u32[]{:S(2)}, u32[]{:S(2)}) collective-permute-start(bf16[8,7168]{1,0:T(8,128)(2,1)S(1)} %add_convert_fusion.5), channel_id=1, source_target_pairs={{0,0},{1,1},{2,2},{3,3},{4,4},{5,5},{6,6},{7,7},{8,8},{9,9},{10,10... | collective-permute-start | bytes 344072 | tf_op jit(solution)/shard_map/ppermute | solution.py:26
  89.7 3.3 %collective-permute-done.23 = bf16[8,7168]{1,0:T(8,128)(2,1)S(1)} collective-permute-done((bf16[8,7168]{1,0:T(8,128)(2,1)S(1)}, bf16[8,7168]{1,0:T(8,128)(2,1)S(1)}, u32[]{:S(2)}, u32[]{:S(2)}) %collective-permute-start.23) | collective-permute-done | bytes 114720 | tf_op jit(solution)/shard_map/ppermute | solution.py:17
  93.0 2.3 %collective-permute-start.24 = (bf16[8,7168]{1,0:T(8,128)(2,1)S(1)}, bf16[8,7168]{1,0:T(8,128)(2,1)S(1)}, u32[]{:S(2)}, u32[]{:S(2)}) collective-permute-start(bf16[8,7168]{1,0:T(8,128)(2,1)S(1)} %add_convert_fusion.4), channel_id=1, source_target_pairs={{0,0},{1,1},{2,2},{3,3},{4,4},{5,5},{6,6},{7,7},{8,8},{9,9},{10,10... | collective-permute-start | bytes 344072 | tf_op jit(solution)/shard_map/ppermute | solution.py:26
  95.4 2.8 %collective-permute-done.11 = bf16[8,7168]{1,0:T(8,128)(2,1)S(1)} collective-permute-done((bf16[8,7168]{1,0:T(8,128)(2,1)S(1)}, bf16[8,7168]{1,0:T(8,128)(2,1)S(1)}, u32[]{:S(2)}, u32[]{:S(2)}) %collective-permute-start.11) | collective-permute-done | bytes 114720 | tf_op jit(solution)/shard_map/ppermute | solution.py:26
  98.2 0.9 collective-permute-start.12
  99.1 6.0 %collective-permute-done.24 = bf16[8,7168]{1,0:T(8,128)(2,1)S(1)} collective-permute-done((bf16[8,7168]{1,0:T(8,128)(2,1)S(1)}, bf16[8,7168]{1,0:T(8,128)(2,1)S(1)}, u32[]{:S(2)}, u32[]{:S(2)}) %collective-permute-start.24) | collective-permute-done | bytes 114720 | tf_op jit(solution)/shard_map/ppermute | solution.py:26
  105.1 1.2 collective-permute-done.12
  106.4 2.9 %collective-permute-start.13 = (bf16[16,7168]{1,0:T(8,128)(2,1)S(1)}, bf16[16,7168]{1,0:T(8,128)(2,1)S(1)}, u32[]{:S(2)}, u32[]{:S(2)}) collective-permute-start(bf16[16,7168]{1,0:T(8,128)(2,1)S(1)} %pad_maximum_fusion.5), channel_id=1, source_target_pairs={{0,64},{16,208},{32,96},{48,240},{64,0},{80,144},{96,32},{112,176}... | collective-permute-start | bytes 688136 | tf_op jit(solution)/shard_map/ppermute | solution.py:34
  109.3 2.4 %collective-permute-done.25 = bf16[8,7168]{1,0:T(8,128)(2,1)S(1)} collective-permute-done((bf16[8,7168]{1,0:T(8,128)(2,1)S(1)}, bf16[8,7168]{1,0:T(8,128)(2,1)S(1)}, u32[]{:S(2)}, u32[]{:S(2)}) %collective-permute-start.25) | collective-permute-done | bytes 114720 | tf_op jit(solution)/shard_map/ppermute | solution.py:17
  111.7 4.1 %collective-permute-start.26 = (bf16[16,7168]{1,0:T(8,128)(2,1)S(1)}, bf16[16,7168]{1,0:T(8,128)(2,1)S(1)}, u32[]{:S(2)}, u32[]{:S(2)}) collective-permute-start(bf16[16,7168]{1,0:T(8,128)(2,1)S(1)} %constant_dynamic-update-slice_fusion.3.a), channel_id=1, source_target_pairs={{0,64},{16,208},{32,96},{48,240},{64,0},{80,144},{96,32},{112,176}... | collective-permute-start | bytes 688136 | tf_op jit(solution)/shard_map/ppermute | solution.py:34
  115.9 0.8 collective-permute-start.14
  116.7 2.7 %collective-permute-done.26.b = bf16[16,7168]{1,0:T(8,128)(2,1)S(1)} collective-permute-done((bf16[16,7168]{1,0:T(8,128)(2,1)S(1)}, bf16[16,7168]{1,0:T(8,128)(2,1)S(1)}, u32[]{:S(2)}, u32[]{:S(2)}) %collective-permute-start.26) | collective-permute-done | bytes 229408 | tf_op jit(solution)/shard_map/ppermute | solution.py:34
  119.4 0.9 copy-done.4
  120.3 1.0 collective-permute-start.27
  121.3 8.8 %collective-permute-start.28 = (bf16[448,256]{1,0:T(8,128)(2,1)S(1)}, bf16[448,256]{1,0:T(8,128)(2,1)S(1)}, u32[]{:S(2)}, u32[]{:S(2)}) collective-permute-start(bf16[448,256]{1,0:T(8,128)(2,1)S(1)} %copy-done.4), channel_id=1, source_target_pairs={{0,240},{16,224},{32,208},{48,192},{64,176},{80,160},{96,144},{112... | collective-permute-start | bytes 688136 | tf_op jit(solution)/shard_map/ppermute | solution.py:386
  130.1 0.5 collective-permute-start.16
  130.6 0.0 collective-permute-start.29
  130.6 10.6 %collective-permute-done.28._.theirs_ref = bf16[448,256]{1,0:T(8,128)(2,1)S(1)} collective-permute-done((bf16[448,256]{1,0:T(8,128)(2,1)S(1)}, bf16[448,256]{1,0:T(8,128)(2,1)S(1)}, u32[]{:S(2)}, u32[]{:S(2)}) %collective-permute-start.28) | collective-permute-done | bytes 229408 | tf_op jit(solution)/shard_map/ppermute | solution.py:386
  141.2 0.1 collective-permute-start.30
  141.3 1.9 %combine.2 = bf16[128,7168]{1,0:T(8,128)(2,1)} custom-call(bf16[128,128]{1,0:T(8,128)(2,1)S(1)} %get-tuple-element.17._.refs_0_, bf16[128,128]{1,0:T(8,128)(2,1)S(1)} %get-tuple-element.18.refs_1_, bf16[32,7168]{1,0:T(8,128)(2,1)S(1)} %constant_dynamic-update-slice_fusion.refs_2_, bf16[32,7168]{1,0:T(8,128)(2,1)S(1)} %collective-permute-done.14.refs_3_, ...), custom_call_target="tpu_custom_call" | custom-call | flops 469762048 | bytes 3670016 | tf_op jit(solution)/shard_map/combine/pallas_call | solution.py:358
  143.2 0.8 finish.1
  144.0 1.5 combine.3
  (52 shorter events, 0.4 us)
Async XLA Ops:
  7.2 112.2 %reduce-scatter.2.cloned.1.call-start = ((), (), s32[]{:S(2)}) async-start(), calls=%async_computation.1 | async-start | bytes 3899392 | tf_op jit(solution)/shard_map/reduce_scatter | solution.py:385
  8.1 13.8 %collective-permute-start = (bf16[128,256]{1,0:T(8,128)(2,1)S(1)}, bf16[128,256]{1,0:T(8,128)(2,1)S(1)}, u32[]{:S(2)}, u32[]{:S(2)}) collective-permute-start(bf16[128,256]{1,0:T(8,128)(2,1)S(1)} %slice_select_fusion), channel_id=1, source_target_pairs={{0,240},{16,224},{32,208},{48,192},{64,176},{80,160},{96,144},{112... | collective-permute-start | bytes 196616 | tf_op jit(solution)/shard_map/ppermute | solution.py:382
  14.7 0.7 copy-start.7
  15.4 0.7 copy-start.8
  16.1 19.7 %copy-start.1 = (bf16[1,7168,128]{2,1,0:T(8,128)(2,1)S(1)}, bf16[1,7168,128]{2,1,0:T(8,128)(2,1)}, u32[]{:S(2)}) copy-start(bf16[1,7168,128]{2,1,0:T(8,128)(2,1)} %param.11) | copy-start | bytes 5505028
  16.1 19.8 %copy-start = (bf16[128,7168]{1,0:T(8,128)(2,1)S(1)}, bf16[128,7168]{1,0:T(8,128)(2,1)}, u32[]{:S(2)}) copy-start(bf16[128,7168]{1,0:T(8,128)(2,1)} %tok_ref.3) | copy-start | bytes 5505028
  16.1 19.8 %copy-start.6 = (bf16[1,128,512]{2,1,0:T(8,128)(2,1)S(1)}, bf16[1,128,512]{2,1,0:T(8,128)(2,1)}, u32[]{:S(2)}) copy-start(bf16[1,128,512]{2,1,0:T(8,128)(2,1)} %lat_ref.1) | copy-start | bytes 393220
  19.6 20.0 %collective-permute-start.2 = (bf16[8,7168]{1,0:T(8,128)(2,1)S(1)}, bf16[8,7168]{1,0:T(8,128)(2,1)S(1)}, u32[]{:S(2)}, u32[]{:S(2)}) collective-permute-start(bf16[8,7168]{1,0:T(8,128)(2,1)S(1)} %get-tuple-element.20), channel_id=1, source_target_pairs={{0,4},{1,5},{2,6},{3,7},{4,0},{5,1},{6,2},{7,3},{8,12},{9,13},{10,... | collective-permute-start | bytes 344072 | tf_op jit(solution)/shard_map/ppermute | solution.py:26
  21.9 18.2 %collective-permute-start.1 = (bf16[8,7168]{1,0:T(8,128)(2,1)S(1)}, bf16[8,7168]{1,0:T(8,128)(2,1)S(1)}, u32[]{:S(2)}, u32[]{:S(2)}) collective-permute-start(bf16[8,7168]{1,0:T(8,128)(2,1)S(1)} %later.2), channel_id=1, source_target_pairs={{0,0},{1,1},{2,2},{3,3},{4,4},{5,5},{6,6},{7,7},{8,8},{9,9},{10,10... | collective-permute-start | bytes 344072 | tf_op jit(solution)/shard_map/ppermute | solution.py:26
  31.5 10.4 %collective-permute-start.17 = (bf16[8,7168]{1,0:T(8,128)(2,1)S(1)}, bf16[8,7168]{1,0:T(8,128)(2,1)S(1)}, u32[]{:S(2)}, u32[]{:S(2)}) collective-permute-start(bf16[8,7168]{1,0:T(8,128)(2,1)S(1)} %get-tuple-element.24), channel_id=1, source_target_pairs={{0,0},{1,1},{2,2},{3,3},{4,4},{5,5},{6,6},{7,7},{8,8},{9,9},{10,10... | collective-permute-start | bytes 344072 | tf_op jit(solution)/shard_map/ppermute | solution.py:26
  33.4 8.5 %collective-permute-start.18 = (bf16[8,7168]{1,0:T(8,128)(2,1)S(1)}, bf16[8,7168]{1,0:T(8,128)(2,1)S(1)}, u32[]{:S(2)}, u32[]{:S(2)}) collective-permute-start(bf16[8,7168]{1,0:T(8,128)(2,1)S(1)} %get-tuple-element.25), channel_id=1, source_target_pairs={{0,4},{1,5},{2,6},{3,7},{4,0},{5,1},{6,2},{7,3},{8,12},{9,13},{10,... | collective-permute-start | bytes 344072 | tf_op jit(solution)/shard_map/ppermute | solution.py:26
  35.8 20.2 %collective-permute-start.5 = (bf16[7168,128]{1,0:T(8,128)(2,1)S(1)}, bf16[7168,128]{1,0:T(8,128)(2,1)}, u32[]{:S(2)}, u32[]{:S(2)}) collective-permute-start(bf16[7168,128]{1,0:T(8,128)(2,1)S(1)} %bitcast.8), channel_id=1, source_target_pairs={{0,16},{16,0},{32,48},{48,32},{64,80},{80,64},{96,112},{112,96},{1... | collective-permute-start | bytes 5505032 | tf_op jit(solution)/shard_map/ppermute | solution.py:17
  39.5 16.4 %collective-permute-start.6 = (bf16[7168,128]{1,0:T(8,128)(2,1)}, bf16[7168,128]{1,0:T(8,128)(2,1)S(1)}, u32[]{:S(2)}, u32[]{:S(2)}) collective-permute-start(bf16[7168,128]{1,0:T(8,128)(2,1)} %bitcast.11), channel_id=1, source_target_pairs={{0,16},{16,0},{32,48},{48,32},{64,80},{80,64},{96,112},{112,96},{1... | collective-permute-start | bytes 5505032 | tf_op jit(solution)/shard_map/ppermute | solution.py:17
  40.1 15.9 %collective-permute-start.7 = (bf16[128,7168]{1,0:T(8,128)(2,1)}, bf16[128,7168]{1,0:T(8,128)(2,1)S(1)}, u32[]{:S(2)}, u32[]{:S(2)}) collective-permute-start(bf16[128,7168]{1,0:T(8,128)(2,1)} %bitcast.14), channel_id=1, source_target_pairs={{0,16},{16,0},{32,48},{48,32},{64,80},{80,64},{96,112},{112,96},{1... | collective-permute-start | bytes 5505032 | tf_op jit(solution)/shard_map/ppermute | solution.py:17
  41.9 6.1 %collective-permute-start.3 = (bf16[16,7168]{1,0:T(8,128)(2,1)S(1)}, bf16[16,7168]{1,0:T(8,128)(2,1)S(1)}, u32[]{:S(2)}, u32[]{:S(2)}) collective-permute-start(bf16[16,7168]{1,0:T(8,128)(2,1)S(1)} %pad_maximum_fusion.4), channel_id=1, source_target_pairs={{0,64},{16,208},{32,96},{48,240},{64,0},{80,144},{96,32},{112,176}... | collective-permute-start | bytes 688136 | tf_op jit(solution)/shard_map/ppermute | solution.py:34
  41.9 14.0 %copy-start.2 = (bf16[1,7168,128]{2,1,0:T(8,128)(2,1)S(1)}, bf16[1,7168,128]{2,1,0:T(8,128)(2,1)}, u32[]{:S(2)}) copy-start(bf16[1,7168,128]{2,1,0:T(8,128)(2,1)} %param.12) | copy-start | bytes 5505028
  42.0 14.0 %copy-start.3 = (bf16[1,128,7168]{2,1,0:T(8,128)(2,1)S(1)}, bf16[1,128,7168]{2,1,0:T(8,128)(2,1)}, u32[]{:S(2)}) copy-start(bf16[1,128,7168]{2,1,0:T(8,128)(2,1)} %param.13) | copy-start | bytes 5505028
  42.0 8.5 %collective-permute-start.19 = (bf16[16,7168]{1,0:T(8,128)(2,1)S(1)}, bf16[16,7168]{1,0:T(8,128)(2,1)S(1)}, u32[]{:S(2)}, u32[]{:S(2)}) collective-permute-start(bf16[16,7168]{1,0:T(8,128)(2,1)S(1)} %pad_maximum_fusion.6), channel_id=1, source_target_pairs={{0,64},{16,208},{32,96},{48,240},{64,0},{80,144},{96,32},{112,176}... | collective-permute-start | bytes 688136 | tf_op jit(solution)/shard_map/ppermute | solution.py:34
  48.0 7.8 %collective-permute-start.4 = (bf16[32,7168]{1,0:T(8,128)(2,1)S(1)}, bf16[32,7168]{1,0:T(8,128)(2,1)S(1)}, u32[]{:S(2)}, u32[]{:S(2)}) collective-permute-start(bf16[32,7168]{1,0:T(8,128)(2,1)S(1)} %pad_maximum_fusion.2), channel_id=1, source_target_pairs={{0,192},{16,80},{32,224},{48,112},{64,128},{80,16},{96,160},{112,4... | collective-permute-start | bytes 1376264 | tf_op jit(solution)/shard_map/ppermute | solution.py:34
  50.5 10.3 %collective-permute-start.20 = (bf16[32,7168]{1,0:T(8,128)(2,1)S(1)}, bf16[32,7168]{1,0:T(8,128)(2,1)S(1)}, u32[]{:S(2)}, u32[]{:S(2)}) collective-permute-start(bf16[32,7168]{1,0:T(8,128)(2,1)S(1)} %pad_maximum_fusion.3), channel_id=1, source_target_pairs={{0,192},{16,80},{32,224},{48,112},{64,128},{80,16},{96,160},{112,4... | collective-permute-start | bytes 1376264 | tf_op jit(solution)/shard_map/ppermute | solution.py:34
  59.6 8.4 %collective-permute-start.8 = (bf16[32,7168]{1,0:T(8,128)(2,1)S(1)}, bf16[32,7168]{1,0:T(8,128)(2,1)S(1)}, u32[]{:S(2)}, u32[]{:S(2)}) collective-permute-start(bf16[32,7168]{1,0:T(8,128)(2,1)S(1)} %get-tuple-element.22), channel_id=1, source_target_pairs={{0,192},{16,80},{32,224},{48,112},{64,128},{80,16},{96,160},{112,4... | collective-permute-start | bytes 1376264 | tf_op jit(solution)/shard_map/ppermute | solution.py:34
  67.5 9.1 %collective-permute-start.21 = (bf16[32,7168]{1,0:T(8,128)(2,1)S(1)}, bf16[32,7168]{1,0:T(8,128)(2,1)S(1)}, u32[]{:S(2)}, u32[]{:S(2)}) collective-permute-start(bf16[32,7168]{1,0:T(8,128)(2,1)S(1)} %get-tuple-element.29), channel_id=1, source_target_pairs={{0,192},{16,80},{32,224},{48,112},{64,128},{80,16},{96,160},{112,4... | collective-permute-start | bytes 1376264 | tf_op jit(solution)/shard_map/ppermute | solution.py:34
  68.1 8.7 %collective-permute-start.9 = (bf16[16,7168]{1,0:T(8,128)(2,1)S(1)}, bf16[16,7168]{1,0:T(8,128)(2,1)S(1)}, u32[]{:S(2)}, u32[]{:S(2)}) collective-permute-start(bf16[16,7168]{1,0:T(8,128)(2,1)S(1)} %slice.43), channel_id=1, source_target_pairs={{0,64},{16,208},{32,96},{48,240},{64,0},{80,144},{96,32},{112,176}... | collective-permute-start | bytes 688136 | tf_op jit(solution)/shard_map/ppermute | solution.py:34
  76.7 6.2 %collective-permute-start.22 = (bf16[16,7168]{1,0:T(8,128)(2,1)S(1)}, bf16[16,7168]{1,0:T(8,128)(2,1)S(1)}, u32[]{:S(2)}, u32[]{:S(2)}) collective-permute-start(bf16[16,7168]{1,0:T(8,128)(2,1)S(1)} %slice.47), channel_id=1, source_target_pairs={{0,64},{16,208},{32,96},{48,240},{64,0},{80,144},{96,32},{112,176}... | collective-permute-start | bytes 688136 | tf_op jit(solution)/shard_map/ppermute | solution.py:34
  76.9 8.3 %collective-permute-start.10 = (bf16[8,7168]{1,0:T(8,128)(2,1)S(1)}, bf16[8,7168]{1,0:T(8,128)(2,1)S(1)}, u32[]{:S(2)}, u32[]{:S(2)}) collective-permute-start(bf16[8,7168]{1,0:T(8,128)(2,1)S(1)} %slice.45), channel_id=1, source_target_pairs={{0,32},{16,48},{32,0},{48,16},{64,96},{80,112},{96,64},{112,80},{1... | collective-permute-start | bytes 344072 | tf_op jit(solution)/shard_map/ppermute | solution.py:17
  83.0 10.0 %collective-permute-start.23 = (bf16[8,7168]{1,0:T(8,128)(2,1)S(1)}, bf16[8,7168]{1,0:T(8,128)(2,1)S(1)}, u32[]{:S(2)}, u32[]{:S(2)}) collective-permute-start(bf16[8,7168]{1,0:T(8,128)(2,1)S(1)} %slice.49), channel_id=1, source_target_pairs={{0,32},{16,48},{32,0},{48,16},{64,96},{80,112},{96,64},{112,80},{1... | collective-permute-start | bytes 344072 | tf_op jit(solution)/shard_map/ppermute | solution.py:17
  85.2 13.0 %collective-permute-start.11 = (bf16[8,7168]{1,0:T(8,128)(2,1)S(1)}, bf16[8,7168]{1,0:T(8,128)(2,1)S(1)}, u32[]{:S(2)}, u32[]{:S(2)}) collective-permute-start(bf16[8,7168]{1,0:T(8,128)(2,1)S(1)} %add_convert_fusion.5), channel_id=1, source_target_pairs={{0,0},{1,1},{2,2},{3,3},{4,4},{5,5},{6,6},{7,7},{8,8},{9,9},{10,10... | collective-permute-start | bytes 344072 | tf_op jit(solution)/shard_map/ppermute | solution.py:26
  93.0 12.1 %collective-permute-start.24 = (bf16[8,7168]{1,0:T(8,128)(2,1)S(1)}, bf16[8,7168]{1,0:T(8,128)(2,1)S(1)}, u32[]{:S(2)}, u32[]{:S(2)}) collective-permute-start(bf16[8,7168]{1,0:T(8,128)(2,1)S(1)} %add_convert_fusion.4), channel_id=1, source_target_pairs={{0,0},{1,1},{2,2},{3,3},{4,4},{5,5},{6,6},{7,7},{8,8},{9,9},{10,10... | collective-permute-start | bytes 344072 | tf_op jit(solution)/shard_map/ppermute | solution.py:26
  98.2 8.2 %collective-permute-start.12 = (bf16[8,7168]{1,0:T(8,128)(2,1)S(1)}, bf16[8,7168]{1,0:T(8,128)(2,1)S(1)}, u32[]{:S(2)}, u32[]{:S(2)}) collective-permute-start(bf16[8,7168]{1,0:T(8,128)(2,1)S(1)} %collective-permute-done.11), channel_id=1, source_target_pairs={{0,32},{16,48},{32,0},{48,16},{64,96},{80,112},{96,64},{112,80},{1... | collective-permute-start | bytes 344072 | tf_op jit(solution)/shard_map/ppermute | solution.py:17
  105.1 6.6 %collective-permute-start.25 = (bf16[8,7168]{1,0:T(8,128)(2,1)S(1)}, bf16[8,7168]{1,0:T(8,128)(2,1)S(1)}, u32[]{:S(2)}, u32[]{:S(2)}) collective-permute-start(bf16[8,7168]{1,0:T(8,128)(2,1)S(1)} %collective-permute-done.24), channel_id=1, source_target_pairs={{0,32},{16,48},{32,0},{48,16},{64,96},{80,112},{96,64},{112,80},{1... | collective-permute-start | bytes 344072 | tf_op jit(solution)/shard_map/ppermute | solution.py:17
  106.4 9.4 %collective-permute-start.13 = (bf16[16,7168]{1,0:T(8,128)(2,1)S(1)}, bf16[16,7168]{1,0:T(8,128)(2,1)S(1)}, u32[]{:S(2)}, u32[]{:S(2)}) collective-permute-start(bf16[16,7168]{1,0:T(8,128)(2,1)S(1)} %pad_maximum_fusion.5), channel_id=1, source_target_pairs={{0,64},{16,208},{32,96},{48,240},{64,0},{80,144},{96,32},{112,176}... | collective-permute-start | bytes 688136 | tf_op jit(solution)/shard_map/ppermute | solution.py:34
  111.7 7.6 %collective-permute-start.26 = (bf16[16,7168]{1,0:T(8,128)(2,1)S(1)}, bf16[16,7168]{1,0:T(8,128)(2,1)S(1)}, u32[]{:S(2)}, u32[]{:S(2)}) collective-permute-start(bf16[16,7168]{1,0:T(8,128)(2,1)S(1)} %constant_dynamic-update-slice_fusion.3.a), channel_id=1, source_target_pairs={{0,64},{16,208},{32,96},{48,240},{64,0},{80,144},{96,32},{112,176}... | collective-permute-start | bytes 688136 | tf_op jit(solution)/shard_map/ppermute | solution.py:34
  115.9 14.2 %collective-permute-start.14 = (bf16[32,7168]{1,0:T(8,128)(2,1)S(1)}, bf16[32,7168]{1,0:T(8,128)(2,1)S(1)}, u32[]{:S(2)}, u32[]{:S(2)}) collective-permute-start(bf16[32,7168]{1,0:T(8,128)(2,1)S(1)} %constant_dynamic-update-slice_fusion.refs_2_), channel_id=1, source_target_pairs={{0,192},{16,80},{32,224},{48,112},{64,128},{80,16},{96,160},{112,4... | collective-permute-start | bytes 1376264 | tf_op jit(solution)/shard_map/ppermute | solution.py:34
  119.4 0.9 copy-start.4
  120.3 20.8 %collective-permute-start.27 = (bf16[32,7168]{1,0:T(8,128)(2,1)S(1)}, bf16[32,7168]{1,0:T(8,128)(2,1)S(1)}, u32[]{:S(2)}, u32[]{:S(2)}) collective-permute-start(bf16[32,7168]{1,0:T(8,128)(2,1)S(1)} %join.1.refs_1_), channel_id=1, source_target_pairs={{0,192},{16,80},{32,224},{48,112},{64,128},{80,16},{96,160},{112,4... | collective-permute-start | bytes 1376264 | tf_op jit(solution)/shard_map/ppermute | solution.py:34
  121.3 19.8 %collective-permute-start.28 = (bf16[448,256]{1,0:T(8,128)(2,1)S(1)}, bf16[448,256]{1,0:T(8,128)(2,1)S(1)}, u32[]{:S(2)}, u32[]{:S(2)}) collective-permute-start(bf16[448,256]{1,0:T(8,128)(2,1)S(1)} %copy-done.4), channel_id=1, source_target_pairs={{0,240},{16,224},{32,208},{48,192},{64,176},{80,160},{96,144},{112... | collective-permute-start | bytes 688136 | tf_op jit(solution)/shard_map/ppermute | solution.py:386
  130.1 11.2 %collective-permute-start.15 = (bf16[32,7168]{1,0:T(8,128)(2,1)S(1)}, bf16[32,7168]{1,0:T(8,128)(2,1)S(1)}, u32[]{:S(2)}, u32[]{:S(2)}) collective-permute-start(bf16[32,7168]{1,0:T(8,128)(2,1)S(1)} %constant_dynamic-update-slice_fusion.refs_2_), channel_id=1, source_target_pairs={{0,16},{16,0},{32,48},{48,32},{64,80},{80,64},{96,112},{112,96},{1... | collective-permute-start | bytes 1376264 | tf_op jit(solution)/shard_map/ppermute | solution.py:17
  130.1 11.2 %collective-permute-start.16 = (bf16[32,7168]{1,0:T(8,128)(2,1)S(1)}, bf16[32,7168]{1,0:T(8,128)(2,1)S(1)}, u32[]{:S(2)}, u32[]{:S(2)}) collective-permute-start(bf16[32,7168]{1,0:T(8,128)(2,1)S(1)} %collective-permute-done.14.refs_3_), channel_id=1, source_target_pairs={{0,16},{16,0},{32,48},{48,32},{64,80},{80,64},{96,112},{112,96},{1... | collective-permute-start | bytes 1376264 | tf_op jit(solution)/shard_map/ppermute | solution.py:17
  130.6 13.4 %collective-permute-start.29 = (bf16[32,7168]{1,0:T(8,128)(2,1)S(1)}, bf16[32,7168]{1,0:T(8,128)(2,1)S(1)}, u32[]{:S(2)}, u32[]{:S(2)}) collective-permute-start(bf16[32,7168]{1,0:T(8,128)(2,1)S(1)} %join.1.refs_1_), channel_id=1, source_target_pairs={{0,16},{16,0},{32,48},{48,32},{64,80},{80,64},{96,112},{112,96},{1... | collective-permute-start | bytes 1376264 | tf_op jit(solution)/shard_map/ppermute | solution.py:17
  141.2 2.8 %collective-permute-start.30 = (bf16[32,7168]{1,0:T(8,128)(2,1)S(1)}, bf16[32,7168]{1,0:T(8,128)(2,1)S(1)}, u32[]{:S(2)}, u32[]{:S(2)}) collective-permute-start(bf16[32,7168]{1,0:T(8,128)(2,1)S(1)} %later.3.refs_2_), channel_id=1, source_target_pairs={{0,16},{16,0},{32,48},{48,32},{64,80},{80,64},{96,112},{112,96},{1... | collective-permute-start | bytes 1376264 | tf_op jit(solution)/shard_map/ppermute | solution.py:17
  141.3 1.9 %copy-start.5 = (bf16[448,256]{1,0:T(8,128)(2,1)S(1)}, bf16[448,256]{1,0:T(8,128)(2,1)}, u32[]{:S(2)}) copy-start(bf16[448,256]{1,0:T(8,128)(2,1)} %reduce-scatter.2.cloned.1.call-done._.share_ref) | copy-start | bytes 688132
Sparse Core Ops, SparseCore 0:
  39.7 68.5 reduce-scatter.1

commit v5 on v4

--- a/solution.py
+++ b/solution.py
@@ -231,21 +231,22 @@
     out[size:] = b[...]
 
 
-def pass_kernel(a, _, out):
+def pass_kernel(a, *refs):
+    out = refs[-1]
     out[...] = a[...]
 
 
-def later(a, after):
+def later(a, *after):
     vmem = pl.BlockSpec(memory_space=pltpu.VMEM)
     return pl.pallas_call(
         pass_kernel,
-        in_specs=[vmem, pl.BlockSpec(memory_space=pl.ANY)],
+        in_specs=[vmem] + [pl.BlockSpec(memory_space=pl.ANY)] * len(after),
         out_specs=vmem,
         out_shape=pltpu.VMEM(a.shape, a.dtype),
         cost_estimate=cost(0, 4 * a.size),
         compiler_params=pltpu.CompilerParams(vmem_limit_bytes=8 << 20),
         name="later",
-    )(near(a), after)
+    )(near(a), *after)
 
 
 def join(a, b, after):
@@ -380,7 +381,7 @@
     width = latent.shape[1] // 2
     other = jnp.where(p[0] < 8, latent[:, width:], latent[:, :width])
     got = lax.ppermute(other, "pipe", mirror)
-    send0 = later(send0, got)
+    send0 = later(send0, got, wg2)
     part, sel, hi, lo = latent_part(p, s, ids, gates, latent_grad, got, tokens)
     share = lax.psum_scatter(part, "expert", scatter_dimension=0, tiled=True)
     theirs = lax.ppermute(share, "pipe", mirror)
@@ -391,7 +392,7 @@
     kept, sent, fa, fb = forward(rows, wg, wu, wg2, wu2, wd, wd2, hi)
     routed = combine([hi, lo], collect(kept, sent))
     dkept, dsent = backward(drows, fa, fb, wd, wd2, wg, wu, wg2, wu2)
-    token_grad = combine([sel], collect(dkept, dsent, share, theirs))
+    token_grad = combine([sel], collect(dkept, dsent, sel, theirs))
     return routed, token_grad, kv_grad
 
 

time: 153 us -> 152 us (level)
  waiting for transfers between devices: 58.6 us -> 53.4 us
  starting transfers between devices: 53.8 us -> 57.8 us
    ppermute x12, starting transfers between devices: 12.6 us -> 17.8 us  [along_x(): return lax.ppermute(value, 'pipe', pairs)]
    ppermute x1, starting transfers between devices: 6.59 us -> 3.37 us  [per_device(): got = lax.ppermute(other, 'pipe', mirror)]
    ppermute x11, starting transfers between devices: 2.85 us -> 5.8 us  [across(): return lax.ppermute(value, 'pipe', [(i, i ^ mask) for i in range(16)])]
    ppermute x12, waiting for transfers between devices: 28.4 us -> 25.8 us  [along_x(): return lax.ppermute(value, 'pipe', pairs)]
    ppermute x6, waiting for transfers between devices: 10.6 us -> 8.16 us  [shifted(): return lax.ppermute(value, ('pipe', 'expert'), pairs)]
    ppermute x1, starting transfers between devices: 8.77 us -> 6.75 us  [per_device(): theirs = lax.ppermute(share, 'pipe', mirror)]
  transfers between devices with their start and end apart: 32 -> 32, of which waited for: 15 -> 15; matrix products, arithmetic and copies ran while one was open for 0% -> 1% of each run, Pallas kernels for 13% -> 14%
where the time goes in v5:
time: 152 us; the launch traced here: 151 us
  starting transfers between devices  57.8 us (38%)
  waiting for transfers between devices  53.4 us (35%)
  Pallas kernels  22.6 us (15%)
  between operations  14.5 us (10%)
  local copies, waits for them, and re-layouts  1.52 us (1%)
    ppermute x12, waiting for transfers between devices, along_x(): return lax.ppermute(value, 'pipe', pairs)  25.8 us
    ppermute x6, starting transfers between devices, shifted(): return lax.ppermute(value, ('pipe', 'expert'), pairs)  24.1 us
    ppermute x12, starting transfers between devices, along_x(): return lax.ppermute(value, 'pipe', pairs)  17.8 us
    ppermute x11, waiting for transfers between devices, across(): return lax.ppermute(value, 'pipe', [(i, i ^ mask) for i in range(16)])  10.1 us
    ppermute x1, waiting for transfers between devices, per_device(): theirs = lax.ppermute(share, 'pipe', mirror)  9.35 us
    ppermute x6, waiting for transfers between devices, shifted(): return lax.ppermute(value, ('pipe', 'expert'), pairs)  8.16 us
    pallas_call x1, Pallas kernels, backward(): pl.pallas_call(backward_kernel, in_specs=[vmem] * 9, out_specs=[vmem] * 2...  7.2 us
    ppermute x1, starting transfers between devices, per_device(): theirs = lax.ppermute(share, 'pipe', mirror)  6.75 us
  transfers between devices with their start and end apart: 32, of which 15 were waited for; matrix products, arithmetic and copies ran while one was open for 1% of the time, Pallas kernels for 14%

profile of v5, /device:TPU:1, one launch (start us, length us, event | category | flops | bytes accessed | tf_op | source)
XLA Modules:
  0.0 151.4 jit_solution(3118461133149025226)
XLA Ops:
  7.2 0.0 reduce-scatter.2.cloned.1.call-start
  7.2 3.3 %collective-permute-start.1 = (bf16[7168,128]{1,0:T(8,128)(2,1)}, bf16[7168,128]{1,0:T(8,128)(2,1)S(1)}, u32[]{:S(2)}, u32[]{:S(2)}) collective-permute-start(bf16[7168,128]{1,0:T(8,128)(2,1)} %bitcast.8), channel_id=1, source_target_pairs={{0,16},{16,0},{32,48},{48,32},{64,80},{80,64},{96,112},{112,96},{1... | collective-permute-start | bytes 5505032 | tf_op jit(solution)/shard_map/ppermute | solution.py:17
  10.5 0.9 slice_select_fusion
  11.4 3.4 %collective-permute-start = (bf16[128,256]{1,0:T(8,128)(2,1)S(1)}, bf16[128,256]{1,0:T(8,128)(2,1)S(1)}, u32[]{:S(2)}, u32[]{:S(2)}) collective-permute-start(bf16[128,256]{1,0:T(8,128)(2,1)S(1)} %slice_select_fusion), channel_id=1, source_target_pairs={{0,240},{16,224},{32,208},{48,192},{64,176},{80,160},{96,144},{112... | collective-permute-start | bytes 196616 | tf_op jit(solution)/shard_map/ppermute | solution.py:383
  14.8 0.7 copy-done.5
  15.5 0.7 copy-done.7
  16.2 3.3 %select.1 = (bf16[8,7168]{1,0:T(8,128)(2,1)S(1)}, bf16[8,7168]{1,0:T(8,128)(2,1)S(1)}, bf16[8,7168]{1,0:T(8,128)(2,1)S(1)}, bf16[8,7168]{1,0:T(8,128)(2,1)S(1)}) custom-call(s32[1]{0:T(128)} %bitcast.p_ref, s32[1]{0:T(128)} %bitcast.1.s_ref, s32[8,128]{1,0:T(8,128)S(1)} %bitcast.15, f32[8,128]{1,0:T(8,128)S(1)} %bitcast.17, bf16[128,7168]{1,0:T(8,128)(2,1)} %tok_ref.3, ...), custom_call_target="tpu_custom_call" | custom-call | flops 58720256 | bytes 3670016 | tf_op jit(solution)/shard_map/select/pallas_call | solution.py:136
  19.5 0.0 copy-start
  19.5 0.0 copy-start.3
  19.5 0.0 copy-start.8
  19.6 2.4 %collective-permute-start.3 = (bf16[8,7168]{1,0:T(8,128)(2,1)S(1)}, bf16[8,7168]{1,0:T(8,128)(2,1)S(1)}, u32[]{:S(2)}, u32[]{:S(2)}) collective-permute-start(bf16[8,7168]{1,0:T(8,128)(2,1)S(1)} %get-tuple-element.20), channel_id=1, source_target_pairs={{0,4},{1,5},{2,6},{3,7},{4,0},{5,1},{6,2},{7,3},{8,12},{9,13},{10,... | collective-permute-start | bytes 344072 | tf_op jit(solution)/shard_map/ppermute | solution.py:26
  22.0 9.6 %collective-permute-start.2 = (bf16[8,7168]{1,0:T(8,128)(2,1)S(1)}, bf16[8,7168]{1,0:T(8,128)(2,1)S(1)}, u32[]{:S(2)}, u32[]{:S(2)}) collective-permute-start(bf16[8,7168]{1,0:T(8,128)(2,1)S(1)} %later.2), channel_id=1, source_target_pairs={{0,0},{1,1},{2,2},{3,3},{4,4},{5,5},{6,6},{7,7},{8,8},{9,9},{10,10... | collective-permute-start | bytes 344072 | tf_op jit(solution)/shard_map/ppermute | solution.py:26
  31.6 1.9 %collective-permute-start.17 = (bf16[8,7168]{1,0:T(8,128)(2,1)S(1)}, bf16[8,7168]{1,0:T(8,128)(2,1)S(1)}, u32[]{:S(2)}, u32[]{:S(2)}) collective-permute-start(bf16[8,7168]{1,0:T(8,128)(2,1)S(1)} %get-tuple-element.24), channel_id=1, source_target_pairs={{0,0},{1,1},{2,2},{3,3},{4,4},{5,5},{6,6},{7,7},{8,8},{9,9},{10,10... | collective-permute-start | bytes 344072 | tf_op jit(solution)/shard_map/ppermute | solution.py:26
  33.6 2.3 %collective-permute-start.18 = (bf16[8,7168]{1,0:T(8,128)(2,1)S(1)}, bf16[8,7168]{1,0:T(8,128)(2,1)S(1)}, u32[]{:S(2)}, u32[]{:S(2)}) collective-permute-start(bf16[8,7168]{1,0:T(8,128)(2,1)S(1)} %get-tuple-element.25), channel_id=1, source_target_pairs={{0,4},{1,5},{2,6},{3,7},{4,0},{5,1},{6,2},{7,3},{8,12},{9,13},{10,... | collective-permute-start | bytes 344072 | tf_op jit(solution)/shard_map/ppermute | solution.py:26
  35.9 0.1 collective-permute-start.6
  36.0 3.6 %latent_part.1 = (bf16[7168,256]{1,0:T(8,128)(2,1)}, bf16[128,128]{1,0:T(8,128)(2,1)S(1)}, bf16[128,128]{1,0:T(8,128)(2,1)S(1)}, bf16[128,128]{1,0:T(8,128)(2,1)S(1)}) custom-call(s32[1]{0:T(128)} %bitcast.p_ref, s32[1]{0:T(128)} %bitcast.1.s_ref, s32[8,128]{1,0:T(8,128)S(1)} %bitcast.16, f32[8,128]{1,0:T(8,128)S(1)} %bitcast.18, ...), custom_call_target="tpu_custom_call" | custom-call | flops 469762048 | bytes 5505024 | tf_op jit(solution)/shard_map/latent_part/pallas_call | solution.py:185
  39.7 0.0 reduce-scatter.2.cloned.1.call-update
  39.7 0.6 collective-permute-start.7
  40.3 1.6 %collective-permute-start.4 = (bf16[16,7168]{1,0:T(8,128)(2,1)S(1)}, bf16[16,7168]{1,0:T(8,128)(2,1)S(1)}, u32[]{:S(2)}, u32[]{:S(2)}) collective-permute-start(bf16[16,7168]{1,0:T(8,128)(2,1)S(1)} %pad_maximum_fusion.4), channel_id=1, source_target_pairs={{0,64},{16,208},{32,96},{48,240},{64,0},{80,144},{96,32},{112,176}... | collective-permute-start | bytes 688136 | tf_op jit(solution)/shard_map/ppermute | solution.py:34
  41.9 0.5 collective-permute-done.17
  42.4 0.0 copy-start.1
  42.4 0.9 collective-permute-start.19
  43.4 3.1 %collective-permute-done.4 = bf16[16,7168]{1,0:T(8,128)(2,1)S(1)} collective-permute-done((bf16[16,7168]{1,0:T(8,128)(2,1)S(1)}, bf16[16,7168]{1,0:T(8,128)(2,1)S(1)}, u32[]{:S(2)}, u32[]{:S(2)}) %collective-permute-start.4) | collective-permute-done | bytes 229408 | tf_op jit(solution)/shard_map/ppermute | solution.py:34
  46.5 0.1 collective-permute-start.5
  46.6 2.3 %collective-permute-done.19 = bf16[16,7168]{1,0:T(8,128)(2,1)S(1)} collective-permute-done((bf16[16,7168]{1,0:T(8,128)(2,1)S(1)}, bf16[16,7168]{1,0:T(8,128)(2,1)S(1)}, u32[]{:S(2)}, u32[]{:S(2)}) %collective-permute-start.19) | collective-permute-done | bytes 229408 | tf_op jit(solution)/shard_map/ppermute | solution.py:34
  48.9 0.1 collective-permute-start.20
  49.0 5.6 %collective-permute-done.5 = bf16[32,7168]{1,0:T(8,128)(2,1)S(1)} collective-permute-done((bf16[32,7168]{1,0:T(8,128)(2,1)S(1)}, bf16[32,7168]{1,0:T(8,128)(2,1)S(1)}, u32[]{:S(2)}, u32[]{:S(2)}) %collective-permute-start.5) | collective-permute-done | bytes 458784 | tf_op jit(solution)/shard_map/ppermute | solution.py:34
  54.6 0.1 pad_maximum_fusion.rows
  54.7 4.2 %forward.1 = (bf16[32,7168]{1,0:T(8,128)(2,1)S(1)}, bf16[32,7168]{1,0:T(8,128)(2,1)S(1)}, f32[64,256]{1,0:T(8,128)S(1)}, f32[64,256]{1,0:T(8,128)S(1)}) custom-call(bf16[64,7168]{1,0:T(8,128)(2,1)S(1)} %pad_maximum_fusion.rows, bf16[7168,128]{1,0:T(8,128)(2,1)S(1)} %bitcast.9, bf16[7168,128]{1,0:T(8,128)(2,1)} %bitcast.6.wu, ...), custom_call_target="tpu_custom_call" | custom-call | flops 704643072 | bytes 12845056 | tf_op jit(solution)/shard_map/forward/pallas_call | solution.py:293
  58.9 1.8 %collective-permute-start.8 = (bf16[32,7168]{1,0:T(8,128)(2,1)S(1)}, bf16[32,7168]{1,0:T(8,128)(2,1)S(1)}, u32[]{:S(2)}, u32[]{:S(2)}) collective-permute-start(bf16[32,7168]{1,0:T(8,128)(2,1)S(1)} %get-tuple-element.22), channel_id=1, source_target_pairs={{0,192},{16,80},{32,224},{48,112},{64,128},{80,16},{96,160},{112,4... | collective-permute-start | bytes 1376264 | tf_op jit(solution)/shard_map/ppermute | solution.py:34
  60.8 0.1 pad_maximum_fusion.1.rows
  60.8 7.2 %backward.1 = (bf16[32,7168]{1,0:T(8,128)(2,1)S(1)}, bf16[32,7168]{1,0:T(8,128)(2,1)S(1)}) custom-call(bf16[64,7168]{1,0:T(8,128)(2,1)S(1)} %pad_maximum_fusion.1.rows, f32[64,256]{1,0:T(8,128)S(1)} %get-tuple-element.26.fa, f32[64,256]{1,0:T(8,128)S(1)} %get-tuple-element.27.fb, bf16[128,7168]{1,0:T(8,128)(2,1)S(1)} %bitcast.13, ...), custom_call_target="tpu_custom_call" | custom-call | flops 704643072 | bytes 12845056 | tf_op jit(solution)/shard_map/backward/pallas_call | solution.py:325
  68.0 0.5 collective-permute-start.21
  68.5 0.1 add_convert_fusion.1
  68.7 0.6 collective-permute-start.9
  69.3 7.6 %collective-permute-done.21 = bf16[32,7168]{1,0:T(8,128)(2,1)S(1)} collective-permute-done((bf16[32,7168]{1,0:T(8,128)(2,1)S(1)}, bf16[32,7168]{1,0:T(8,128)(2,1)S(1)}, u32[]{:S(2)}, u32[]{:S(2)}) %collective-permute-start.21) | collective-permute-done | bytes 458784 | tf_op jit(solution)/shard_map/ppermute | solution.py:34
  76.9 0.1 add_convert_fusion
  77.1 0.3 collective-permute-start.22
  77.4 0.1 add_convert_fusion.3
  77.4 0.6 collective-permute-start.10
  78.1 5.4 %collective-permute-done.22 = bf16[16,7168]{1,0:T(8,128)(2,1)S(1)} collective-permute-done((bf16[16,7168]{1,0:T(8,128)(2,1)S(1)}, bf16[16,7168]{1,0:T(8,128)(2,1)S(1)}, u32[]{:S(2)}, u32[]{:S(2)}) %collective-permute-start.22) | collective-permute-done | bytes 229408 | tf_op jit(solution)/shard_map/ppermute | solution.py:34
  83.4 0.1 add_convert_fusion.2
  83.5 0.6 collective-permute-start.23
  84.1 3.3 %collective-permute-done.10 = bf16[8,7168]{1,0:T(8,128)(2,1)S(1)} collective-permute-done((bf16[8,7168]{1,0:T(8,128)(2,1)S(1)}, bf16[8,7168]{1,0:T(8,128)(2,1)S(1)}, u32[]{:S(2)}, u32[]{:S(2)}) %collective-permute-start.10) | collective-permute-done | bytes 114720 | tf_op jit(solution)/shard_map/ppermute | solution.py:17
  87.4 3.4 %collective-permute-start.11 = (bf16[8,7168]{1,0:T(8,128)(2,1)S(1)}, bf16[8,7168]{1,0:T(8,128)(2,1)S(1)}, u32[]{:S(2)}, u32[]{:S(2)}) collective-permute-start(bf16[8,7168]{1,0:T(8,128)(2,1)S(1)} %add_convert_fusion.5), channel_id=1, source_target_pairs={{0,0},{1,1},{2,2},{3,3},{4,4},{5,5},{6,6},{7,7},{8,8},{9,9},{10,10... | collective-permute-start | bytes 344072 | tf_op jit(solution)/shard_map/ppermute | solution.py:26
  90.8 2.2 %collective-permute-done.23 = bf16[8,7168]{1,0:T(8,128)(2,1)S(1)} collective-permute-done((bf16[8,7168]{1,0:T(8,128)(2,1)S(1)}, bf16[8,7168]{1,0:T(8,128)(2,1)S(1)}, u32[]{:S(2)}, u32[]{:S(2)}) %collective-permute-start.23) | collective-permute-done | bytes 114720 | tf_op jit(solution)/shard_map/ppermute | solution.py:17
  93.1 4.5 %collective-permute-start.24 = (bf16[8,7168]{1,0:T(8,128)(2,1)S(1)}, bf16[8,7168]{1,0:T(8,128)(2,1)S(1)}, u32[]{:S(2)}, u32[]{:S(2)}) collective-permute-start(bf16[8,7168]{1,0:T(8,128)(2,1)S(1)} %add_convert_fusion.4), channel_id=1, source_target_pairs={{0,0},{1,1},{2,2},{3,3},{4,4},{5,5},{6,6},{7,7},{8,8},{9,9},{10,10... | collective-permute-start | bytes 344072 | tf_op jit(solution)/shard_map/ppermute | solution.py:26
  97.6 3.0 %collective-permute-done.11 = bf16[8,7168]{1,0:T(8,128)(2,1)S(1)} collective-permute-done((bf16[8,7168]{1,0:T(8,128)(2,1)S(1)}, bf16[8,7168]{1,0:T(8,128)(2,1)S(1)}, u32[]{:S(2)}, u32[]{:S(2)}) %collective-permute-start.11) | collective-permute-done | bytes 114720 | tf_op jit(solution)/shard_map/ppermute | solution.py:26
  100.6 4.7 %collective-permute-done.24 = bf16[8,7168]{1,0:T(8,128)(2,1)S(1)} collective-permute-done((bf16[8,7168]{1,0:T(8,128)(2,1)S(1)}, bf16[8,7168]{1,0:T(8,128)(2,1)S(1)}, u32[]{:S(2)}, u32[]{:S(2)}) %collective-permute-start.24) | collective-permute-done | bytes 114720 | tf_op jit(solution)/shard_map/ppermute | solution.py:26
  105.3 3.5 %collective-permute-done.12 = bf16[8,7168]{1,0:T(8,128)(2,1)S(1)} collective-permute-done((bf16[8,7168]{1,0:T(8,128)(2,1)S(1)}, bf16[8,7168]{1,0:T(8,128)(2,1)S(1)}, u32[]{:S(2)}, u32[]{:S(2)}) %collective-permute-start.12) | collective-permute-done | bytes 114720 | tf_op jit(solution)/shard_map/ppermute | solution.py:17
  108.8 1.6 %collective-permute-start.13 = (bf16[16,7168]{1,0:T(8,128)(2,1)S(1)}, bf16[16,7168]{1,0:T(8,128)(2,1)S(1)}, u32[]{:S(2)}, u32[]{:S(2)}) collective-permute-start(bf16[16,7168]{1,0:T(8,128)(2,1)S(1)} %pad_maximum_fusion.5), channel_id=1, source_target_pairs={{0,64},{16,208},{32,96},{48,240},{64,0},{80,144},{96,32},{112,176}... | collective-permute-start | bytes 688136 | tf_op jit(solution)/shard_map/ppermute | solution.py:34
  110.4 1.0 collective-permute-done.25
  111.4 3.3 %collective-permute-start.26 = (bf16[16,7168]{1,0:T(8,128)(2,1)S(1)}, bf16[16,7168]{1,0:T(8,128)(2,1)S(1)}, u32[]{:S(2)}, u32[]{:S(2)}) collective-permute-start(bf16[16,7168]{1,0:T(8,128)(2,1)S(1)} %constant_dynamic-update-slice_fusion.3.a), channel_id=1, source_target_pairs={{0,64},{16,208},{32,96},{48,240},{64,0},{80,144},{96,32},{112,176}... | collective-permute-start | bytes 688136 | tf_op jit(solution)/shard_map/ppermute | solution.py:34
  114.7 0.7 collective-permute-done.13
  115.4 3.2 %collective-permute-start.14 = (bf16[32,7168]{1,0:T(8,128)(2,1)S(1)}, bf16[32,7168]{1,0:T(8,128)(2,1)S(1)}, u32[]{:S(2)}, u32[]{:S(2)}) collective-permute-start(bf16[32,7168]{1,0:T(8,128)(2,1)S(1)} %constant_dynamic-update-slice_fusion.refs_2_), channel_id=1, source_target_pairs={{0,192},{16,80},{32,224},{48,112},{64,128},{80,16},{96,160},{112,4... | collective-permute-start | bytes 1376264 | tf_op jit(solution)/shard_map/ppermute | solution.py:34
  118.7 3.7 %collective-permute-start.27 = (bf16[32,7168]{1,0:T(8,128)(2,1)S(1)}, bf16[32,7168]{1,0:T(8,128)(2,1)S(1)}, u32[]{:S(2)}, u32[]{:S(2)}) collective-permute-start(bf16[32,7168]{1,0:T(8,128)(2,1)S(1)} %join.1.refs_1_), channel_id=1, source_target_pairs={{0,192},{16,80},{32,224},{48,112},{64,128},{80,16},{96,160},{112,4... | collective-permute-start | bytes 1376264 | tf_op jit(solution)/shard_map/ppermute | solution.py:34
  122.3 6.7 %collective-permute-start.28 = (bf16[448,256]{1,0:T(8,128)(2,1)}, bf16[448,256]{1,0:T(8,128)(2,1)S(1)}, u32[]{:S(2)}, u32[]{:S(2)}) collective-permute-start(bf16[448,256]{1,0:T(8,128)(2,1)} %reduce-scatter.2.cloned.1.call-done.share_ref), channel_id=1, source_target_pairs={{0,240},{16,224},{32,208},{48,192},{64,176},{80,160},{96,144},{112... | collective-permute-start | bytes 688136 | tf_op jit(solution)/shard_map/ppermute | solution.py:387
  129.1 0.5 collective-permute-start.16
  129.6 1.2 collective-permute-done.27.a
  130.8 9.4 %collective-permute-done.28.refs_0_.theirs_ref = bf16[448,256]{1,0:T(8,128)(2,1)S(1)} collective-permute-done((bf16[448,256]{1,0:T(8,128)(2,1)}, bf16[448,256]{1,0:T(8,128)(2,1)S(1)}, u32[]{:S(2)}, u32[]{:S(2)}) %collective-permute-start.28) | collective-permute-done | bytes 229408 | tf_op jit(solution)/shard_map/ppermute | solution.py:387
  140.2 0.1 collective-permute-start.30
  140.3 1.9 %combine.2 = bf16[128,7168]{1,0:T(8,128)(2,1)} custom-call(bf16[128,128]{1,0:T(8,128)(2,1)S(1)} %get-tuple-element.17._.refs_0_, bf16[128,128]{1,0:T(8,128)(2,1)S(1)} %get-tuple-element.18.refs_1_, bf16[32,7168]{1,0:T(8,128)(2,1)S(1)} %constant_dynamic-update-slice_fusion.refs_2_, bf16[32,7168]{1,0:T(8,128)(2,1)S(1)} %collective-permute-done.14.refs_3_, ...), custom_call_target="tpu_custom_call" | custom-call | flops 469762048 | bytes 3670016 | tf_op jit(solution)/shard_map/combine/pallas_call | solution.py:359
  142.2 0.8 finish.1
  143.0 1.5 combine.3
  (52 shorter events, 0.4 us)
Async XLA Ops:
  7.2 115.2 %reduce-scatter.2.cloned.1.call-start = ((), (), s32[]{:S(2)}) async-start(), calls=%async_computation.1 | async-start | bytes 3899392 | tf_op jit(solution)/shard_map/reduce_scatter | solution.py:386
  7.2 14.8 %collective-permute-start.1 = (bf16[7168,128]{1,0:T(8,128)(2,1)}, bf16[7168,128]{1,0:T(8,128)(2,1)S(1)}, u32[]{:S(2)}, u32[]{:S(2)}) collective-permute-start(bf16[7168,128]{1,0:T(8,128)(2,1)} %bitcast.8), channel_id=1, source_target_pairs={{0,16},{16,0},{32,48},{48,32},{64,80},{80,64},{96,112},{112,96},{1... | collective-permute-start | bytes 5505032 | tf_op jit(solution)/shard_map/ppermute | solution.py:17
  11.4 10.6 %collective-permute-start = (bf16[128,256]{1,0:T(8,128)(2,1)S(1)}, bf16[128,256]{1,0:T(8,128)(2,1)S(1)}, u32[]{:S(2)}, u32[]{:S(2)}) collective-permute-start(bf16[128,256]{1,0:T(8,128)(2,1)S(1)} %slice_select_fusion), channel_id=1, source_target_pairs={{0,240},{16,224},{32,208},{48,192},{64,176},{80,160},{96,144},{112... | collective-permute-start | bytes 196616 | tf_op jit(solution)/shard_map/ppermute | solution.py:383
  14.8 0.7 copy-start.5
  15.5 0.7 copy-start.7
  19.5 16.5 %copy-start = (bf16[128,7168]{1,0:T(8,128)(2,1)S(1)}, bf16[128,7168]{1,0:T(8,128)(2,1)}, u32[]{:S(2)}) copy-start(bf16[128,7168]{1,0:T(8,128)(2,1)} %tok_ref.3) | copy-start | bytes 5505028
  19.5 16.5 %copy-start.3 = (bf16[1,128,512]{2,1,0:T(8,128)(2,1)S(1)}, bf16[1,128,512]{2,1,0:T(8,128)(2,1)}, u32[]{:S(2)}) copy-start(bf16[1,128,512]{2,1,0:T(8,128)(2,1)} %lat_ref.1) | copy-start | bytes 393220
  19.5 16.5 %copy-start.6 = (s32[128,8]{0,1:T(8,128)S(1)}, s32[128,8]{0,1:T(8,128)}, u32[]{:S(2)}) copy-start(s32[128,8]{0,1:T(8,128)} %param.9) | copy-start | bytes 12292
  19.5 16.5 %copy-start.8 = (f32[128,8]{0,1:T(8,128)S(1)}, f32[128,8]{0,1:T(8,128)}, u32[]{:S(2)}) copy-start(f32[128,8]{0,1:T(8,128)} %param.10) | copy-start | bytes 12292
  19.6 20.1 %collective-permute-start.3 = (bf16[8,7168]{1,0:T(8,128)(2,1)S(1)}, bf16[8,7168]{1,0:T(8,128)(2,1)S(1)}, u32[]{:S(2)}, u32[]{:S(2)}) collective-permute-start(bf16[8,7168]{1,0:T(8,128)(2,1)S(1)} %get-tuple-element.20), channel_id=1, source_target_pairs={{0,4},{1,5},{2,6},{3,7},{4,0},{5,1},{6,2},{7,3},{8,12},{9,13},{10,... | collective-permute-start | bytes 344072 | tf_op jit(solution)/shard_map/ppermute | solution.py:26
  22.0 18.2 %collective-permute-start.2 = (bf16[8,7168]{1,0:T(8,128)(2,1)S(1)}, bf16[8,7168]{1,0:T(8,128)(2,1)S(1)}, u32[]{:S(2)}, u32[]{:S(2)}) collective-permute-start(bf16[8,7168]{1,0:T(8,128)(2,1)S(1)} %later.2), channel_id=1, source_target_pairs={{0,0},{1,1},{2,2},{3,3},{4,4},{5,5},{6,6},{7,7},{8,8},{9,9},{10,10... | collective-permute-start | bytes 344072 | tf_op jit(solution)/shard_map/ppermute | solution.py:26
  31.6 10.7 %collective-permute-start.17 = (bf16[8,7168]{1,0:T(8,128)(2,1)S(1)}, bf16[8,7168]{1,0:T(8,128)(2,1)S(1)}, u32[]{:S(2)}, u32[]{:S(2)}) collective-permute-start(bf16[8,7168]{1,0:T(8,128)(2,1)S(1)} %get-tuple-element.24), channel_id=1, source_target_pairs={{0,0},{1,1},{2,2},{3,3},{4,4},{5,5},{6,6},{7,7},{8,8},{9,9},{10,10... | collective-permute-start | bytes 344072 | tf_op jit(solution)/shard_map/ppermute | solution.py:26
  33.6 8.8 %collective-permute-start.18 = (bf16[8,7168]{1,0:T(8,128)(2,1)S(1)}, bf16[8,7168]{1,0:T(8,128)(2,1)S(1)}, u32[]{:S(2)}, u32[]{:S(2)}) collective-permute-start(bf16[8,7168]{1,0:T(8,128)(2,1)S(1)} %get-tuple-element.25), channel_id=1, source_target_pairs={{0,4},{1,5},{2,6},{3,7},{4,0},{5,1},{6,2},{7,3},{8,12},{9,13},{10,... | collective-permute-start | bytes 344072 | tf_op jit(solution)/shard_map/ppermute | solution.py:26
  35.9 18.8 %collective-permute-start.6 = (bf16[7168,128]{1,0:T(8,128)(2,1)}, bf16[7168,128]{1,0:T(8,128)(2,1)}, u32[]{:S(2)}, u32[]{:S(2)}) collective-permute-start(bf16[7168,128]{1,0:T(8,128)(2,1)} %bitcast.6.wu), channel_id=1, source_target_pairs={{0,16},{16,0},{32,48},{48,32},{64,80},{80,64},{96,112},{112,96},{1... | collective-permute-start | bytes 5505032 | tf_op jit(solution)/shard_map/ppermute | solution.py:17
  39.7 15.0 %collective-permute-start.7 = (bf16[128,7168]{1,0:T(8,128)(2,1)}, bf16[128,7168]{1,0:T(8,128)(2,1)S(1)}, u32[]{:S(2)}, u32[]{:S(2)}) collective-permute-start(bf16[128,7168]{1,0:T(8,128)(2,1)} %bitcast.11), channel_id=1, source_target_pairs={{0,16},{16,0},{32,48},{48,32},{64,80},{80,64},{96,112},{112,96},{1... | collective-permute-start | bytes 5505032 | tf_op jit(solution)/shard_map/ppermute | solution.py:17
  40.3 6.2 %collective-permute-start.4 = (bf16[16,7168]{1,0:T(8,128)(2,1)S(1)}, bf16[16,7168]{1,0:T(8,128)(2,1)S(1)}, u32[]{:S(2)}, u32[]{:S(2)}) collective-permute-start(bf16[16,7168]{1,0:T(8,128)(2,1)S(1)} %pad_maximum_fusion.4), channel_id=1, source_target_pairs={{0,64},{16,208},{32,96},{48,240},{64,0},{80,144},{96,32},{112,176}... | collective-permute-start | bytes 688136 | tf_op jit(solution)/shard_map/ppermute | solution.py:34
  42.4 12.3 %copy-start.1 = (bf16[1,7168,128]{2,1,0:T(8,128)(2,1)S(1)}, bf16[1,7168,128]{2,1,0:T(8,128)(2,1)}, u32[]{:S(2)}) copy-start(bf16[1,7168,128]{2,1,0:T(8,128)(2,1)} %param.11) | copy-start | bytes 5505028
  42.4 12.3 %copy-start.2 = (bf16[1,128,7168]{2,1,0:T(8,128)(2,1)S(1)}, bf16[1,128,7168]{2,1,0:T(8,128)(2,1)}, u32[]{:S(2)}) copy-start(bf16[1,128,7168]{2,1,0:T(8,128)(2,1)} %param.13) | copy-start | bytes 5505028
  42.4 6.5 %collective-permute-start.19 = (bf16[16,7168]{1,0:T(8,128)(2,1)S(1)}, bf16[16,7168]{1,0:T(8,128)(2,1)S(1)}, u32[]{:S(2)}, u32[]{:S(2)}) collective-permute-start(bf16[16,7168]{1,0:T(8,128)(2,1)S(1)} %pad_maximum_fusion.6), channel_id=1, source_target_pairs={{0,64},{16,208},{32,96},{48,240},{64,0},{80,144},{96,32},{112,176}... | collective-permute-start | bytes 688136 | tf_op jit(solution)/shard_map/ppermute | solution.py:34
  46.5 8.1 %collective-permute-start.5 = (bf16[32,7168]{1,0:T(8,128)(2,1)S(1)}, bf16[32,7168]{1,0:T(8,128)(2,1)S(1)}, u32[]{:S(2)}, u32[]{:S(2)}) collective-permute-start(bf16[32,7168]{1,0:T(8,128)(2,1)S(1)} %pad_maximum_fusion.2), channel_id=1, source_target_pairs={{0,192},{16,80},{32,224},{48,112},{64,128},{80,16},{96,160},{112,4... | collective-permute-start | bytes 1376264 | tf_op jit(solution)/shard_map/ppermute | solution.py:34
  48.9 11.8 %collective-permute-start.20 = (bf16[32,7168]{1,0:T(8,128)(2,1)S(1)}, bf16[32,7168]{1,0:T(8,128)(2,1)S(1)}, u32[]{:S(2)}, u32[]{:S(2)}) collective-permute-start(bf16[32,7168]{1,0:T(8,128)(2,1)S(1)} %pad_maximum_fusion.3), channel_id=1, source_target_pairs={{0,192},{16,80},{32,224},{48,112},{64,128},{80,16},{96,160},{112,4... | collective-permute-start | bytes 1376264 | tf_op jit(solution)/shard_map/ppermute | solution.py:34
  58.9 9.6 %collective-permute-start.8 = (bf16[32,7168]{1,0:T(8,128)(2,1)S(1)}, bf16[32,7168]{1,0:T(8,128)(2,1)S(1)}, u32[]{:S(2)}, u32[]{:S(2)}) collective-permute-start(bf16[32,7168]{1,0:T(8,128)(2,1)S(1)} %get-tuple-element.22), channel_id=1, source_target_pairs={{0,192},{16,80},{32,224},{48,112},{64,128},{80,16},{96,160},{112,4... | collective-permute-start | bytes 1376264 | tf_op jit(solution)/shard_map/ppermute | solution.py:34
  68.0 8.9 %collective-permute-start.21 = (bf16[32,7168]{1,0:T(8,128)(2,1)S(1)}, bf16[32,7168]{1,0:T(8,128)(2,1)S(1)}, u32[]{:S(2)}, u32[]{:S(2)}) collective-permute-start(bf16[32,7168]{1,0:T(8,128)(2,1)S(1)} %get-tuple-element.29), channel_id=1, source_target_pairs={{0,192},{16,80},{32,224},{48,112},{64,128},{80,16},{96,160},{112,4... | collective-permute-start | bytes 1376264 | tf_op jit(solution)/shard_map/ppermute | solution.py:34
  68.7 8.7 %collective-permute-start.9 = (bf16[16,7168]{1,0:T(8,128)(2,1)S(1)}, bf16[16,7168]{1,0:T(8,128)(2,1)S(1)}, u32[]{:S(2)}, u32[]{:S(2)}) collective-permute-start(bf16[16,7168]{1,0:T(8,128)(2,1)S(1)} %slice.43), channel_id=1, source_target_pairs={{0,64},{16,208},{32,96},{48,240},{64,0},{80,144},{96,32},{112,176}... | collective-permute-start | bytes 688136 | tf_op jit(solution)/shard_map/ppermute | solution.py:34
  77.1 6.3 %collective-permute-start.22 = (bf16[16,7168]{1,0:T(8,128)(2,1)S(1)}, bf16[16,7168]{1,0:T(8,128)(2,1)S(1)}, u32[]{:S(2)}, u32[]{:S(2)}) collective-permute-start(bf16[16,7168]{1,0:T(8,128)(2,1)S(1)} %slice.47), channel_id=1, source_target_pairs={{0,64},{16,208},{32,96},{48,240},{64,0},{80,144},{96,32},{112,176}... | collective-permute-start | bytes 688136 | tf_op jit(solution)/shard_map/ppermute | solution.py:34
  77.4 10.0 %collective-permute-start.10 = (bf16[8,7168]{1,0:T(8,128)(2,1)S(1)}, bf16[8,7168]{1,0:T(8,128)(2,1)S(1)}, u32[]{:S(2)}, u32[]{:S(2)}) collective-permute-start(bf16[8,7168]{1,0:T(8,128)(2,1)S(1)} %slice.45), channel_id=1, source_target_pairs={{0,32},{16,48},{32,0},{48,16},{64,96},{80,112},{96,64},{112,80},{1... | collective-permute-start | bytes 344072 | tf_op jit(solution)/shard_map/ppermute | solution.py:17
  83.5 9.6 %collective-permute-start.23 = (bf16[8,7168]{1,0:T(8,128)(2,1)S(1)}, bf16[8,7168]{1,0:T(8,128)(2,1)S(1)}, u32[]{:S(2)}, u32[]{:S(2)}) collective-permute-start(bf16[8,7168]{1,0:T(8,128)(2,1)S(1)} %slice.49), channel_id=1, source_target_pairs={{0,32},{16,48},{32,0},{48,16},{64,96},{80,112},{96,64},{112,80},{1... | collective-permute-start | bytes 344072 | tf_op jit(solution)/shard_map/ppermute | solution.py:17
  87.4 13.2 %collective-permute-start.11 = (bf16[8,7168]{1,0:T(8,128)(2,1)S(1)}, bf16[8,7168]{1,0:T(8,128)(2,1)S(1)}, u32[]{:S(2)}, u32[]{:S(2)}) collective-permute-start(bf16[8,7168]{1,0:T(8,128)(2,1)S(1)} %add_convert_fusion.5), channel_id=1, source_target_pairs={{0,0},{1,1},{2,2},{3,3},{4,4},{5,5},{6,6},{7,7},{8,8},{9,9},{10,10... | collective-permute-start | bytes 344072 | tf_op jit(solution)/shard_map/ppermute | solution.py:26
  93.1 12.2 %collective-permute-start.24 = (bf16[8,7168]{1,0:T(8,128)(2,1)S(1)}, bf16[8,7168]{1,0:T(8,128)(2,1)S(1)}, u32[]{:S(2)}, u32[]{:S(2)}) collective-permute-start(bf16[8,7168]{1,0:T(8,128)(2,1)S(1)} %add_convert_fusion.4), channel_id=1, source_target_pairs={{0,0},{1,1},{2,2},{3,3},{4,4},{5,5},{6,6},{7,7},{8,8},{9,9},{10,10... | collective-permute-start | bytes 344072 | tf_op jit(solution)/shard_map/ppermute | solution.py:26
  100.6 8.2 %collective-permute-start.12 = (bf16[8,7168]{1,0:T(8,128)(2,1)S(1)}, bf16[8,7168]{1,0:T(8,128)(2,1)S(1)}, u32[]{:S(2)}, u32[]{:S(2)}) collective-permute-start(bf16[8,7168]{1,0:T(8,128)(2,1)S(1)} %collective-permute-done.11), channel_id=1, source_target_pairs={{0,32},{16,48},{32,0},{48,16},{64,96},{80,112},{96,64},{112,80},{1... | collective-permute-start | bytes 344072 | tf_op jit(solution)/shard_map/ppermute | solution.py:17
  105.3 6.1 %collective-permute-start.25 = (bf16[8,7168]{1,0:T(8,128)(2,1)S(1)}, bf16[8,7168]{1,0:T(8,128)(2,1)S(1)}, u32[]{:S(2)}, u32[]{:S(2)}) collective-permute-start(bf16[8,7168]{1,0:T(8,128)(2,1)S(1)} %collective-permute-done.24), channel_id=1, source_target_pairs={{0,32},{16,48},{32,0},{48,16},{64,96},{80,112},{96,64},{112,80},{1... | collective-permute-start | bytes 344072 | tf_op jit(solution)/shard_map/ppermute | solution.py:17
  108.8 6.6 %collective-permute-start.13 = (bf16[16,7168]{1,0:T(8,128)(2,1)S(1)}, bf16[16,7168]{1,0:T(8,128)(2,1)S(1)}, u32[]{:S(2)}, u32[]{:S(2)}) collective-permute-start(bf16[16,7168]{1,0:T(8,128)(2,1)S(1)} %pad_maximum_fusion.5), channel_id=1, source_target_pairs={{0,64},{16,208},{32,96},{48,240},{64,0},{80,144},{96,32},{112,176}... | collective-permute-start | bytes 688136 | tf_op jit(solution)/shard_map/ppermute | solution.py:34
  111.4 7.2 %collective-permute-start.26 = (bf16[16,7168]{1,0:T(8,128)(2,1)S(1)}, bf16[16,7168]{1,0:T(8,128)(2,1)S(1)}, u32[]{:S(2)}, u32[]{:S(2)}) collective-permute-start(bf16[16,7168]{1,0:T(8,128)(2,1)S(1)} %constant_dynamic-update-slice_fusion.3.a), channel_id=1, source_target_pairs={{0,64},{16,208},{32,96},{48,240},{64,0},{80,144},{96,32},{112,176}... | collective-permute-start | bytes 688136 | tf_op jit(solution)/shard_map/ppermute | solution.py:34
  115.4 13.7 %collective-permute-start.14 = (bf16[32,7168]{1,0:T(8,128)(2,1)S(1)}, bf16[32,7168]{1,0:T(8,128)(2,1)S(1)}, u32[]{:S(2)}, u32[]{:S(2)}) collective-permute-start(bf16[32,7168]{1,0:T(8,128)(2,1)S(1)} %constant_dynamic-update-slice_fusion.refs_2_), channel_id=1, source_target_pairs={{0,192},{16,80},{32,224},{48,112},{64,128},{80,16},{96,160},{112,4... | collective-permute-start | bytes 1376264 | tf_op jit(solution)/shard_map/ppermute | solution.py:34
  118.7 12.1 %collective-permute-start.27 = (bf16[32,7168]{1,0:T(8,128)(2,1)S(1)}, bf16[32,7168]{1,0:T(8,128)(2,1)S(1)}, u32[]{:S(2)}, u32[]{:S(2)}) collective-permute-start(bf16[32,7168]{1,0:T(8,128)(2,1)S(1)} %join.1.refs_1_), channel_id=1, source_target_pairs={{0,192},{16,80},{32,224},{48,112},{64,128},{80,16},{96,160},{112,4... | collective-permute-start | bytes 1376264 | tf_op jit(solution)/shard_map/ppermute | solution.py:34
  122.3 17.8 %collective-permute-start.28 = (bf16[448,256]{1,0:T(8,128)(2,1)}, bf16[448,256]{1,0:T(8,128)(2,1)S(1)}, u32[]{:S(2)}, u32[]{:S(2)}) collective-permute-start(bf16[448,256]{1,0:T(8,128)(2,1)} %reduce-scatter.2.cloned.1.call-done.share_ref), channel_id=1, source_target_pairs={{0,240},{16,224},{32,208},{48,192},{64,176},{80,160},{96,144},{112... | collective-permute-start | bytes 688136 | tf_op jit(solution)/shard_map/ppermute | solution.py:387
  129.1 11.2 %collective-permute-start.15 = (bf16[32,7168]{1,0:T(8,128)(2,1)S(1)}, bf16[32,7168]{1,0:T(8,128)(2,1)S(1)}, u32[]{:S(2)}, u32[]{:S(2)}) collective-permute-start(bf16[32,7168]{1,0:T(8,128)(2,1)S(1)} %constant_dynamic-update-slice_fusion.refs_2_), channel_id=1, source_target_pairs={{0,16},{16,0},{32,48},{48,32},{64,80},{80,64},{96,112},{112,96},{1... | collective-permute-start | bytes 1376264 | tf_op jit(solution)/shard_map/ppermute | solution.py:17
  129.1 11.2 %collective-permute-start.16 = (bf16[32,7168]{1,0:T(8,128)(2,1)S(1)}, bf16[32,7168]{1,0:T(8,128)(2,1)S(1)}, u32[]{:S(2)}, u32[]{:S(2)}) collective-permute-start(bf16[32,7168]{1,0:T(8,128)(2,1)S(1)} %collective-permute-done.14.refs_3_), channel_id=1, source_target_pairs={{0,16},{16,0},{32,48},{48,32},{64,80},{80,64},{96,112},{112,96},{1... | collective-permute-start | bytes 1376264 | tf_op jit(solution)/shard_map/ppermute | solution.py:17
  129.6 13.4 %collective-permute-start.29 = (bf16[32,7168]{1,0:T(8,128)(2,1)S(1)}, bf16[32,7168]{1,0:T(8,128)(2,1)S(1)}, u32[]{:S(2)}, u32[]{:S(2)}) collective-permute-start(bf16[32,7168]{1,0:T(8,128)(2,1)S(1)} %join.1.refs_1_), channel_id=1, source_target_pairs={{0,16},{16,0},{32,48},{48,32},{64,80},{80,64},{96,112},{112,96},{1... | collective-permute-start | bytes 1376264 | tf_op jit(solution)/shard_map/ppermute | solution.py:17
  140.2 2.8 %collective-permute-start.30 = (bf16[32,7168]{1,0:T(8,128)(2,1)S(1)}, bf16[32,7168]{1,0:T(8,128)(2,1)S(1)}, u32[]{:S(2)}, u32[]{:S(2)}) collective-permute-start(bf16[32,7168]{1,0:T(8,128)(2,1)S(1)} %later.3.refs_2_), channel_id=1, source_target_pairs={{0,16},{16,0},{32,48},{48,32},{64,80},{80,64},{96,112},{112,96},{1... | collective-permute-start | bytes 1376264 | tf_op jit(solution)/shard_map/ppermute | solution.py:17
  140.3 1.9 %copy-start.4 = (bf16[448,256]{1,0:T(8,128)(2,1)S(1)}, bf16[448,256]{1,0:T(8,128)(2,1)}, u32[]{:S(2)}) copy-start(bf16[448,256]{1,0:T(8,128)(2,1)} %reduce-scatter.2.cloned.1.call-done.share_ref) | copy-start | bytes 688132
Sparse Core Ops, SparseCore 0:
  39.8 69.9 reduce-scatter.1

commit v6 on v5

--- a/solution.py
+++ b/solution.py
@@ -180,7 +180,7 @@
     tok, d = tokens.shape
     width = got.shape[1]
     n = 16
-    group = 4
+    group = 2
     table = jax.ShapeDtypeStruct((tok, tok), BF)
     return pl.pallas_call(
         latent_kernel,
@@ -201,7 +201,7 @@
         cost_estimate=cost(2 * tok * d * width, 2 * tok * d + 2 * d * width),
         compiler_params=pltpu.CompilerParams(vmem_limit_bytes=16 << 20),
         name="latent_part",
-    )(p, s, ids, gates, latent, got, tokens)
+    )(p, s, ids, gates, latent, got, near(tokens))
 
 
 def finish_kernel(p_ref, share_ref, theirs_ref, out_ref):

time: 152 us -> 154 us (1.013)
  starting transfers between devices: 57.8 us -> 63.7 us
  waiting for transfers between devices: 53.4 us -> 48 us
    ppermute x11, starting transfers between devices: 5.8 us -> 10.3 us  [across(): return lax.ppermute(value, 'pipe', [(i, i ^ mask) for i in range(16)])]
    ppermute x1, starting transfers between devices: 6.75 us -> 11.2 us  [per_device(): theirs = lax.ppermute(share, 'pipe', mirror)]
    ppermute x12, starting transfers between devices: 17.8 us -> 13.6 us  [along_x(): return lax.ppermute(value, 'pipe', pairs)]
    ppermute x11, waiting for transfers between devices: 10.1 us -> 6.5 us  [across(): return lax.ppermute(value, 'pipe', [(i, i ^ mask) for i in range(16)])]
  transfers between devices with their start and end apart: 32 -> 32, of which waited for: 15 -> 15; matrix products, arithmetic and copies ran while one was open for 1% -> 1% of each run, Pallas kernels for 14% -> 15%
where the time goes in v6:
time: 154 us; the launch traced here: 153 us
  starting transfers between devices  63.7 us (41%)
  waiting for transfers between devices  48 us (31%)
  Pallas kernels  24.1 us (16%)
  between operations  14.5 us (9%)
    ppermute x6, starting transfers between devices, shifted(): return lax.ppermute(value, ('pipe', 'expert'), pairs)  25.2 us
    ppermute x12, waiting for transfers between devices, along_x(): return lax.ppermute(value, 'pipe', pairs)  24.3 us
    ppermute x12, starting transfers between devices, along_x(): return lax.ppermute(value, 'pipe', pairs)  13.6 us
    ppermute x1, starting transfers between devices, per_device(): theirs = lax.ppermute(share, 'pipe', mirror)  11.2 us
    ppermute x1, waiting for transfers between devices, per_device(): theirs = lax.ppermute(share, 'pipe', mirror)  10.3 us
    ppermute x11, starting transfers between devices, across(): return lax.ppermute(value, 'pipe', [(i, i ^ mask) for i in range(16)])  10.3 us
    pallas_call x1, Pallas kernels, backward(): pl.pallas_call(backward_kernel, in_specs=[vmem] * 9, out_specs=[vmem] * 2...  7.19 us
    ppermute x6, waiting for transfers between devices, shifted(): return lax.ppermute(value, ('pipe', 'expert'), pairs)  6.78 us
  transfers between devices with their start and end apart: 32, of which 15 were waited for; matrix products, arithmetic and copies ran while one was open for 1% of the time, Pallas kernels for 15%

profile of v6, /device:TPU:1, one launch (start us, length us, event | category | flops | bytes accessed | tf_op | source)
XLA Modules:
  0.0 153.3 jit_solution(11882698385077280406)
XLA Ops:
  7.2 0.0 reduce-scatter.2.cloned.1.call-start
  7.2 3.3 %collective-permute-start.1 = (bf16[7168,128]{1,0:T(8,128)(2,1)}, bf16[7168,128]{1,0:T(8,128)(2,1)S(1)}, u32[]{:S(2)}, u32[]{:S(2)}) collective-permute-start(bf16[7168,128]{1,0:T(8,128)(2,1)} %bitcast.8), channel_id=1, source_target_pairs={{0,16},{16,0},{32,48},{48,32},{64,80},{80,64},{96,112},{112,96},{1... | collective-permute-start | bytes 5505032 | tf_op jit(solution)/shard_map/ppermute | solution.py:17
  10.5 0.9 slice_select_fusion
  11.4 3.4 %collective-permute-start = (bf16[128,256]{1,0:T(8,128)(2,1)S(1)}, bf16[128,256]{1,0:T(8,128)(2,1)S(1)}, u32[]{:S(2)}, u32[]{:S(2)}) collective-permute-start(bf16[128,256]{1,0:T(8,128)(2,1)S(1)} %slice_select_fusion), channel_id=1, source_target_pairs={{0,240},{16,224},{32,208},{48,192},{64,176},{80,160},{96,144},{112... | collective-permute-start | bytes 196616 | tf_op jit(solution)/shard_map/ppermute | solution.py:383
  14.8 0.7 copy-done.5
  15.5 0.7 copy-done.7
  16.2 3.3 %select.1 = (bf16[8,7168]{1,0:T(8,128)(2,1)S(1)}, bf16[8,7168]{1,0:T(8,128)(2,1)S(1)}, bf16[8,7168]{1,0:T(8,128)(2,1)S(1)}, bf16[8,7168]{1,0:T(8,128)(2,1)S(1)}) custom-call(s32[1]{0:T(128)} %bitcast.p_ref, s32[1]{0:T(128)} %bitcast.1.s_ref, s32[8,128]{1,0:T(8,128)S(1)} %bitcast.15, f32[8,128]{1,0:T(8,128)S(1)} %bitcast.17, bf16[128,7168]{1,0:T(8,128)(2,1)} %tok_ref.3, ...), custom_call_target="tpu_custom_call" | custom-call | flops 58720256 | bytes 3670016 | tf_op jit(solution)/shard_map/select/pallas_call | solution.py:136
  19.5 0.0 copy-start
  19.5 0.0 copy-start.3
  19.6 2.4 %collective-permute-start.3 = (bf16[8,7168]{1,0:T(8,128)(2,1)S(1)}, bf16[8,7168]{1,0:T(8,128)(2,1)S(1)}, u32[]{:S(2)}, u32[]{:S(2)}) collective-permute-start(bf16[8,7168]{1,0:T(8,128)(2,1)S(1)} %get-tuple-element.20), channel_id=1, source_target_pairs={{0,4},{1,5},{2,6},{3,7},{4,0},{5,1},{6,2},{7,3},{8,12},{9,13},{10,... | collective-permute-start | bytes 344072 | tf_op jit(solution)/shard_map/ppermute | solution.py:26
  22.0 9.6 %collective-permute-start.2 = (bf16[8,7168]{1,0:T(8,128)(2,1)S(1)}, bf16[8,7168]{1,0:T(8,128)(2,1)S(1)}, u32[]{:S(2)}, u32[]{:S(2)}) collective-permute-start(bf16[8,7168]{1,0:T(8,128)(2,1)S(1)} %later.2), channel_id=1, source_target_pairs={{0,0},{1,1},{2,2},{3,3},{4,4},{5,5},{6,6},{7,7},{8,8},{9,9},{10,10... | collective-permute-start | bytes 344072 | tf_op jit(solution)/shard_map/ppermute | solution.py:26
  31.6 1.9 %collective-permute-start.17 = (bf16[8,7168]{1,0:T(8,128)(2,1)S(1)}, bf16[8,7168]{1,0:T(8,128)(2,1)S(1)}, u32[]{:S(2)}, u32[]{:S(2)}) collective-permute-start(bf16[8,7168]{1,0:T(8,128)(2,1)S(1)} %get-tuple-element.24), channel_id=1, source_target_pairs={{0,0},{1,1},{2,2},{3,3},{4,4},{5,5},{6,6},{7,7},{8,8},{9,9},{10,10... | collective-permute-start | bytes 344072 | tf_op jit(solution)/shard_map/ppermute | solution.py:26
  33.6 2.3 %collective-permute-start.18 = (bf16[8,7168]{1,0:T(8,128)(2,1)S(1)}, bf16[8,7168]{1,0:T(8,128)(2,1)S(1)}, u32[]{:S(2)}, u32[]{:S(2)}) collective-permute-start(bf16[8,7168]{1,0:T(8,128)(2,1)S(1)} %get-tuple-element.25), channel_id=1, source_target_pairs={{0,4},{1,5},{2,6},{3,7},{4,0},{5,1},{6,2},{7,3},{8,12},{9,13},{10,... | collective-permute-start | bytes 344072 | tf_op jit(solution)/shard_map/ppermute | solution.py:26
  35.9 0.1 collective-permute-start.6
  36.0 5.1 %latent_part.1 = (bf16[7168,256]{1,0:T(8,128)(2,1)}, bf16[128,128]{1,0:T(8,128)(2,1)S(1)}, bf16[128,128]{1,0:T(8,128)(2,1)S(1)}, bf16[128,128]{1,0:T(8,128)(2,1)S(1)}) custom-call(s32[1]{0:T(128)} %bitcast.p_ref, s32[1]{0:T(128)} %bitcast.1.s_ref, s32[8,128]{1,0:T(8,128)S(1)} %bitcast.16, f32[8,128]{1,0:T(8,128)S(1)} %bitcast.18, ...), custom_call_target="tpu_custom_call" | custom-call | flops 469762048 | bytes 5505024 | tf_op jit(solution)/shard_map/latent_part/pallas_call | solution.py:185
  41.2 0.0 reduce-scatter.2.cloned.1.call-update
  41.2 0.6 collective-permute-start.7
  41.8 1.6 %collective-permute-start.4 = (bf16[16,7168]{1,0:T(8,128)(2,1)S(1)}, bf16[16,7168]{1,0:T(8,128)(2,1)S(1)}, u32[]{:S(2)}, u32[]{:S(2)}) collective-permute-start(bf16[16,7168]{1,0:T(8,128)(2,1)S(1)} %pad_maximum_fusion.4), channel_id=1, source_target_pairs={{0,64},{16,208},{32,96},{48,240},{64,0},{80,144},{96,32},{112,176}... | collective-permute-start | bytes 688136 | tf_op jit(solution)/shard_map/ppermute | solution.py:34
  43.5 1.2 collective-permute-start.19
  44.7 3.3 %collective-permute-done.4 = bf16[16,7168]{1,0:T(8,128)(2,1)S(1)} collective-permute-done((bf16[16,7168]{1,0:T(8,128)(2,1)S(1)}, bf16[16,7168]{1,0:T(8,128)(2,1)S(1)}, u32[]{:S(2)}, u32[]{:S(2)}) %collective-permute-start.4) | collective-permute-done | bytes 229408 | tf_op jit(solution)/shard_map/ppermute | solution.py:34
  48.0 0.1 collective-permute-start.5
  48.1 2.3 %collective-permute-done.19 = bf16[16,7168]{1,0:T(8,128)(2,1)S(1)} collective-permute-done((bf16[16,7168]{1,0:T(8,128)(2,1)S(1)}, bf16[16,7168]{1,0:T(8,128)(2,1)S(1)}, u32[]{:S(2)}, u32[]{:S(2)}) %collective-permute-start.19) | collective-permute-done | bytes 229408 | tf_op jit(solution)/shard_map/ppermute | solution.py:34
  50.4 0.1 collective-permute-start.20
  50.5 5.3 %collective-permute-done.5 = bf16[32,7168]{1,0:T(8,128)(2,1)S(1)} collective-permute-done((bf16[32,7168]{1,0:T(8,128)(2,1)S(1)}, bf16[32,7168]{1,0:T(8,128)(2,1)S(1)}, u32[]{:S(2)}, u32[]{:S(2)}) %collective-permute-start.5) | collective-permute-done | bytes 458784 | tf_op jit(solution)/shard_map/ppermute | solution.py:34
  55.8 0.1 pad_maximum_fusion.rows
  55.9 4.2 %forward.1 = (bf16[32,7168]{1,0:T(8,128)(2,1)S(1)}, bf16[32,7168]{1,0:T(8,128)(2,1)S(1)}, f32[64,256]{1,0:T(8,128)S(1)}, f32[64,256]{1,0:T(8,128)S(1)}) custom-call(bf16[64,7168]{1,0:T(8,128)(2,1)S(1)} %pad_maximum_fusion.rows, bf16[7168,128]{1,0:T(8,128)(2,1)S(1)} %bitcast.9, bf16[7168,128]{1,0:T(8,128)(2,1)} %bitcast.6.wu, ...), custom_call_target="tpu_custom_call" | custom-call | flops 704643072 | bytes 12845056 | tf_op jit(solution)/shard_map/forward/pallas_call | solution.py:293
  60.1 0.7 collective-permute-start.8
  60.8 0.1 pad_maximum_fusion.1.rows
  60.8 7.2 %backward.1 = (bf16[32,7168]{1,0:T(8,128)(2,1)S(1)}, bf16[32,7168]{1,0:T(8,128)(2,1)S(1)}) custom-call(bf16[64,7168]{1,0:T(8,128)(2,1)S(1)} %pad_maximum_fusion.1.rows, f32[64,256]{1,0:T(8,128)S(1)} %get-tuple-element.26.fa, f32[64,256]{1,0:T(8,128)S(1)} %get-tuple-element.27.fb, bf16[128,7168]{1,0:T(8,128)(2,1)S(1)} %bitcast.13, ...), custom_call_target="tpu_custom_call" | custom-call | flops 704643072 | bytes 12845056 | tf_op jit(solution)/shard_map/backward/pallas_call | solution.py:325
  68.0 1.0 collective-permute-start.21
  69.0 0.1 add_convert_fusion.1
  69.1 1.6 %collective-permute-start.9 = (bf16[16,7168]{1,0:T(8,128)(2,1)S(1)}, bf16[16,7168]{1,0:T(8,128)(2,1)S(1)}, u32[]{:S(2)}, u32[]{:S(2)}) collective-permute-start(bf16[16,7168]{1,0:T(8,128)(2,1)S(1)} %slice.43), channel_id=1, source_target_pairs={{0,64},{16,208},{32,96},{48,240},{64,0},{80,144},{96,32},{112,176}... | collective-permute-start | bytes 688136 | tf_op jit(solution)/shard_map/ppermute | solution.py:34
  70.8 5.0 %collective-permute-done.21 = bf16[32,7168]{1,0:T(8,128)(2,1)S(1)} collective-permute-done((bf16[32,7168]{1,0:T(8,128)(2,1)S(1)}, bf16[32,7168]{1,0:T(8,128)(2,1)S(1)}, u32[]{:S(2)}, u32[]{:S(2)}) %collective-permute-start.21) | collective-permute-done | bytes 458784 | tf_op jit(solution)/shard_map/ppermute | solution.py:34
  75.8 0.1 add_convert_fusion
  76.0 1.6 %collective-permute-start.22 = (bf16[16,7168]{1,0:T(8,128)(2,1)S(1)}, bf16[16,7168]{1,0:T(8,128)(2,1)S(1)}, u32[]{:S(2)}, u32[]{:S(2)}) collective-permute-start(bf16[16,7168]{1,0:T(8,128)(2,1)S(1)} %slice.47), channel_id=1, source_target_pairs={{0,64},{16,208},{32,96},{48,240},{64,0},{80,144},{96,32},{112,176}... | collective-permute-start | bytes 688136 | tf_op jit(solution)/shard_map/ppermute | solution.py:34
  77.6 0.1 add_convert_fusion.3
  77.7 1.8 %collective-permute-start.10 = (bf16[8,7168]{1,0:T(8,128)(2,1)S(1)}, bf16[8,7168]{1,0:T(8,128)(2,1)S(1)}, u32[]{:S(2)}, u32[]{:S(2)}) collective-permute-start(bf16[8,7168]{1,0:T(8,128)(2,1)S(1)} %slice.45), channel_id=1, source_target_pairs={{0,32},{16,48},{32,0},{48,16},{64,96},{80,112},{96,64},{112,80},{1... | collective-permute-start | bytes 344072 | tf_op jit(solution)/shard_map/ppermute | solution.py:17
  79.5 4.0 %collective-permute-done.22 = bf16[16,7168]{1,0:T(8,128)(2,1)S(1)} collective-permute-done((bf16[16,7168]{1,0:T(8,128)(2,1)S(1)}, bf16[16,7168]{1,0:T(8,128)(2,1)S(1)}, u32[]{:S(2)}, u32[]{:S(2)}) %collective-permute-start.22) | collective-permute-done | bytes 229408 | tf_op jit(solution)/shard_map/ppermute | solution.py:34
  83.4 0.1 add_convert_fusion.2
  83.5 1.3 collective-permute-start.23
  84.9 1.3 collective-permute-done.10
  86.2 6.2 %collective-permute-start.11 = (bf16[8,7168]{1,0:T(8,128)(2,1)S(1)}, bf16[8,7168]{1,0:T(8,128)(2,1)S(1)}, u32[]{:S(2)}, u32[]{:S(2)}) collective-permute-start(bf16[8,7168]{1,0:T(8,128)(2,1)S(1)} %add_convert_fusion.5), channel_id=1, source_target_pairs={{0,0},{1,1},{2,2},{3,3},{4,4},{5,5},{6,6},{7,7},{8,8},{9,9},{10,10... | collective-permute-start | bytes 344072 | tf_op jit(solution)/shard_map/ppermute | solution.py:26
  92.3 2.3 %collective-permute-done.23 = bf16[8,7168]{1,0:T(8,128)(2,1)S(1)} collective-permute-done((bf16[8,7168]{1,0:T(8,128)(2,1)S(1)}, bf16[8,7168]{1,0:T(8,128)(2,1)S(1)}, u32[]{:S(2)}, u32[]{:S(2)}) %collective-permute-start.23) | collective-permute-done | bytes 114720 | tf_op jit(solution)/shard_map/ppermute | solution.py:17
  94.7 2.8 %collective-permute-start.24 = (bf16[8,7168]{1,0:T(8,128)(2,1)S(1)}, bf16[8,7168]{1,0:T(8,128)(2,1)S(1)}, u32[]{:S(2)}, u32[]{:S(2)}) collective-permute-start(bf16[8,7168]{1,0:T(8,128)(2,1)S(1)} %add_convert_fusion.4), channel_id=1, source_target_pairs={{0,0},{1,1},{2,2},{3,3},{4,4},{5,5},{6,6},{7,7},{8,8},{9,9},{10,10... | collective-permute-start | bytes 344072 | tf_op jit(solution)/shard_map/ppermute | solution.py:26
  97.5 1.0 collective-permute-done.11
  98.5 2.6 %collective-permute-start.12 = (bf16[8,7168]{1,0:T(8,128)(2,1)S(1)}, bf16[8,7168]{1,0:T(8,128)(2,1)S(1)}, u32[]{:S(2)}, u32[]{:S(2)}) collective-permute-start(bf16[8,7168]{1,0:T(8,128)(2,1)S(1)} %collective-permute-done.11), channel_id=1, source_target_pairs={{0,32},{16,48},{32,0},{48,16},{64,96},{80,112},{96,64},{112,80},{1... | collective-permute-start | bytes 344072 | tf_op jit(solution)/shard_map/ppermute | solution.py:17
  101.1 5.8 %collective-permute-done.24 = bf16[8,7168]{1,0:T(8,128)(2,1)S(1)} collective-permute-done((bf16[8,7168]{1,0:T(8,128)(2,1)S(1)}, bf16[8,7168]{1,0:T(8,128)(2,1)S(1)}, u32[]{:S(2)}, u32[]{:S(2)}) %collective-permute-start.24) | collective-permute-done | bytes 114720 | tf_op jit(solution)/shard_map/ppermute | solution.py:26
  106.9 1.5 collective-permute-done.12
  108.4 3.3 %collective-permute-start.13 = (bf16[16,7168]{1,0:T(8,128)(2,1)S(1)}, bf16[16,7168]{1,0:T(8,128)(2,1)S(1)}, u32[]{:S(2)}, u32[]{:S(2)}) collective-permute-start(bf16[16,7168]{1,0:T(8,128)(2,1)S(1)} %pad_maximum_fusion.5), channel_id=1, source_target_pairs={{0,64},{16,208},{32,96},{48,240},{64,0},{80,144},{96,32},{112,176}... | collective-permute-start | bytes 688136 | tf_op jit(solution)/shard_map/ppermute | solution.py:34
  111.7 1.4 collective-permute-done.25
  113.1 2.1 %collective-permute-start.26 = (bf16[16,7168]{1,0:T(8,128)(2,1)S(1)}, bf16[16,7168]{1,0:T(8,128)(2,1)S(1)}, u32[]{:S(2)}, u32[]{:S(2)}) collective-permute-start(bf16[16,7168]{1,0:T(8,128)(2,1)S(1)} %constant_dynamic-update-slice_fusion.3.a), channel_id=1, source_target_pairs={{0,64},{16,208},{32,96},{48,240},{64,0},{80,144},{96,32},{112,176}... | collective-permute-start | bytes 688136 | tf_op jit(solution)/shard_map/ppermute | solution.py:34
  115.2 0.2 collective-permute-done.13
  115.5 0.1 collective-permute-start.14
  115.6 4.1 %collective-permute-done.26.b = bf16[16,7168]{1,0:T(8,128)(2,1)S(1)} collective-permute-done((bf16[16,7168]{1,0:T(8,128)(2,1)S(1)}, bf16[16,7168]{1,0:T(8,128)(2,1)S(1)}, u32[]{:S(2)}, u32[]{:S(2)}) %collective-permute-start.26) | collective-permute-done | bytes 229408 | tf_op jit(solution)/shard_map/ppermute | solution.py:34
  119.7 0.1 collective-permute-start.27
  119.8 0.0 reduce-scatter.2.cloned.1.call-done.share_ref
  119.8 11.2 %collective-permute-start.28 = (bf16[448,256]{1,0:T(8,128)(2,1)}, bf16[448,256]{1,0:T(8,128)(2,1)S(1)}, u32[]{:S(2)}, u32[]{:S(2)}) collective-permute-start(bf16[448,256]{1,0:T(8,128)(2,1)} %reduce-scatter.2.cloned.1.call-done.share_ref), channel_id=1, source_target_pairs={{0,240},{16,224},{32,208},{48,192},{64,176},{80,160},{96,144},{112... | collective-permute-start | bytes 688136 | tf_op jit(solution)/shard_map/ppermute | solution.py:387
  131.0 0.5 collective-permute-start.16
  131.5 0.2 collective-permute-done.27.a
  131.7 10.3 %collective-permute-done.28.refs_0_.theirs_ref = bf16[448,256]{1,0:T(8,128)(2,1)S(1)} collective-permute-done((bf16[448,256]{1,0:T(8,128)(2,1)}, bf16[448,256]{1,0:T(8,128)(2,1)S(1)}, u32[]{:S(2)}, u32[]{:S(2)}) %collective-permute-start.28) | collective-permute-done | bytes 229408 | tf_op jit(solution)/shard_map/ppermute | solution.py:387
  142.1 0.1 collective-permute-start.30
  142.2 1.9 %combine.2 = bf16[128,7168]{1,0:T(8,128)(2,1)} custom-call(bf16[128,128]{1,0:T(8,128)(2,1)S(1)} %get-tuple-element.17._.refs_0_, bf16[128,128]{1,0:T(8,128)(2,1)S(1)} %get-tuple-element.18.refs_1_, bf16[32,7168]{1,0:T(8,128)(2,1)S(1)} %constant_dynamic-update-slice_fusion.refs_2_, bf16[32,7168]{1,0:T(8,128)(2,1)S(1)} %collective-permute-done.14.refs_3_, ...), custom_call_target="tpu_custom_call" | custom-call | flops 469762048 | bytes 3670016 | tf_op jit(solution)/shard_map/combine/pallas_call | solution.py:359
  144.1 0.8 finish.1
  144.9 1.5 combine.3
  (52 shorter events, 0.4 us)
Async XLA Ops:
  7.2 112.6 %reduce-scatter.2.cloned.1.call-start = ((), (), s32[]{:S(2)}) async-start(), calls=%async_computation.1 | async-start | bytes 3899392 | tf_op jit(solution)/shard_map/reduce_scatter | solution.py:386
  7.2 14.8 %collective-permute-start.1 = (bf16[7168,128]{1,0:T(8,128)(2,1)}, bf16[7168,128]{1,0:T(8,128)(2,1)S(1)}, u32[]{:S(2)}, u32[]{:S(2)}) collective-permute-start(bf16[7168,128]{1,0:T(8,128)(2,1)} %bitcast.8), channel_id=1, source_target_pairs={{0,16},{16,0},{32,48},{48,32},{64,80},{80,64},{96,112},{112,96},{1... | collective-permute-start | bytes 5505032 | tf_op jit(solution)/shard_map/ppermute | solution.py:17
  11.4 10.6 %collective-permute-start = (bf16[128,256]{1,0:T(8,128)(2,1)S(1)}, bf16[128,256]{1,0:T(8,128)(2,1)S(1)}, u32[]{:S(2)}, u32[]{:S(2)}) collective-permute-start(bf16[128,256]{1,0:T(8,128)(2,1)S(1)} %slice_select_fusion), channel_id=1, source_target_pairs={{0,240},{16,224},{32,208},{48,192},{64,176},{80,160},{96,144},{112... | collective-permute-start | bytes 196616 | tf_op jit(solution)/shard_map/ppermute | solution.py:383
  14.8 0.7 copy-start.5
  15.5 0.7 copy-start.7
  19.5 16.5 %copy-start = (bf16[128,7168]{1,0:T(8,128)(2,1)S(1)}, bf16[128,7168]{1,0:T(8,128)(2,1)}, u32[]{:S(2)}) copy-start(bf16[128,7168]{1,0:T(8,128)(2,1)} %tok_ref.3) | copy-start | bytes 5505028
  19.5 16.5 %copy-start.3 = (bf16[1,128,512]{2,1,0:T(8,128)(2,1)S(1)}, bf16[1,128,512]{2,1,0:T(8,128)(2,1)}, u32[]{:S(2)}) copy-start(bf16[1,128,512]{2,1,0:T(8,128)(2,1)} %lat_ref.1) | copy-start | bytes 393220
  19.5 16.5 %copy-start.6 = (s32[128,8]{0,1:T(8,128)S(1)}, s32[128,8]{0,1:T(8,128)}, u32[]{:S(2)}) copy-start(s32[128,8]{0,1:T(8,128)} %param.9) | copy-start | bytes 12292
  19.5 16.5 %copy-start.8 = (f32[128,8]{0,1:T(8,128)S(1)}, f32[128,8]{0,1:T(8,128)}, u32[]{:S(2)}) copy-start(f32[128,8]{0,1:T(8,128)} %param.10) | copy-start | bytes 12292
  19.6 21.6 %collective-permute-start.3 = (bf16[8,7168]{1,0:T(8,128)(2,1)S(1)}, bf16[8,7168]{1,0:T(8,128)(2,1)S(1)}, u32[]{:S(2)}, u32[]{:S(2)}) collective-permute-start(bf16[8,7168]{1,0:T(8,128)(2,1)S(1)} %get-tuple-element.20), channel_id=1, source_target_pairs={{0,4},{1,5},{2,6},{3,7},{4,0},{5,1},{6,2},{7,3},{8,12},{9,13},{10,... | collective-permute-start | bytes 344072 | tf_op jit(solution)/shard_map/ppermute | solution.py:26
  22.0 19.7 %collective-permute-start.2 = (bf16[8,7168]{1,0:T(8,128)(2,1)S(1)}, bf16[8,7168]{1,0:T(8,128)(2,1)S(1)}, u32[]{:S(2)}, u32[]{:S(2)}) collective-permute-start(bf16[8,7168]{1,0:T(8,128)(2,1)S(1)} %later.2), channel_id=1, source_target_pairs={{0,0},{1,1},{2,2},{3,3},{4,4},{5,5},{6,6},{7,7},{8,8},{9,9},{10,10... | collective-permute-start | bytes 344072 | tf_op jit(solution)/shard_map/ppermute | solution.py:26
  31.6 11.8 %collective-permute-start.17 = (bf16[8,7168]{1,0:T(8,128)(2,1)S(1)}, bf16[8,7168]{1,0:T(8,128)(2,1)S(1)}, u32[]{:S(2)}, u32[]{:S(2)}) collective-permute-start(bf16[8,7168]{1,0:T(8,128)(2,1)S(1)} %get-tuple-element.24), channel_id=1, source_target_pairs={{0,0},{1,1},{2,2},{3,3},{4,4},{5,5},{6,6},{7,7},{8,8},{9,9},{10,10... | collective-permute-start | bytes 344072 | tf_op jit(solution)/shard_map/ppermute | solution.py:26
  33.6 9.8 %collective-permute-start.18 = (bf16[8,7168]{1,0:T(8,128)(2,1)S(1)}, bf16[8,7168]{1,0:T(8,128)(2,1)S(1)}, u32[]{:S(2)}, u32[]{:S(2)}) collective-permute-start(bf16[8,7168]{1,0:T(8,128)(2,1)S(1)} %get-tuple-element.25), channel_id=1, source_target_pairs={{0,4},{1,5},{2,6},{3,7},{4,0},{5,1},{6,2},{7,3},{8,12},{9,13},{10,... | collective-permute-start | bytes 344072 | tf_op jit(solution)/shard_map/ppermute | solution.py:26
  35.9 20.0 %collective-permute-start.6 = (bf16[7168,128]{1,0:T(8,128)(2,1)}, bf16[7168,128]{1,0:T(8,128)(2,1)}, u32[]{:S(2)}, u32[]{:S(2)}) collective-permute-start(bf16[7168,128]{1,0:T(8,128)(2,1)} %bitcast.6.wu), channel_id=1, source_target_pairs={{0,16},{16,0},{32,48},{48,32},{64,80},{80,64},{96,112},{112,96},{1... | collective-permute-start | bytes 5505032 | tf_op jit(solution)/shard_map/ppermute | solution.py:17
  41.2 14.7 %collective-permute-start.7 = (bf16[128,7168]{1,0:T(8,128)(2,1)}, bf16[128,7168]{1,0:T(8,128)(2,1)S(1)}, u32[]{:S(2)}, u32[]{:S(2)}) collective-permute-start(bf16[128,7168]{1,0:T(8,128)(2,1)} %bitcast.11), channel_id=1, source_target_pairs={{0,16},{16,0},{32,48},{48,32},{64,80},{80,64},{96,112},{112,96},{1... | collective-permute-start | bytes 5505032 | tf_op jit(solution)/shard_map/ppermute | solution.py:17
  41.8 6.2 %collective-permute-start.4 = (bf16[16,7168]{1,0:T(8,128)(2,1)S(1)}, bf16[16,7168]{1,0:T(8,128)(2,1)S(1)}, u32[]{:S(2)}, u32[]{:S(2)}) collective-permute-start(bf16[16,7168]{1,0:T(8,128)(2,1)S(1)} %pad_maximum_fusion.4), channel_id=1, source_target_pairs={{0,64},{16,208},{32,96},{48,240},{64,0},{80,144},{96,32},{112,176}... | collective-permute-start | bytes 688136 | tf_op jit(solution)/shard_map/ppermute | solution.py:34
  43.4 12.4 %copy-start.1 = (bf16[1,7168,128]{2,1,0:T(8,128)(2,1)S(1)}, bf16[1,7168,128]{2,1,0:T(8,128)(2,1)}, u32[]{:S(2)}) copy-start(bf16[1,7168,128]{2,1,0:T(8,128)(2,1)} %param.11) | copy-start | bytes 5505028
  43.5 12.4 %copy-start.2 = (bf16[1,128,7168]{2,1,0:T(8,128)(2,1)S(1)}, bf16[1,128,7168]{2,1,0:T(8,128)(2,1)}, u32[]{:S(2)}) copy-start(bf16[1,128,7168]{2,1,0:T(8,128)(2,1)} %param.13) | copy-start | bytes 5505028
  43.5 6.9 %collective-permute-start.19 = (bf16[16,7168]{1,0:T(8,128)(2,1)S(1)}, bf16[16,7168]{1,0:T(8,128)(2,1)S(1)}, u32[]{:S(2)}, u32[]{:S(2)}) collective-permute-start(bf16[16,7168]{1,0:T(8,128)(2,1)S(1)} %pad_maximum_fusion.6), channel_id=1, source_target_pairs={{0,64},{16,208},{32,96},{48,240},{64,0},{80,144},{96,32},{112,176}... | collective-permute-start | bytes 688136 | tf_op jit(solution)/shard_map/ppermute | solution.py:34
  48.0 7.8 %collective-permute-start.5 = (bf16[32,7168]{1,0:T(8,128)(2,1)S(1)}, bf16[32,7168]{1,0:T(8,128)(2,1)S(1)}, u32[]{:S(2)}, u32[]{:S(2)}) collective-permute-start(bf16[32,7168]{1,0:T(8,128)(2,1)S(1)} %pad_maximum_fusion.2), channel_id=1, source_target_pairs={{0,192},{16,80},{32,224},{48,112},{64,128},{80,16},{96,160},{112,4... | collective-permute-start | bytes 1376264 | tf_op jit(solution)/shard_map/ppermute | solution.py:34
  50.4 10.3 %collective-permute-start.20 = (bf16[32,7168]{1,0:T(8,128)(2,1)S(1)}, bf16[32,7168]{1,0:T(8,128)(2,1)S(1)}, u32[]{:S(2)}, u32[]{:S(2)}) collective-permute-start(bf16[32,7168]{1,0:T(8,128)(2,1)S(1)} %pad_maximum_fusion.3), channel_id=1, source_target_pairs={{0,192},{16,80},{32,224},{48,112},{64,128},{80,16},{96,160},{112,4... | collective-permute-start | bytes 1376264 | tf_op jit(solution)/shard_map/ppermute | solution.py:34
  60.1 8.9 %collective-permute-start.8 = (bf16[32,7168]{1,0:T(8,128)(2,1)S(1)}, bf16[32,7168]{1,0:T(8,128)(2,1)S(1)}, u32[]{:S(2)}, u32[]{:S(2)}) collective-permute-start(bf16[32,7168]{1,0:T(8,128)(2,1)S(1)} %get-tuple-element.22), channel_id=1, source_target_pairs={{0,192},{16,80},{32,224},{48,112},{64,128},{80,16},{96,160},{112,4... | collective-permute-start | bytes 1376264 | tf_op jit(solution)/shard_map/ppermute | solution.py:34
  68.0 7.8 %collective-permute-start.21 = (bf16[32,7168]{1,0:T(8,128)(2,1)S(1)}, bf16[32,7168]{1,0:T(8,128)(2,1)S(1)}, u32[]{:S(2)}, u32[]{:S(2)}) collective-permute-start(bf16[32,7168]{1,0:T(8,128)(2,1)S(1)} %get-tuple-element.29), channel_id=1, source_target_pairs={{0,192},{16,80},{32,224},{48,112},{64,128},{80,16},{96,160},{112,4... | collective-permute-start | bytes 1376264 | tf_op jit(solution)/shard_map/ppermute | solution.py:34
  69.1 8.4 %collective-permute-start.9 = (bf16[16,7168]{1,0:T(8,128)(2,1)S(1)}, bf16[16,7168]{1,0:T(8,128)(2,1)S(1)}, u32[]{:S(2)}, u32[]{:S(2)}) collective-permute-start(bf16[16,7168]{1,0:T(8,128)(2,1)S(1)} %slice.43), channel_id=1, source_target_pairs={{0,64},{16,208},{32,96},{48,240},{64,0},{80,144},{96,32},{112,176}... | collective-permute-start | bytes 688136 | tf_op jit(solution)/shard_map/ppermute | solution.py:34
  76.0 7.5 %collective-permute-start.22 = (bf16[16,7168]{1,0:T(8,128)(2,1)S(1)}, bf16[16,7168]{1,0:T(8,128)(2,1)S(1)}, u32[]{:S(2)}, u32[]{:S(2)}) collective-permute-start(bf16[16,7168]{1,0:T(8,128)(2,1)S(1)} %slice.47), channel_id=1, source_target_pairs={{0,64},{16,208},{32,96},{48,240},{64,0},{80,144},{96,32},{112,176}... | collective-permute-start | bytes 688136 | tf_op jit(solution)/shard_map/ppermute | solution.py:34
  77.7 8.5 %collective-permute-start.10 = (bf16[8,7168]{1,0:T(8,128)(2,1)S(1)}, bf16[8,7168]{1,0:T(8,128)(2,1)S(1)}, u32[]{:S(2)}, u32[]{:S(2)}) collective-permute-start(bf16[8,7168]{1,0:T(8,128)(2,1)S(1)} %slice.45), channel_id=1, source_target_pairs={{0,32},{16,48},{32,0},{48,16},{64,96},{80,112},{96,64},{112,80},{1... | collective-permute-start | bytes 344072 | tf_op jit(solution)/shard_map/ppermute | solution.py:17
  83.5 11.1 %collective-permute-start.23 = (bf16[8,7168]{1,0:T(8,128)(2,1)S(1)}, bf16[8,7168]{1,0:T(8,128)(2,1)S(1)}, u32[]{:S(2)}, u32[]{:S(2)}) collective-permute-start(bf16[8,7168]{1,0:T(8,128)(2,1)S(1)} %slice.49), channel_id=1, source_target_pairs={{0,32},{16,48},{32,0},{48,16},{64,96},{80,112},{96,64},{112,80},{1... | collective-permute-start | bytes 344072 | tf_op jit(solution)/shard_map/ppermute | solution.py:17
  86.2 12.4 %collective-permute-start.11 = (bf16[8,7168]{1,0:T(8,128)(2,1)S(1)}, bf16[8,7168]{1,0:T(8,128)(2,1)S(1)}, u32[]{:S(2)}, u32[]{:S(2)}) collective-permute-start(bf16[8,7168]{1,0:T(8,128)(2,1)S(1)} %add_convert_fusion.5), channel_id=1, source_target_pairs={{0,0},{1,1},{2,2},{3,3},{4,4},{5,5},{6,6},{7,7},{8,8},{9,9},{10,10... | collective-permute-start | bytes 344072 | tf_op jit(solution)/shard_map/ppermute | solution.py:26
  94.7 12.1 %collective-permute-start.24 = (bf16[8,7168]{1,0:T(8,128)(2,1)S(1)}, bf16[8,7168]{1,0:T(8,128)(2,1)S(1)}, u32[]{:S(2)}, u32[]{:S(2)}) collective-permute-start(bf16[8,7168]{1,0:T(8,128)(2,1)S(1)} %add_convert_fusion.4), channel_id=1, source_target_pairs={{0,0},{1,1},{2,2},{3,3},{4,4},{5,5},{6,6},{7,7},{8,8},{9,9},{10,10... | collective-permute-start | bytes 344072 | tf_op jit(solution)/shard_map/ppermute | solution.py:26
  98.5 9.8 %collective-permute-start.12 = (bf16[8,7168]{1,0:T(8,128)(2,1)S(1)}, bf16[8,7168]{1,0:T(8,128)(2,1)S(1)}, u32[]{:S(2)}, u32[]{:S(2)}) collective-permute-start(bf16[8,7168]{1,0:T(8,128)(2,1)S(1)} %collective-permute-done.11), channel_id=1, source_target_pairs={{0,32},{16,48},{32,0},{48,16},{64,96},{80,112},{96,64},{112,80},{1... | collective-permute-start | bytes 344072 | tf_op jit(solution)/shard_map/ppermute | solution.py:17
  106.8 6.2 %collective-permute-start.25 = (bf16[8,7168]{1,0:T(8,128)(2,1)S(1)}, bf16[8,7168]{1,0:T(8,128)(2,1)S(1)}, u32[]{:S(2)}, u32[]{:S(2)}) collective-permute-start(bf16[8,7168]{1,0:T(8,128)(2,1)S(1)} %collective-permute-done.24), channel_id=1, source_target_pairs={{0,32},{16,48},{32,0},{48,16},{64,96},{80,112},{96,64},{112,80},{1... | collective-permute-start | bytes 344072 | tf_op jit(solution)/shard_map/ppermute | solution.py:17
  108.4 7.1 %collective-permute-start.13 = (bf16[16,7168]{1,0:T(8,128)(2,1)S(1)}, bf16[16,7168]{1,0:T(8,128)(2,1)S(1)}, u32[]{:S(2)}, u32[]{:S(2)}) collective-permute-start(bf16[16,7168]{1,0:T(8,128)(2,1)S(1)} %pad_maximum_fusion.5), channel_id=1, source_target_pairs={{0,64},{16,208},{32,96},{48,240},{64,0},{80,144},{96,32},{112,176}... | collective-permute-start | bytes 688136 | tf_op jit(solution)/shard_map/ppermute | solution.py:34
  113.1 6.6 %collective-permute-start.26 = (bf16[16,7168]{1,0:T(8,128)(2,1)S(1)}, bf16[16,7168]{1,0:T(8,128)(2,1)S(1)}, u32[]{:S(2)}, u32[]{:S(2)}) collective-permute-start(bf16[16,7168]{1,0:T(8,128)(2,1)S(1)} %constant_dynamic-update-slice_fusion.3.a), channel_id=1, source_target_pairs={{0,64},{16,208},{32,96},{48,240},{64,0},{80,144},{96,32},{112,176}... | collective-permute-start | bytes 688136 | tf_op jit(solution)/shard_map/ppermute | solution.py:34
  115.5 15.5 %collective-permute-start.14 = (bf16[32,7168]{1,0:T(8,128)(2,1)S(1)}, bf16[32,7168]{1,0:T(8,128)(2,1)S(1)}, u32[]{:S(2)}, u32[]{:S(2)}) collective-permute-start(bf16[32,7168]{1,0:T(8,128)(2,1)S(1)} %constant_dynamic-update-slice_fusion.refs_2_), channel_id=1, source_target_pairs={{0,192},{16,80},{32,224},{48,112},{64,128},{80,16},{96,160},{112,4... | collective-permute-start | bytes 1376264 | tf_op jit(solution)/shard_map/ppermute | solution.py:34
  119.7 12.0 %collective-permute-start.27 = (bf16[32,7168]{1,0:T(8,128)(2,1)S(1)}, bf16[32,7168]{1,0:T(8,128)(2,1)S(1)}, u32[]{:S(2)}, u32[]{:S(2)}) collective-permute-start(bf16[32,7168]{1,0:T(8,128)(2,1)S(1)} %join.1.refs_1_), channel_id=1, source_target_pairs={{0,192},{16,80},{32,224},{48,112},{64,128},{80,16},{96,160},{112,4... | collective-permute-start | bytes 1376264 | tf_op jit(solution)/shard_map/ppermute | solution.py:34
  119.8 22.2 %collective-permute-start.28 = (bf16[448,256]{1,0:T(8,128)(2,1)}, bf16[448,256]{1,0:T(8,128)(2,1)S(1)}, u32[]{:S(2)}, u32[]{:S(2)}) collective-permute-start(bf16[448,256]{1,0:T(8,128)(2,1)} %reduce-scatter.2.cloned.1.call-done.share_ref), channel_id=1, source_target_pairs={{0,240},{16,224},{32,208},{48,192},{64,176},{80,160},{96,144},{112... | collective-permute-start | bytes 688136 | tf_op jit(solution)/shard_map/ppermute | solution.py:387
  131.0 11.2 %collective-permute-start.15 = (bf16[32,7168]{1,0:T(8,128)(2,1)S(1)}, bf16[32,7168]{1,0:T(8,128)(2,1)S(1)}, u32[]{:S(2)}, u32[]{:S(2)}) collective-permute-start(bf16[32,7168]{1,0:T(8,128)(2,1)S(1)} %constant_dynamic-update-slice_fusion.refs_2_), channel_id=1, source_target_pairs={{0,16},{16,0},{32,48},{48,32},{64,80},{80,64},{96,112},{112,96},{1... | collective-permute-start | bytes 1376264 | tf_op jit(solution)/shard_map/ppermute | solution.py:17
  131.0 11.2 %collective-permute-start.16 = (bf16[32,7168]{1,0:T(8,128)(2,1)S(1)}, bf16[32,7168]{1,0:T(8,128)(2,1)S(1)}, u32[]{:S(2)}, u32[]{:S(2)}) collective-permute-start(bf16[32,7168]{1,0:T(8,128)(2,1)S(1)} %collective-permute-done.14.refs_3_), channel_id=1, source_target_pairs={{0,16},{16,0},{32,48},{48,32},{64,80},{80,64},{96,112},{112,96},{1... | collective-permute-start | bytes 1376264 | tf_op jit(solution)/shard_map/ppermute | solution.py:17
  131.5 13.4 %collective-permute-start.29 = (bf16[32,7168]{1,0:T(8,128)(2,1)S(1)}, bf16[32,7168]{1,0:T(8,128)(2,1)S(1)}, u32[]{:S(2)}, u32[]{:S(2)}) collective-permute-start(bf16[32,7168]{1,0:T(8,128)(2,1)S(1)} %join.1.refs_1_), channel_id=1, source_target_pairs={{0,16},{16,0},{32,48},{48,32},{64,80},{80,64},{96,112},{112,96},{1... | collective-permute-start | bytes 1376264 | tf_op jit(solution)/shard_map/ppermute | solution.py:17
  142.1 2.8 %collective-permute-start.30 = (bf16[32,7168]{1,0:T(8,128)(2,1)S(1)}, bf16[32,7168]{1,0:T(8,128)(2,1)S(1)}, u32[]{:S(2)}, u32[]{:S(2)}) collective-permute-start(bf16[32,7168]{1,0:T(8,128)(2,1)S(1)} %later.3.refs_2_), channel_id=1, source_target_pairs={{0,16},{16,0},{32,48},{48,32},{64,80},{80,64},{96,112},{112,96},{1... | collective-permute-start | bytes 1376264 | tf_op jit(solution)/shard_map/ppermute | solution.py:17
  142.2 1.9 %copy-start.4 = (bf16[448,256]{1,0:T(8,128)(2,1)S(1)}, bf16[448,256]{1,0:T(8,128)(2,1)}, u32[]{:S(2)}) copy-start(bf16[448,256]{1,0:T(8,128)(2,1)} %reduce-scatter.2.cloned.1.call-done.share_ref) | copy-start | bytes 688132
Sparse Core Ops, SparseCore 0:
  41.3 68.3 reduce-scatter.1
